TPU v7x, 32 devices: a whole 2x2x4 slice. The times are simulated.
32 devices in a mesh: sample: 4 (over y, x), space: 8 (over z, core).
Axes of the slice: x: 2, y: 2, z: 4, core: 2. Of those that a mesh axis runs over, the one named last changes fastest.
Arguments:
- slabs: bfloat16 [4, 64, 32, 3072], P('sample', 'space'), may hold values from -6 to 6
- weight: bfloat16 [3, 3, 3, 96, 192], replicated, may hold values from -0.125 to 0.125
- cotangent: bfloat16 [4, 32, 16, 3072], P('sample', 'space'), may hold values from -6 to 6
Outputs:
- activation: bfloat16 [4, 32, 16, 3072], P('sample', 'space')
- input_grad: bfloat16 [4, 64, 32, 3072], P('sample', 'space')
- weight_grad: float32 [3, 3, 3, 96, 192], P(None, None, None, None, 'space')
All inputs are finite; a program needn't handle non-finite values.
Results may differ from a plain program's by a relative error of at most 0.007.
Values may be sent and summed in bfloat16 or wider, within the bound.
No kernel may reach another device: no remote copies, remote signals or barrier semaphores. Data moves between devices by JAX's collectives and lax.ppermute only.
A program may use at most 64 MiB of HBM per device.

v0:
```python
import jax
import jax.numpy as jnp
from jax import lax
from jax.sharding import PartitionSpec as P

CIN = 96
COUT = 192
DEPTH = 64
H = 32
W = 32
DOUT = 32
HOUT = 16
WOUT = 16


def from_behind(block, axis, distance):
    devices = range(lax.axis_size(axis))
    route = [(i - distance, i) for i in devices if i - distance in devices]
    return lax.ppermute(block, axis, route)


def parity_view(padded):
    count, depth_two, rows_two, cols_two, chans = padded.shape
    return padded.reshape(count, depth_two // 2, 2, rows_two // 2, 2, cols_two // 2, 2, chans)


def window_rows(parity, depth_off, row_off, col_off, out_d, out_h, out_w):
    piece = parity[
        :,
        depth_off // 2 : depth_off // 2 + out_d,
        depth_off % 2,
        row_off // 2 : row_off // 2 + out_h,
        row_off % 2,
        col_off // 2 : col_off // 2 + out_w,
        col_off % 2,
        :,
    ]
    return piece.reshape(-1, parity.shape[-1])


def conv_forward(padded, weight):
    count = padded.shape[0]
    out_d, out_h, out_w = (
        padded.shape[1] // 2 - 1,
        padded.shape[2] // 2 - 1,
        padded.shape[3] // 2 - 1,
    )
    parity = parity_view(padded)
    total = jnp.zeros((count * out_d * out_h * out_w, weight.shape[4]), jnp.float32)
    for depth_off in range(3):
        for row_off in range(3):
            for col_off in range(3):
                rows = window_rows(parity, depth_off, row_off, col_off, out_d, out_h, out_w)
                total = total + jnp.dot(
                    rows, weight[depth_off, row_off, col_off], preferred_element_type=jnp.float32
                )
    return total.reshape(count, out_d, out_h, out_w, weight.shape[4])


def kernel_terms(padded, grad_rows):
    out_d, out_h, out_w = (
        padded.shape[1] // 2 - 1,
        padded.shape[2] // 2 - 1,
        padded.shape[3] // 2 - 1,
    )
    parity = parity_view(padded)
    collected = []
    for depth_off in range(3):
        for row_off in range(3):
            for col_off in range(3):
                rows = window_rows(parity, depth_off, row_off, col_off, out_d, out_h, out_w)
                collected.append(
                    lax.dot_general(
                        rows,
                        grad_rows,
                        (((0,), (0,)), ((), ())),
                        preferred_element_type=jnp.float32,
                    )
                )
    return jnp.stack(collected).reshape(3, 3, 3, padded.shape[-1], grad_rows.shape[-1])


def padded_input_grad(grad_rows, weight, count, out_d, out_h, out_w):
    chans = weight.shape[3]
    buffers = {}
    for depth_off in range(3):
        for row_off in range(3):
            for col_off in range(3):
                term = jnp.dot(
                    grad_rows,
                    weight[depth_off, row_off, col_off].T,
                    preferred_element_type=jnp.float32,
                )
                term = term.reshape(count, out_d, out_h, out_w, chans)
                term = jnp.pad(
                    term,
                    (
                        (0, 0),
                        (depth_off // 2, 1 - depth_off // 2),
                        (row_off // 2, 1 - row_off // 2),
                        (col_off // 2, 1 - col_off // 2),
                        (0, 0),
                    ),
                )
                key_par = (depth_off % 2, row_off % 2, col_off % 2)
                if key_par in buffers:
                    buffers[key_par] = buffers[key_par] + term
                else:
                    buffers[key_par] = term
    ordered = [buffers[pd, ph, pw] for pd in range(2) for ph in range(2) for pw in range(2)]
    stacked = jnp.stack(ordered).reshape(2, 2, 2, count, out_d + 1, out_h + 1, out_w + 1, chans)
    stacked = jnp.transpose(stacked, (3, 4, 0, 5, 1, 6, 2, 7))
    return stacked.reshape(count, 2 * (out_d + 1), 2 * (out_h + 1), 2 * (out_w + 1), chans)


def derivative(preact):
    sigmoid_val = jax.nn.sigmoid(preact)
    return sigmoid_val * (1.0 + preact * (1.0 - sigmoid_val))


def per_device(slabs, weight, cotangent):
    group_size, depth_dev = (slabs.shape[0], slabs.shape[1])
    bands = lax.axis_size("space") // group_size
    band_rows = H // bands
    out_rows = band_rows // 2
    out_dev = depth_dev // 2
    cells = (
        slabs.reshape(group_size, depth_dev, bands, band_rows, W * CIN)
        .transpose(0, 2, 1, 3, 4)
        .reshape(group_size * bands, depth_dev, band_rows, W * CIN)
    )
    cot_cells = (
        cotangent.reshape(group_size, out_dev, bands, out_rows, WOUT * COUT)
        .transpose(0, 2, 1, 3, 4)
        .reshape(group_size * bands, out_dev, out_rows, WOUT * COUT)
    )
    whole_cells, whole_cot = (
        lax.all_to_all(cells, "space", split_axis=0, concat_axis=1, tiled=True),
        lax.all_to_all(cot_cells, "space", split_axis=0, concat_axis=1, tiled=True),
    )
    band_index = lax.axis_index("space") % bands
    inside = band_index != 0
    above = from_behind(whole_cells[:, :, band_rows - 1 :], "space", 1)
    above = jnp.where(inside, above, jnp.zeros_like(above))
    field = jnp.concatenate([above, whole_cells], axis=2).reshape(1, DEPTH, band_rows + 1, W, CIN)
    padded = jnp.pad(field, ((0, 0), (1, 1), (0, 1), (1, 1), (0, 0)))
    preact = conv_forward(padded, weight)
    result = jax.nn.silu(preact).astype(jnp.bfloat16)
    grad_pre = (whole_cot.reshape(preact.shape).astype(jnp.float32) * derivative(preact)).astype(
        jnp.bfloat16
    )
    grad_rows = grad_pre.reshape(-1, COUT)
    grad_pad = padded_input_grad(grad_rows, weight, 1, DOUT, out_rows, WOUT)
    grad_full = grad_pad[:, 1 : DEPTH + 1, :, 1 : W + 1].reshape(1, DEPTH, band_rows + 2, W * CIN)
    top_grad = grad_full[:, :, :1]
    top_grad = jnp.where(inside, top_grad, jnp.zeros_like(top_grad))
    below_grad = from_behind(top_grad.astype(jnp.bfloat16), "space", -1).astype(top_grad.dtype)
    grad_own = grad_full[:, :, 1 : band_rows + 1]
    grad_own = jnp.concatenate(
        [grad_own[:, :, : band_rows - 1], grad_own[:, :, band_rows - 1 :] + below_grad], axis=2
    )
    grad_in = grad_own.astype(jnp.bfloat16)
    partial_w = kernel_terms(padded, grad_rows)
    back_act, back_grad = (
        lax.all_to_all(
            result.reshape(1, DOUT, out_rows, WOUT * COUT),
            "space",
            split_axis=1,
            concat_axis=0,
            tiled=True,
        ),
        lax.all_to_all(grad_in, "space", split_axis=1, concat_axis=0, tiled=True),
    )
    activation = (
        back_act.reshape(group_size, bands, out_dev, out_rows, WOUT * COUT)
        .transpose(0, 2, 1, 3, 4)
        .reshape(group_size, out_dev, HOUT, WOUT * COUT)
    )
    input_grad = (
        back_grad.reshape(group_size, bands, depth_dev, band_rows, W * CIN)
        .transpose(0, 2, 1, 3, 4)
        .reshape(group_size, depth_dev, H, W * CIN)
    )
    batch_total = group_size * lax.axis_size("sample")
    summed = lax.psum(partial_w, "sample")
    gradient = lax.psum_scatter(summed, "space", scatter_dimension=4, tiled=True)
    return (activation, input_grad, gradient / batch_total)


def solution(mesh):
    placed = (P("sample", "space", None, None), P(), P("sample", "space", None, None))
    return jax.shard_map(
        per_device,
        mesh=mesh,
        in_specs=placed,
        out_specs=(
            P("sample", "space", None, None),
            P("sample", "space", None, None),
            P(None, None, None, None, "space"),
        ),
        check_vma=False,
    )
```

profile of v0, /device:TPU:0, one launch (start us, length us, event | category | flops | bytes accessed | tf_op | source)
XLA Modules:
  0.0 321.4 jit_solution(11337097288794359994)
XLA Ops:
  7.2 3.4 %copy.157 = bf16[1,8,32,3072]{3,1,2,0:T(8,128)(2,1)} copy(bf16[1,8,32,3072]{3,2,1,0:T(8,128)(2,1)} %param.3) | data formatting | bytes 3145728 | tf_op args[0]
  10.6 6.5 %all-to-all-start = ((bf16[8,8,4,3072]{3,1,2,0:T(8,128)(2,1)}), bf16[8,8,4,3072]{3,1,2,0:T(8,128)(2,1)S(1)}, u32[]{:S(2)}, u32[]{:S(2)}) async-start(bf16[8,8,4,3072]{3,1,2,0:T(8,128)(2,1)} %bitcast.2), calls=%async_computation | async-start | bytes 3145728 | tf_op jit(solution)/shard_map/all_to_all | solution.py:138
  18.3 36.6 %all-to-all-done = bf16[8,8,4,3072]{3,1,2,0:T(8,128)(2,1)S(1)} async-done(((bf16[8,8,4,3072]{3,1,2,0:T(8,128)(2,1)}), bf16[8,8,4,3072]{3,1,2,0:T(8,128)(2,1)S(1)}, u32[]{:S(2)}, u32[]{:S(2)}) %all-to-all-start) | async-done | bytes 1572896 | tf_op jit(solution)/shard_map/all_to_all | solution.py:138
  54.9 3.5 %all-to-all-start.2 = ((bf16[8,4,2,3072]{3,2,1,0:T(2,128)(2,1)}), bf16[8,4,2,3072]{3,2,1,0:T(2,128)(2,1)S(1)}, u32[]{:S(2)}, u32[]{:S(2)}) async-start(bf16[8,4,2,3072]{3,2,1,0:T(2,128)(2,1)} %bitcast.599), calls=%async_computation.2 | async-start | bytes 786432 | tf_op jit(solution)/shard_map/all_to_all | solution.py:139
  59.7 2.3 collective-permute-start
  62.0 8.8 %all-to-all-done.2 = bf16[8,4,2,3072]{3,2,1,0:T(2,128)(2,1)S(1)} async-done(((bf16[8,4,2,3072]{3,2,1,0:T(2,128)(2,1)}), bf16[8,4,2,3072]{3,2,1,0:T(2,128)(2,1)S(1)}, u32[]{:S(2)}, u32[]{:S(2)}) %all-to-all-start.2) | async-done | bytes 393248 | tf_op jit(solution)/shard_map/all_to_all | solution.py:139
  72.5 3.6 %concatenate.21 = bf16[1,64,4,32,96]{4,3,1,2,0:T(8,128)(2,1)S(1)} reshape(bf16[8,8,4,3072]{3,1,0,2:T(8,128)(2,1)} %copy-done) | data formatting | bytes 3145728 | tf_op jit(solution)/shard_map/concatenate | solution.py:145
  76.7 4.4 %fusion.8 = bf16[1,66,6,34,96]{4,3,1,2,0:T(8,128)(2,1)} fusion(bf16[1,64,4,32,96]{4,3,1,2,0:T(8,128)(2,1)S(1)} %concatenate.21, bf16[1,64,1,32,96]{4,3,1,2,0:T(8,128)(2,1)S(1)} %concatenate.20), kind=kLoop, calls=%fused_computation.14 | loop fusion | flops 24558336 | bytes 4551168 | tf_op jit(solution)/shard_map/concatenate | solution.py:145
  81.0 7.1 %reshape.328 = bf16[1,33,2,3,2,17,2,96]{7,6,5,2,1,4,3,0:T(2,128)(2,1)S(1)} reshape(bf16[1,66,6,34,96]{4,3,1,2,0:T(8,128)(2,1)} %fusion.8) | data formatting | bytes 5170176 | tf_op jit(solution)/shard_map/reshape | solution.py:24
  88.1 4.2 %fusion.150 = (bf16[1,32,1,2,1,16,1,96]{7,6,5,2,1,4,3,0:T(2,128)(2,1)S(1)}, bf16[1,32,1,2,1,16,1,96]{7,6,5,2,1,4,3,0:T(2,128)(2,1)S(1)}, bf16[1,32,1,2,1,16,1,96...) fusion(bf16[1,33,2,3,2,17,2,96]{7,6,5,2,1,4,3,0:T(2,128)(2,1)S(, ...), kind=kLoop, calls=%fused_computation.255 | loop fusion | bytes 3145728 | tf_op jit(solution)/shard_map/slice | solution.py:28
  92.3 11.2 %fusion.149 = (bf16[1,32,1,2,1,16,1,96]{7,6,5,2,1,4,3,0:T(2,128)(2,1)S(1)}, bf16[1,32,1,2,1,16,1,96]{7,6,5,2,1,4,3,0:T(2,128)(2,1)S(1)}, bf16[1,32,1,2,1,16,1,96...) fusion(bf16[1,33,2,3,2,17,2,96]{7,6,5,2,1,4,3,0:T(2,128)(2,1)S(, ...), kind=kLoop, calls=%fused_computation.254 | loop fusion | bytes 7471104 | tf_op jit(solution)/shard_map/slice | solution.py:28
  105.0 2.0 copy-done.1
  115.8 1.3 multiply_convert_fusion
  125.7 13.7 %convolution_bitcast_fusion.2 = f32[1,32,2,16,96]{4,3,2,1,0:T(8,128)S(1)} fusion(bf16[32,2,16,192]{3,2,1,0:T(8,128)(2,1)S(1)} %bitcast.626, bf16[3,3,3,96,192]{4,3,2,1,0:T(8,128)(2,1)S(1)} %copy-done.1), kind=kOutput, calls=%fused_computation.48 | convolution fusion | flops 37748736 | bytes 966656 | tf_op jit(solution)/shard_map/dot_general | solution.py:89
  141.6 8.2 %copy.196 = f32[2,2,2,1,33,3,17,96]{7,3,2,6,1,5,0,4:T(1,128)} copy(f32[2,2,2,1,33,3,17,96]{7,6,5,4,2,1,0,3:T(8,128)S(1)} %bitcast.629) | data formatting | bytes 10340352 | tf_op jit(solution)/shard_map/reshape | solution.py:111
  149.8 22.0 %slice_reduce_fusion = f32[64,6,32,96]{3,2,1,0:T(8,128)} fusion(f32[1,66,6,34,96]{4,0,3,2,1:T(1,128)} %bitcast.628), kind=kLoop, calls=%fused_computation.9 | loop fusion | bytes 9437184 | tf_op jit(solution)/shard_map/slice | solution.py:154
  171.8 8.1 %reshape.329 = f32[1,64,6,3072]{3,2,1,0:T(8,128)} reshape(f32[64,6,32,96]{3,2,1,0:T(8,128)} %slice_reduce_fusion) | data formatting | bytes 9437184 | tf_op jit(solution)/shard_map/reshape | solution.py:154
  179.9 3.4 %slice.325 = bf16[1,64,1,3072]{3,2,1,0:T(2,128)(2,1)S(1)} slice(f32[1,64,6,3072]{3,2,1,0:T(8,128)} %reshape.329), slice={[0:1], [0:64], [0:1], [0:3072]} | slice | bytes 786432 | tf_op jit(solution)/shard_map/slice | solution.py:155
  183.3 4.5 %slice.324 = f32[1,64,1,3072]{3,2,1,0:T(1,128)} slice(f32[1,64,6,3072]{3,2,1,0:T(8,128)} %reshape.329), slice={[0:1], [0:64], [4:5], [0:3072]} | slice | bytes 1572864 | tf_op jit(solution)/shard_map/slice | solution.py:160
  187.9 3.8 %slice.323 = bf16[1,64,3,3072]{3,2,1,0:T(4,128)(2,1)S(1)} slice(f32[1,64,6,3072]{3,2,1,0:T(8,128)} %reshape.329), slice={[0:1], [0:64], [1:4], [0:3072]} | slice | bytes 2359296 | tf_op jit(solution)/shard_map/slice | solution.py:160
  199.8 1.5 copy-done.4
  201.2 3.4 %copy.201 = f32[3,3,3,96,192]{3,4,2,1,0:T(8,128)} copy(f32[3,3,3,96,192]{4,3,2,1,0:T(8,128)} %bitcast.633) | data formatting | bytes 3981312 | tf_op jit(solution)/shard_map/reshape | solution.py:80
  206.5 1.5 copy.188
  210.3 4.1 %all-to-all-start.1 = ((bf16[1,32,2,3072]{3,2,0,1:T(2,128)(2,1)}), bf16[1,32,2,3072]{3,2,0,1:T(2,128)(2,1)S(1)}, u32[]{:S(2)}, u32[]{:S(2)}) async-start(bf16[1,32,2,3072]{3,2,0,1:T(2,128)(2,1)} %copy.191), calls=%async_computation.1 | async-start | bytes 786432 | tf_op jit(solution)/shard_map/all_to_all | solution.py:165
  215.7 2.4 copy.198
  218.1 15.3 %all-to-all-done.1 = bf16[1,32,2,3072]{3,2,0,1:T(2,128)(2,1)S(1)} async-done(((bf16[1,32,2,3072]{3,2,0,1:T(2,128)(2,1)}), bf16[1,32,2,3072]{3,2,0,1:T(2,128)(2,1)S(1)}, u32[]{:S(2)}, u32[]{:S(2)}) %all-to-all-start.1) | async-done | bytes 393248 | tf_op jit(solution)/shard_map/all_to_all | solution.py:165
  233.4 3.6 %all-to-all-start.3 = ((bf16[1,64,4,3072]{3,2,0,1:T(4,128)(2,1)}), bf16[1,64,4,3072]{3,2,0,1:T(4,128)(2,1)S(1)}, u32[]{:S(2)}, u32[]{:S(2)}) async-start(bf16[1,64,4,3072]{3,2,0,1:T(4,128)(2,1)} %copy.198), calls=%async_computation.3 | async-start | bytes 3145728 | tf_op jit(solution)/shard_map/all_to_all | solution.py:172
  237.0 14.2 %reduce-scatter.2.cloned.1.call-done = f32[3,3,3,96,24]{3,4,2,1,0:T(8,128)} async-done(((f32[3,3,3,96,192]{3,4,2,1,0:T(8,128)}), f32[3,3,3,96,24]{3,4,2,1,0:T(8,128)}) %reduce-scatter.2.cloned.1.call-update) | async-done | bytes 248848 | tf_op jit(solution)/shard_map/reduce_scatter | solution.py:186
  252.3 28.2 %all-to-all-done.3 = bf16[1,64,4,3072]{3,2,0,1:T(4,128)(2,1)S(1)} async-done(((bf16[1,64,4,3072]{3,2,0,1:T(4,128)(2,1)}), bf16[1,64,4,3072]{3,2,0,1:T(4,128)(2,1)S(1)}, u32[]{:S(2)}, u32[]{:S(2)}) %all-to-all-start.3) | async-done | bytes 1572896 | tf_op jit(solution)/shard_map/all_to_all | solution.py:172
  281.1 2.0 copy.203
  283.1 29.6 %all-reduce.30.cloned.1.call-done = f32[3,3,3,96,24]{3,4,2,1,0:T(8,128)} async-done(((f32[3,3,3,96,24]{3,4,2,1,0:T(8,128)}), f32[3,3,3,96,24]{3,4,2,1,0:T(8,128)}) %all-reduce.30.cloned.1.call-update) | async-done | bytes 248848 | tf_op jit(solution)/shard_map/psum | solution.py:185
  312.7 1.7 broadcast_multiply_fusion
  (245 shorter events, 39.5 us)
Async XLA Ops:
  10.6 6.5 %copy-start.52 = (bf16[1,4,16,3072]{3,2,1,0:T(8,128)(2,1)S(1)}, bf16[1,4,16,3072]{3,2,1,0:T(8,128)(2,1)}, u32[]{:S(2)}) copy-start(bf16[1,4,16,3072]{3,2,1,0:T(8,128)(2,1)} %param.5) | copy-start | bytes 1179652
  10.6 44.3 %all-to-all-start = ((bf16[8,8,4,3072]{3,1,2,0:T(8,128)(2,1)}), bf16[8,8,4,3072]{3,1,2,0:T(8,128)(2,1)S(1)}, u32[]{:S(2)}, u32[]{:S(2)}) async-start(bf16[8,8,4,3072]{3,1,2,0:T(8,128)(2,1)} %bitcast.2), calls=%async_computation | async-start | bytes 3145728 | tf_op jit(solution)/shard_map/all_to_all | solution.py:138
  54.9 15.9 %all-to-all-start.2 = ((bf16[8,4,2,3072]{3,2,1,0:T(2,128)(2,1)}), bf16[8,4,2,3072]{3,2,1,0:T(2,128)(2,1)S(1)}, u32[]{:S(2)}, u32[]{:S(2)}) async-start(bf16[8,4,2,3072]{3,2,1,0:T(2,128)(2,1)} %bitcast.599), calls=%async_computation.2 | async-start | bytes 786432 | tf_op jit(solution)/shard_map/all_to_all | solution.py:139
  58.3 192.9 %reduce-scatter.2.cloned.1.call-start = ((), (), s32[]{:S(2)}) async-start(), calls=%async_computation.5 | async-start | bytes 2985984 | tf_op jit(solution)/shard_map/reduce_scatter | solution.py:186
  59.7 16.4 %collective-permute-start = (bf16[1,64,1,3072]{3,1,2,0:T(8,128)(2,1)S(1)}, bf16[1,64,1,3072]{3,1,2,0:T(8,128)(2,1)S(1)}, u32[]{:S(2)}, u32[]{:S(2)}) collective-permute-start(bf16[1,64,1,3072]{3,1,2,0:T(8,128)(2,1)S(1)} %slice.294), channel_id=1, source_target_pairs={{0,1},{1,2},{2,3},{3,4},{4,5},{5,6},{6,7},{8,9},{9,10},{10,11},{11... | collective-permute-start | bytes 1179656 | tf_op jit(solution)/shard_map/ppermute | solution.py:19
  103.8 4.4 %copy-start.41 = (bf16[1,32,1,2,1,16,1,96]{7,5,3,1,6,4,2,0:T(8,128)(2,1)}, bf16[1,32,1,2,1,16,1,96]{7,5,3,1,6,4,2,0:T(8,128)(2,1)S(1)}, u32[]{:S(2)}) copy-start(bf16[1,32,1,2,1,16,1,96]{7,5,3,1,6,4,2,0:T(8,128)(2,1)S(1)} %copy.165) | copy-start | bytes 589828
  103.9 4.7 %copy-start.39 = (bf16[1,32,1,2,1,16,1,96]{7,5,3,1,6,4,2,0:T(8,128)(2,1)}, bf16[1,32,1,2,1,16,1,96]{7,5,3,1,6,4,2,0:T(8,128)(2,1)S(1)}, u32[]{:S(2)}) copy-start(bf16[1,32,1,2,1,16,1,96]{7,5,3,1,6,4,2,0:T(8,128)(2,1)S(1)} %copy.166) | copy-start | bytes 589828
  103.9 5.0 %copy-start.35 = (bf16[1,32,1,2,1,16,1,96]{7,5,3,1,6,4,2,0:T(8,128)(2,1)}, bf16[1,32,1,2,1,16,1,96]{7,5,3,1,6,4,2,0:T(8,128)(2,1)S(1)}, u32[]{:S(2)}) copy-start(bf16[1,32,1,2,1,16,1,96]{7,5,3,1,6,4,2,0:T(8,128)(2,1)S(1)} %copy.167) | copy-start | bytes 589828
  104.0 5.2 %copy-start.37 = (bf16[1,32,1,2,1,16,1,96]{7,5,3,1,6,4,2,0:T(8,128)(2,1)}, bf16[1,32,1,2,1,16,1,96]{7,5,3,1,6,4,2,0:T(8,128)(2,1)S(1)}, u32[]{:S(2)}) copy-start(bf16[1,32,1,2,1,16,1,96]{7,5,3,1,6,4,2,0:T(8,128)(2,1)S(1)} %copy.168) | copy-start | bytes 589828
  104.0 5.5 %copy-start.33 = (bf16[1,32,1,2,1,16,1,96]{7,5,3,1,6,4,2,0:T(8,128)(2,1)}, bf16[1,32,1,2,1,16,1,96]{7,5,3,1,6,4,2,0:T(8,128)(2,1)S(1)}, u32[]{:S(2)}) copy-start(bf16[1,32,1,2,1,16,1,96]{7,5,3,1,6,4,2,0:T(8,128)(2,1)S(1)} %copy.169) | copy-start | bytes 589828
  104.1 5.8 %copy-start.31 = (bf16[1,32,1,2,1,16,1,96]{7,5,3,1,6,4,2,0:T(8,128)(2,1)}, bf16[1,32,1,2,1,16,1,96]{7,5,3,1,6,4,2,0:T(8,128)(2,1)S(1)}, u32[]{:S(2)}) copy-start(bf16[1,32,1,2,1,16,1,96]{7,5,3,1,6,4,2,0:T(8,128)(2,1)S(1)} %copy.170) | copy-start | bytes 589828
  104.1 6.0 %copy-start.29 = (bf16[1,32,1,2,1,16,1,96]{7,5,3,1,6,4,2,0:T(8,128)(2,1)}, bf16[1,32,1,2,1,16,1,96]{7,5,3,1,6,4,2,0:T(8,128)(2,1)S(1)}, u32[]{:S(2)}) copy-start(bf16[1,32,1,2,1,16,1,96]{7,5,3,1,6,4,2,0:T(8,128)(2,1)S(1)} %copy.171) | copy-start | bytes 589828
  104.2 6.3 %copy-start.27 = (bf16[1,32,1,2,1,16,1,96]{7,5,3,1,6,4,2,0:T(8,128)(2,1)}, bf16[1,32,1,2,1,16,1,96]{7,5,3,1,6,4,2,0:T(8,128)(2,1)S(1)}, u32[]{:S(2)}) copy-start(bf16[1,32,1,2,1,16,1,96]{7,5,3,1,6,4,2,0:T(8,128)(2,1)S(1)} %copy.172) | copy-start | bytes 589828
  104.2 6.6 %copy-start.25 = (bf16[1,32,1,2,1,16,1,96]{7,5,3,1,6,4,2,0:T(8,128)(2,1)}, bf16[1,32,1,2,1,16,1,96]{7,5,3,1,6,4,2,0:T(8,128)(2,1)S(1)}, u32[]{:S(2)}) copy-start(bf16[1,32,1,2,1,16,1,96]{7,5,3,1,6,4,2,0:T(8,128)(2,1)S(1)} %copy.173) | copy-start | bytes 589828
  104.3 6.8 %copy-start.23 = (bf16[1,32,1,2,1,16,1,96]{7,5,3,1,6,4,2,0:T(8,128)(2,1)}, bf16[1,32,1,2,1,16,1,96]{7,5,3,1,6,4,2,0:T(8,128)(2,1)S(1)}, u32[]{:S(2)}) copy-start(bf16[1,32,1,2,1,16,1,96]{7,5,3,1,6,4,2,0:T(8,128)(2,1)S(1)} %copy.174) | copy-start | bytes 589828
  104.4 7.1 %copy-start.21 = (bf16[1,32,1,2,1,16,1,96]{7,5,3,1,6,4,2,0:T(8,128)(2,1)}, bf16[1,32,1,2,1,16,1,96]{7,5,3,1,6,4,2,0:T(8,128)(2,1)S(1)}, u32[]{:S(2)}) copy-start(bf16[1,32,1,2,1,16,1,96]{7,5,3,1,6,4,2,0:T(8,128)(2,1)S(1)} %copy.175) | copy-start | bytes 589828
  104.4 7.4 %copy-start.19 = (bf16[1,32,1,2,1,16,1,96]{7,5,3,1,6,4,2,0:T(8,128)(2,1)}, bf16[1,32,1,2,1,16,1,96]{7,5,3,1,6,4,2,0:T(8,128)(2,1)S(1)}, u32[]{:S(2)}) copy-start(bf16[1,32,1,2,1,16,1,96]{7,5,3,1,6,4,2,0:T(8,128)(2,1)S(1)} %copy.176) | copy-start | bytes 589828
  104.5 7.6 %copy-start.17 = (bf16[1,32,1,2,1,16,1,96]{7,5,3,1,6,4,2,0:T(8,128)(2,1)}, bf16[1,32,1,2,1,16,1,96]{7,5,3,1,6,4,2,0:T(8,128)(2,1)S(1)}, u32[]{:S(2)}) copy-start(bf16[1,32,1,2,1,16,1,96]{7,5,3,1,6,4,2,0:T(8,128)(2,1)S(1)} %copy.177) | copy-start | bytes 589828
  104.5 7.9 %copy-start.15 = (bf16[1,32,1,2,1,16,1,96]{7,5,3,1,6,4,2,0:T(8,128)(2,1)}, bf16[1,32,1,2,1,16,1,96]{7,5,3,1,6,4,2,0:T(8,128)(2,1)S(1)}, u32[]{:S(2)}) copy-start(bf16[1,32,1,2,1,16,1,96]{7,5,3,1,6,4,2,0:T(8,128)(2,1)S(1)} %copy.178) | copy-start | bytes 589828
  104.6 8.2 %copy-start.13 = (bf16[1,32,1,2,1,16,1,96]{7,5,3,1,6,4,2,0:T(8,128)(2,1)}, bf16[1,32,1,2,1,16,1,96]{7,5,3,1,6,4,2,0:T(8,128)(2,1)S(1)}, u32[]{:S(2)}) copy-start(bf16[1,32,1,2,1,16,1,96]{7,5,3,1,6,4,2,0:T(8,128)(2,1)S(1)} %copy.179) | copy-start | bytes 589828
  104.6 8.4 %copy-start.11 = (bf16[1,32,1,2,1,16,1,96]{7,5,3,1,6,4,2,0:T(8,128)(2,1)}, bf16[1,32,1,2,1,16,1,96]{7,5,3,1,6,4,2,0:T(8,128)(2,1)S(1)}, u32[]{:S(2)}) copy-start(bf16[1,32,1,2,1,16,1,96]{7,5,3,1,6,4,2,0:T(8,128)(2,1)S(1)} %copy.180) | copy-start | bytes 589828
  104.7 8.7 %copy-start.9 = (bf16[1,32,1,2,1,16,1,96]{7,5,3,1,6,4,2,0:T(8,128)(2,1)}, bf16[1,32,1,2,1,16,1,96]{7,5,3,1,6,4,2,0:T(8,128)(2,1)S(1)}, u32[]{:S(2)}) copy-start(bf16[1,32,1,2,1,16,1,96]{7,5,3,1,6,4,2,0:T(8,128)(2,1)S(1)} %copy.181) | copy-start | bytes 589828
  104.7 8.9 %copy-start.7 = (bf16[1,32,1,2,1,16,1,96]{7,5,3,1,6,4,2,0:T(8,128)(2,1)}, bf16[1,32,1,2,1,16,1,96]{7,5,3,1,6,4,2,0:T(8,128)(2,1)S(1)}, u32[]{:S(2)}) copy-start(bf16[1,32,1,2,1,16,1,96]{7,5,3,1,6,4,2,0:T(8,128)(2,1)S(1)} %copy.182) | copy-start | bytes 589828
  104.8 9.2 %copy-start.5 = (bf16[1,32,1,2,1,16,1,96]{7,5,3,1,6,4,2,0:T(8,128)(2,1)}, bf16[1,32,1,2,1,16,1,96]{7,5,3,1,6,4,2,0:T(8,128)(2,1)S(1)}, u32[]{:S(2)}) copy-start(bf16[1,32,1,2,1,16,1,96]{7,5,3,1,6,4,2,0:T(8,128)(2,1)S(1)} %copy.183) | copy-start | bytes 589828
  105.0 10.3 %copy-start.49 = (bf16[1,32,1,2,1,16,1,96]{7,5,3,1,6,4,2,0:T(8,128)(2,1)}, bf16[1,32,1,2,1,16,1,96]{7,5,3,1,6,4,2,0:T(8,128)(2,1)S(1)}, u32[]{:S(2)}) copy-start(bf16[1,32,1,2,1,16,1,96]{7,5,3,1,6,4,2,0:T(8,128)(2,1)S(1)} %copy.187) | copy-start | bytes 589828
  183.3 8.4 %copy-start.48 = (bf16[1,32,1,2,1,16,1,96]{7,5,3,1,6,4,2,0:T(8,128)(2,1)S(1)}, bf16[1,32,1,2,1,16,1,96]{7,5,3,1,6,4,2,0:T(8,128)(2,1)}, u32[]{:S(2)}) copy-start(bf16[1,32,1,2,1,16,1,96]{7,5,3,1,6,4,2,0:T(8,128)(2,1)} %copy-done.47) | copy-start | bytes 589828
  187.9 4.4 %copy-start.44 = (bf16[1,32,1,2,1,16,1,96]{7,5,3,1,6,4,2,0:T(8,128)(2,1)S(1)}, bf16[1,32,1,2,1,16,1,96]{7,5,3,1,6,4,2,0:T(8,128)(2,1)}, u32[]{:S(2)}) copy-start(bf16[1,32,1,2,1,16,1,96]{7,5,3,1,6,4,2,0:T(8,128)(2,1)} %copy-done.43) | copy-start | bytes 589828
  204.8 9.6 %collective-permute-start.1 = (bf16[1,64,1,3072]{3,1,2,0:T(8,128)(2,1)S(1)}, bf16[1,64,1,3072]{3,1,2,0:T(8,128)(2,1)}, u32[]{:S(2)}, u32[]{:S(2)}) collective-permute-start(bf16[1,64,1,3072]{3,1,2,0:T(8,128)(2,1)S(1)} %fusion.38), channel_id=1, source_target_pairs={{1,0},{2,1},{3,2},{4,3},{5,4},{6,5},{7,6},{9,8},{10,9},{11,10},{12... | collective-permute-start | bytes 1179656 | tf_op jit(solution)/shard_map/ppermute | solution.py:19
  208.8 5.6 %copy-start.2 = (f32[1,64,1,3072]{3,2,1,0:T(1,128)S(1)}, f32[1,64,1,3072]{3,2,1,0:T(1,128)}, u32[]{:S(2)}) copy-start(f32[1,64,1,3072]{3,2,1,0:T(1,128)} %slice.324) | copy-start | bytes 2359300
  210.3 23.1 %all-to-all-start.1 = ((bf16[1,32,2,3072]{3,2,0,1:T(2,128)(2,1)}), bf16[1,32,2,3072]{3,2,0,1:T(2,128)(2,1)S(1)}, u32[]{:S(2)}, u32[]{:S(2)}) async-start(bf16[1,32,2,3072]{3,2,0,1:T(2,128)(2,1)} %copy.191), calls=%async_computation.1 | async-start | bytes 786432 | tf_op jit(solution)/shard_map/all_to_all | solution.py:165
  233.4 47.2 %all-to-all-start.3 = ((bf16[1,64,4,3072]{3,2,0,1:T(4,128)(2,1)}), bf16[1,64,4,3072]{3,2,0,1:T(4,128)(2,1)S(1)}, u32[]{:S(2)}, u32[]{:S(2)}) async-start(bf16[1,64,4,3072]{3,2,0,1:T(4,128)(2,1)} %copy.198), calls=%async_computation.3 | async-start | bytes 3145728 | tf_op jit(solution)/shard_map/all_to_all | solution.py:172
  237.0 75.7 %all-reduce.30.cloned.1.call-start = ((), (), s32[]{:S(2)}) async-start(), calls=%async_computation.6 | async-start | bytes 663552 | tf_op jit(solution)/shard_map/psum | solution.py:185
  (29 other events, 50.2 us)
Sparse Core Ops, SparseCore 0:
  204.7 46.4 reduce-scatter.1
  254.2 58.4 all-reduce.29
where the time goes:
time: 323 us; the launch traced here: 321 us
  waiting for transfers between devices  133 us (41%)
  local copies, waits for them, and re-layouts  103 us (32%)
  matrix products  38.7 us (12%)
  starting transfers between devices  21.2 us (7%)
  between operations  16.1 us (5%)
  other arithmetic  9.7 us (3%)
    all_to_all x1, waiting for transfers between devices, per_device(): lax.all_to_all(cells, 'space', split_axis=0, concat_axis=1, tiled=True)  36.6 us
    psum x1, waiting for transfers between devices, per_device(): summed = lax.psum(partial_w, 'sample')  29.6 us
    all_to_all x1, waiting for transfers between devices, per_device(): lax.all_to_all(grad_in, 'space', split_axis=1, concat_axis=0, tiled=True)  28.2 us
    slice x1, local copies, waits for them, and re-layouts, per_device(): grad_pad[:, 1:DEPTH + 1, :, 1:W + 1]  22 us
    dot_general x27, matrix products, padded_input_grad(): jnp.dot(grad_rows, weight[depth_off, row_off, col_off].T, preferred_eleme...  21.2 us
    slice x29, local copies, waits for them, and re-layouts, window_rows(): parity[:, depth_off // 2:depth_off // 2 + out_d, depth_off % 2, row_off /...  16.4 us
    all_to_all x1, waiting for transfers between devices, per_device(): lax.all_to_all(result.reshape(1, DOUT, out_rows, WOUT * COUT), 'space', s...  15.3 us
    reduce_scatter x1, waiting for transfers between devices, per_device(): lax.psum_scatter(summed, 'space', scatter_dimension=4, tiled=True)  14.2 us
  transfers between devices with their start and end apart: 8, of which 6 were waited for; matrix products, arithmetic and copies ran while one was open for 6% of the time, Pallas kernels for 0%

commit v1 on v0

v1 whole, which is shorter than its diff:
```python
import functools

import jax
import jax.numpy as jnp
from jax import lax
from jax.experimental import pallas as pl
from jax.experimental.pallas import tpu as pltpu
from jax.sharding import PartitionSpec as P

CIN = 96
COUT = 192
BLOCK = 384
SPAN = 512
TAPS = 9
TERM_TILES = -(-TAPS * 3 * CIN // 128)
F32 = jnp.float32
BF16 = jnp.bfloat16
VMEM_LIMIT = 12 * 1024 * 1024


def iota(shape, axis):
    return lax.broadcasted_iota(jnp.int32, shape, axis)


def row_split(planes):
    shape = (3 * planes * 16, planes * 32)
    row = iota(shape, 0)
    col = iota(shape, 1)
    j = row & 15
    plane = (row >> 4) & (planes - 1)
    b = jnp.where(row >= planes * 32, 2, jnp.where(row >= planes * 16, 1, 0))
    hit = (col == plane * 32 + 2 * j + b - 1) & ((j + b) > 0)
    return jnp.where(hit, 1.0, 0.0).astype(BF16)


def blank(rows, lanes):
    return jnp.zeros((rows, lanes), BF16)


def dot(lhs, rhs):
    return jnp.dot(lhs, rhs, preferred_element_type=F32)


def dot_nt(lhs, rhs):
    return lax.dot_general(lhs, rhs, (((1,), (1,)), ((), ())), preferred_element_type=F32)


def put(wide, per_out, cells, i, m, tap, piece):
    at = i * per_out + m * 16
    wide[at : at + 16, tap * SPAN + 128 : tap * SPAN + 512] = piece
    if m + 1 < cells:
        wide[at + 16 : at + 32, tap * SPAN : tap * SPAN + 128] = piece[:, 256:]
    if m == 0:
        wide[at : at + 16, tap * SPAN : tap * SPAN + 128] = jnp.zeros((16, 128), BF16)


def edge_kernel(x_hbm, edge_ref, sem):
    copy = pltpu.make_async_copy(x_hbm.at[x_hbm.shape[0] - 1], edge_ref, sem)
    copy.start()
    copy.wait()


def own_kernel(
    planes, x_hbm, w_hbm, cot_hbm, wide, band, preact, cot_ref, x_ref, w_ref, sems
):
    outs = planes // 2
    cells = x_ref.shape[2] // BLOCK
    per_out = cells * 16
    x_copy = pltpu.make_async_copy(x_hbm, x_ref, sems.at[0])
    w_copy = pltpu.make_async_copy(w_hbm, w_ref, sems.at[1])
    cot_copy = pltpu.make_async_copy(cot_hbm, cot_ref, sems.at[2])
    x_copy.start()
    w_copy.start()
    cot_copy.start()
    split = row_split(planes)
    wide[0:per_out, 0 : 3 * SPAN] = jnp.zeros((per_out, 3 * SPAN), BF16)
    x_copy.wait()
    x = x_ref[...].reshape(planes * 32, x_ref.shape[2])
    for m in range(cells):
        rows = dot(split, x[:, m * BLOCK : (m + 1) * BLOCK]).astype(BF16)
        for b in range(3):
            for p in range(planes):
                piece = rows[(b * planes + p) * 16 : (b * planes + p + 1) * 16]
                if p % 2 == 0:
                    put(wide, per_out, cells, p // 2, m, 3 + b, piece)
                else:
                    put(wide, per_out, cells, p // 2, m, 6 + b, piece)
                    if p // 2 + 1 < outs:
                        put(wide, per_out, cells, p // 2 + 1, m, b, piece)
    w_copy.wait()
    for tap in range(TAPS):
        w = w_ref[tap]
        even = jnp.concatenate([blank(32, COUT), w, blank(192, COUT)], axis=0)
        odd = jnp.concatenate([blank(224, COUT), w], axis=0)
        band[tap * SPAN : (tap + 1) * SPAN] = jnp.concatenate([even, odd], axis=1)
    preact[...] = dot(wide[...], band[...])
    cot_copy.wait()


def add_terms(turned, edge, wide, terms):
    rows = terms.shape[0]
    per_out = edge.shape[0]
    terms[...] = jnp.zeros_like(terms)
    lane = iota((rows, SPAN), 1)
    even_lanes = (lane >= 32) & (lane < 320)
    odd_lanes = lane >= 224
    for tap in range(TAPS):
        lanes = slice(tap * SPAN, (tap + 1) * SPAN)
        if tap < 3:
            cols = jnp.concatenate([edge[:, lanes], wide[per_out:, lanes]], axis=0)
        else:
            cols = wide[:, lanes]
        both = dot(turned, cols)
        base = tap * 288 // 128 * 128
        shift = tap * 288 - base
        even = jnp.where(even_lanes, both[:rows], 0.0)
        odd = jnp.where(odd_lanes, both[rows:], 0.0)
        even = pltpu.roll(even, (shift - 32) % SPAN, 1)
        odd = pltpu.roll(odd, (shift - 224) % SPAN, 1)
        terms[:, base : base + BLOCK] += (even + odd)[:, :BLOCK]


def share(terms, send_ref, keep_ref):
    rows = send_ref.shape[0]
    send_ref[...] = terms[:rows].astype(BF16)
    keep_ref[...] = terms[rows:]


def halo_kernel(
    width, above_ref, wide, band, pre_ref, cot_ref,
    act_ref, gp_ref, first_ref, turned_ref, edge, send_ref, keep_ref, terms,
):
    outs = cot_ref.shape[0]
    cells = cot_ref.shape[2] // BLOCK
    per_out = cells * 16
    at = lax.axis_index("space")
    core = at % 2
    chip = at // 2
    split_one = row_split(1)
    for m in range(cells):
        lanes = slice(m * BLOCK, (m + 1) * BLOCK)
        plane = above_ref[:, lanes]
        plane = jnp.where(core + chip == 0, jnp.zeros_like(plane), plane)
        above = dot(split_one, plane).astype(BF16)
        for b in range(3):
            put(edge, per_out, cells, 0, m, b, above[b * 16 : b * 16 + 16])
    added = dot(edge[...], band[: 3 * SPAN])
    for i in range(outs):
        for m in range(cells):
            lanes = slice(m * BLOCK, (m + 1) * BLOCK)
            at = i * per_out + m * 16
            value = pre_ref[at : at + 16]
            if i == 0:
                value = value + added[at : at + 16]
            sig = jax.nn.sigmoid(value)
            act_ref[i, :, lanes] = (value * sig).astype(BF16)
            grad = cot_ref[i, :, lanes].astype(F32) * (sig * (1.0 + value * (1.0 - sig)))
            grad = grad.astype(BF16)
            gp_ref[at : at + 16] = grad
            if i == 0:
                first_ref[at : at + 16] = grad

    rows = send_ref.shape[0]
    half = lax.axis_size("space") // 4
    high = rows // half
    shape = (8 * rows, 2 * COUT)
    inner = iota(shape, 0)
    later = inner >= 4 * rows
    inner = inner - jnp.where(later, 4 * rows, 0)
    odd = inner >= 2 * rows
    inner = inner - jnp.where(odd, 2 * rows, 0)
    kept = inner >= rows
    inner = inner - jnp.where(kept, rows, 0)
    source = jnp.where(kept, core, 1 - core) * width + jnp.where(odd, COUT, 0)
    for k in range(half):
        channel = inner - k * high
        inside = (channel >= 0) & (channel < width)
        target = jnp.where(later, chip ^ k, chip ^ (k + half)) * 2 * width
        source = source + jnp.where(inside, channel + target, 0)
        if high != width:
            source = jnp.where((channel >= width) & (channel < high), -1, source)
    order = jnp.where(iota(shape, 1) == source, 1.0, 0.0).astype(BF16)
    turned_ref[...] = dot_nt(order, gp_ref[...]).astype(BF16)
    add_terms(turned_ref[: 4 * rows], edge, wide, terms)
    share(terms, send_ref, keep_ref)


def later_kernel(turned_ref, edge, wide, send_ref, keep_ref, terms):
    add_terms(turned_ref[4 * send_ref.shape[0] :], edge, wide, terms)
    share(terms, send_ref, keep_ref)


def input_kernel(gp_ref, below_ref, band, out_ref):
    per_out = below_ref.shape[0]
    cells = per_out // 16
    here = gp_ref[...]
    following = below_ref[...]
    last = lax.axis_index("space") == lax.axis_size("space") - 1
    following = jnp.where(last, jnp.zeros_like(following), following)
    there = jnp.concatenate([here[per_out:], following], axis=0)
    count = gp_ref.shape[0]
    outs = count // per_out
    shape = (128, 128)
    row = iota(shape, 0)
    below = jnp.where((iota(shape, 1) == row + 1) & ((row & 15) != 15), 1.0, 0.0).astype(BF16)

    def lowered(block):
        return jnp.concatenate(
            [dot(below, block[at : at + 128]).astype(BF16) for at in range(0, count, 128)], axis=0
        )

    here_low = lowered(here)
    there_low = lowered(there)

    def term(grad, a, b):
        tap = a * 3 + b
        return dot_nt(grad, band[tap * SPAN : (tap + 1) * SPAN])

    groups = {
        (0, 0): term(here, 1, 1),
        (0, 1): term(here, 1, 2) + term(here_low, 1, 0),
        (1, 0): term(here, 2, 1) + term(there, 0, 1),
        (1, 1): term(here, 2, 2) + term(here_low, 2, 0) + term(there, 0, 2) + term(there_low, 0, 0),
    }
    shape = (32, 32)
    row = iota(shape, 0)
    weave = jnp.where(iota(shape, 1) == (row >> 1) + (row & 1) * 16, 1.0, 0.0).astype(BF16)
    for i in range(outs):
        for m in range(cells):
            at = i * per_out + m * 16
            for pd in range(2):
                parts = []
                for ph in range(2):
                    y = groups[pd, ph]
                    body = y[at : at + 16, 128:512]
                    if m + 1 < cells:
                        body = jnp.concatenate(
                            [body[:, :256], body[:, 256:] + y[at + 16 : at + 32, :128]], axis=1
                        )
                    parts.append(body.astype(BF16))
                mixed = dot(weave, jnp.concatenate(parts, axis=0)).astype(BF16)
                out_ref[2 * i + pd, :, m * BLOCK : (m + 1) * BLOCK] = mixed


def early_pair_kernel(keep_ref, got_ref, *out_refs):
    total = keep_ref[...] + got_ref[...].astype(F32)
    high = out_refs[0].shape[0]
    for k, ref in enumerate(out_refs):
        ref[...] = total[k * high : (k + 1) * high].astype(ref.dtype)


def later_pair_kernel(early_ref, keep_ref, got_ref, first_ref, passed_ref, *out_refs):
    del early_ref
    passed_ref[...] = first_ref[...]
    early_pair_kernel(keep_ref, got_ref, *out_refs)


def depth_kernel(own_ref, *refs):
    total = own_ref[...]
    for ref in refs[:-1]:
        total = total + ref[...].astype(F32)
    refs[-1][...] = total.astype(BF16)


def sample_kernel(scale, *refs):
    out_ref = refs[-1]
    parts = [ref[...].astype(F32) for ref in refs[:-1]]
    while len(parts) > 1:
        parts = [parts[n] + parts[n + 1] for n in range(0, len(parts), 2)]
    total = parts[0][: out_ref.shape[1]] * scale
    for n in range(out_ref.shape[0]):
        out_ref[n] = total[:, n * CIN : (n + 1) * CIN]


def flipped(size, bits):
    return [(i, i ^ bits) for i in range(size)]


def per_device(slabs, weight, cotangent):
    samples, planes, rows, lanes = slabs.shape
    outs = planes // 2
    space = lax.axis_size("space")
    sample = lax.axis_size("sample")
    depth = space // 2
    width = COUT // space
    high = -(-width // 8) * 8
    half = depth // 2
    part = (high, TERM_TILES * 128)
    group = (half * high, TERM_TILES * 128)
    cells = lanes // BLOCK
    per_out = cells * 16
    count = outs * per_out

    in_chip = flipped(space, 1)
    onward = [(i, (i + 1) % space) for i in range(space)]
    back = [(b, a) for a, b in onward]

    x = slabs.reshape(planes, rows, lanes)
    cot = cotangent.reshape(outs, rows // 2, lanes)
    w = weight.reshape(TAPS, 3 * CIN, COUT)
    x, cot, w = (pltpu.with_memory_space_constraint(array, pltpu.HBM) for array in (x, cot, w))
    vmem = pl.BlockSpec(memory_space=pltpu.VMEM)
    hbm = pl.BlockSpec(memory_space=pltpu.HBM)
    params = pltpu.CompilerParams(vmem_limit_bytes=VMEM_LIMIT)
    shape = jax.ShapeDtypeStruct
    flops = 2 * count * TAPS * SPAN * BLOCK

    edge = pl.pallas_call(
        edge_kernel,
        out_shape=shape((rows, lanes), BF16),
        in_specs=[hbm],
        out_specs=vmem,
        scratch_shapes=[pltpu.SemaphoreType.DMA(())],
        compiler_params=params,
        name="edge_plane",
    )(x)
    above = lax.ppermute(edge, "space", onward)
    wide, band, preact, cot_in = pl.pallas_call(
        functools.partial(own_kernel, planes),
        out_shape=(
            shape((count, TAPS * SPAN), BF16),
            shape((TAPS * SPAN, BLOCK), BF16),
            shape((count, BLOCK), F32),
            shape(cot.shape, BF16),
        ),
        in_specs=[hbm] * 3,
        out_specs=(vmem,) * 4,
        scratch_shapes=[
            pltpu.VMEM(x.shape, BF16),
            pltpu.VMEM(w.shape, BF16),
            pltpu.SemaphoreType.DMA((3,)),
        ],
        compiler_params=params,
        cost_estimate=pl.CostEstimate(flops=flops, bytes_accessed=12 << 20, transcendentals=0),
        name="own_planes",
    )(x, w, cot)

    terms = pltpu.VMEM((2 * group[0], group[1]), F32)
    act, grad, first, turned, halo, send, keep = pl.pallas_call(
        functools.partial(halo_kernel, width),
        out_shape=(
            shape(cot.shape, BF16),
            shape((count, BLOCK), BF16),
            shape((per_out, BLOCK), BF16),
            shape((8 * group[0], count), BF16),
            shape((per_out, 3 * SPAN), BF16),
            shape(group, BF16),
            shape(group, F32),
        ),
        in_specs=[vmem] * 5,
        out_specs=(vmem,) * 7,
        scratch_shapes=[terms],
        compiler_params=params,
        cost_estimate=pl.CostEstimate(
            flops=flops // 2, bytes_accessed=8 << 20, transcendentals=count * BLOCK
        ),
        name="halo_and_early_half",
    )(above, wide, band, preact, cot_in)
    got = lax.ppermute(send, "space", in_chip)
    later_send, later_keep = pl.pallas_call(
        later_kernel,
        out_shape=(shape(group, BF16), shape(group, F32)),
        in_specs=[vmem] * 3,
        out_specs=(vmem,) * 2,
        scratch_shapes=[terms],
        compiler_params=params,
        cost_estimate=pl.CostEstimate(flops=flops // 2, bytes_accessed=8 << 20, transcendentals=0),
        name="later_half",
    )(turned, halo, wide)
    later_got = lax.ppermute(later_send, "space", in_chip)

    early = pl.pallas_call(
        early_pair_kernel,
        out_shape=(shape(part, BF16),) * half,
        in_specs=[vmem] * 2,
        out_specs=(vmem,) * half,
        compiler_params=params,
        name="early_pair_sum",
    )(keep, got)
    came = [
        lax.ppermute(early[k - half], "space", flipped(space, 2 * k))
        for k in reversed(range(half, depth))
    ]
    first, own, *later = pl.pallas_call(
        later_pair_kernel,
        out_shape=(shape(first.shape, BF16), shape(part, F32)) + (shape(part, BF16),) * (half - 1),
        in_specs=[vmem] * 4,
        out_specs=(vmem,) * (half + 1),
        compiler_params=params,
        name="later_pair_sum",
    )(early[0], later_keep, later_got, first)
    came += [lax.ppermute(later[k - 1], "space", flipped(space, 2 * k)) for k in range(1, half)]
    below = lax.ppermute(first, "space", back)

    grad_in = pl.pallas_call(
        input_kernel,
        out_shape=shape(x.shape, BF16),
        in_specs=[vmem] * 3,
        out_specs=vmem,
        compiler_params=params,
        cost_estimate=pl.CostEstimate(flops=flops, bytes_accessed=8 << 20, transcendentals=0),
        name="input_grad",
    )(grad, below, band)

    total = pl.pallas_call(
        depth_kernel,
        out_shape=shape(part, BF16),
        in_specs=[vmem] * depth,
        out_specs=vmem,
        compiler_params=params,
        name="depth_sum",
    )(own, *came)
    others = [lax.ppermute(total, "sample", flipped(sample, j)) for j in range(1, sample)]
    kernel_grad = pl.pallas_call(
        functools.partial(sample_kernel, 1.0 / (samples * sample)),
        out_shape=shape((TAPS * 3, width, CIN), F32),
        in_specs=[vmem] * sample,
        out_specs=vmem,
        compiler_params=params,
        name="sample_sum",
    )(total, *others)
    kernel_grad = jnp.transpose(kernel_grad, (0, 2, 1)).reshape(3, 3, 3, CIN, width)
    return act.reshape(cotangent.shape), grad_in.reshape(slabs.shape), kernel_grad


def solution(mesh):
    placed = (P("sample", "space", None, None), P(), P("sample", "space", None, None))
    return jax.shard_map(
        per_device,
        mesh=mesh,
        in_specs=placed,
        out_specs=(
            P("sample", "space", None, None),
            P("sample", "space", None, None),
            P(None, None, None, None, "space"),
        ),
        check_vma=False,
    )
```

time: 323 us -> 39.1 us (0.12)
  waiting for transfers between devices: 133 us -> 12.4 us
  local copies, waits for them, and re-layouts: 103 us -> 0 us
  matrix products: 38.7 us -> 0 us
  between operations: 16.1 us -> 0.68 us
  Pallas kernels: 0 us -> 15.2 us
  starting transfers between devices: 21.2 us -> 10.6 us
  other arithmetic: 9.7 us -> 0 us
    all_to_all x4 -> x0, waiting for transfers between devices: 89 us -> none  [the longest x1 36.6 us: per_device(): lax.all_to_all(cells, 'space', split_axis=0, concat_axis=1, tiled=True)]
    slice x34 -> x0, local copies, waits for them, and re-layouts: 50.2 us -> none  [the longest x1 22 us: per_device(): grad_pad[:, 1:DEPTH + 1, :, 1:W + 1]]
    dot_general x81 -> x0, matrix products: 38.7 us -> none  [the longest x27 21.2 us: padded_input_grad(): jnp.dot(grad_rows, weight[depth_off, row_off, col_off].T, preferred_eleme...]
    psum x1 -> x0, waiting for transfers between devices: 29.6 us -> none  [per_device(): summed = lax.psum(partial_w, 'sample')]
    reshape x7 -> x0, local copies, waits for them, and re-layouts: 28.8 us -> none  [the longest x1 8.21 us: padded_input_grad(): jnp.stack(ordered)]
    all_to_all x4 -> x0, starting transfers between devices: 17.6 us -> none  [the longest x1 6.46 us: per_device(): lax.all_to_all(cells, 'space', split_axis=0, concat_axis=1, tiled=True)]
    pallas_call x0 -> x9, Pallas kernels: none -> 15.2 us  [the longest x1 5.34 us: per_device(): pl.pallas_call(functools.partial(own_kernel, planes), out_shape=(shape((c...]
    reduce_scatter x1 -> x0, waiting for transfers between devices: 14.2 us -> none  [per_device(): lax.psum_scatter(summed, 'space', scatter_dimension=4, tiled=True)]
  transfers between devices with their start and end apart: 8 -> 10, of which waited for: 6 -> 5; matrix products, arithmetic and copies ran while one was open for 6% -> 0% of each run, Pallas kernels for 0% -> 29%
where the time goes in v1:
time: 39.1 us; the launch traced here: 38.9 us
  Pallas kernels  15.2 us (39%)
  waiting for transfers between devices  12.4 us (32%)
  starting transfers between devices  10.6 us (27%)
  between operations  0.68 us (2%)
    ppermute x2, waiting for transfers between devices, per_device(): lax.ppermute(early[k - half], 'space', flipped(space, 2 * k))  9.43 us
    pallas_call x1, Pallas kernels, per_device(): pl.pallas_call(functools.partial(own_kernel, planes), out_shape=(shape((c...  5.34 us
    pallas_call x1, Pallas kernels, per_device(): pl.pallas_call(input_kernel, out_shape=shape(x.shape, BF16), in_specs=[vm...  4.35 us
    ppermute x3, starting transfers between devices, per_device(): lax.ppermute(total, 'sample', flipped(sample, j))  3.55 us
    ppermute x2, starting transfers between devices, per_device(): lax.ppermute(early[k - half], 'space', flipped(space, 2 * k))  3.11 us
    pallas_call x1, Pallas kernels, per_device(): pl.pallas_call(functools.partial(halo_kernel, width), out_shape=(shape(co...  2.26 us
    ppermute x1, waiting for transfers between devices, per_device(): above = lax.ppermute(edge, 'space', onward)  2.04 us
    ppermute x1, starting transfers between devices, per_device(): lax.ppermute(later[k - 1], 'space', flipped(space, 2 * k))  1.41 us
  transfers between devices with their start and end apart: 10, of which 5 were waited for; matrix products, arithmetic and copies ran while one was open for 0% of the time, Pallas kernels for 29%

profile of v1, /device:TPU:0, one launch (start us, length us, event | category | flops | bytes accessed | tf_op | source)
XLA Modules:
  0.0 38.9 jit_solution(2329404124627184714)
XLA Ops:
  0.6 0.9 %edge_plane.1 = bf16[32,3072]{1,0:T(8,128)(2,1)S(1)} custom-call(bf16[8,32,3072]{2,1,0:T(8,128)(2,1)} %bitcast.8), custom_call_target="tpu_custom_call" | custom-call | tf_op jit(solution)/shard_map/edge_plane/pallas_call | solution.py:308
  1.6 0.5 %collective-permute-start = (bf16[32,3072]{1,0:T(8,128)(2,1)S(1)}, bf16[32,3072]{1,0:T(8,128)(2,1)S(1)}, u32[]{:S(2)}, u32[]{:S(2)}) collective-permute-start(bf16[32,3072]{1,0:T(8,128)(2,1)S(1)} %edge_plane.1), channel_id=1, source_target_pairs={{0,1},{1,2},{2,3},{3,4},{4,5},{5,6},{6,7},{7,0},{8,9},{9,10},{10,1... | collective-permute-start | bytes 589832 | tf_op jit(solution)/shard_map/ppermute | solution.py:317
  2.1 5.3 %own_planes.1 = (bf16[512,4608]{1,0:T(8,128)(2,1)S(1)}, bf16[4608,384]{1,0:T(8,128)(2,1)S(1)}, f32[512,384]{1,0:T(8,128)S(1)}, bf16[4,16,3072]{2,1,0:T(8,128)(2,1)S(1)}) custom-call(bf16[8,32,3072]{2,1,0:T(8,128)(2,1)} %bitcast.9, bf16[9,288,192]{2,1,0:T(8,128)(2,1)} %bitcast.11, bf16[4,16,3072]{2,1,0:T(8,128)(2,1)} %bitcast.12), custom_call_target="tpu_custom_call" | custom-call | flops 1811939328 | bytes 12582912 | tf_op jit(solution)/shard_map/own_planes/pallas_call | solution.py:318
  7.4 2.0 %collective-permute-done.above_ref = bf16[32,3072]{1,0:T(8,128)(2,1)S(1)} collective-permute-done((bf16[32,3072]{1,0:T(8,128)(2,1)S(1)}, bf16[32,3072]{1,0:T(8,128)(2,1)S(1)}, u32[]{:S(2)}, u32[]{:S(2)}) %collective-permute-start) | collective-permute-done | bytes 196640 | tf_op jit(solution)/shard_map/ppermute | solution.py:317
  9.5 2.3 %halo_and_early_half.1 = (bf16[4,16,3072]{2,1,0:T(8,128)(2,1)}, bf16[512,384]{1,0:T(8,128)(2,1)S(1)}, bf16[128,384]{1,0:T(8,128)(2,1)S(1)}, bf16[384,512]{1,0:T(...) custom-call(bf16[32,3072]{1,0:T(8,128)(2,1)S(1)} %collective-permute-done.above, ...), custom_call_target="tpu_custom_call" | custom-call | flops 905969664 | bytes 8388608 | tf_op jit(solution)/shard_map/halo_and_early_half/pallas_call | solution.py:339
  11.7 0.7 %collective-permute-start.1 = (bf16[48,2688]{1,0:T(8,128)(2,1)S(1)}, bf16[48,2688]{1,0:T(8,128)(2,1)S(1)}, u32[]{:S(2)}, u32[]{:S(2)}) collective-permute-start(bf16[48,2688]{1,0:T(8,128)(2,1)S(1)} %get-tuple-element.28), channel_id=1, source_target_pairs={{0,1},{1,0},{2,3},{3,2},{4,5},{5,4},{6,7},{7,6},{8,9},{9,8},{10,11... | collective-permute-start | bytes 774152 | tf_op jit(solution)/shard_map/ppermute | solution.py:359
  12.5 1.2 %later_half.1 = (bf16[48,2688]{1,0:T(8,128)(2,1)S(1)}, f32[48,2688]{1,0:T(8,128)S(1)}) custom-call(bf16[384,512]{1,0:T(8,128)(2,1)S(1)} %get-tuple-element.30.turned_ref, bf16[128,1536]{1,0:T(8,128)(2,1)S(1)} %get-tuple-element.31.edge, bf16[512,4608]{1,0:T(8,128)(2,1)S(1)} %get-tuple-element.21.wide), custom_call_target="tpu_custom_call" | custom-call | flops 905969664 | bytes 8388608 | tf_op jit(solution)/shard_map/later_half/pallas_call | solution.py:360
  13.7 0.1 collective-permute-start.2
  13.8 0.0 collective-permute-done.1.got_ref
  13.8 0.1 early_pair_sum.1
  13.8 2.5 %collective-permute-start.4 = (bf16[24,2688]{1,0:T(8,128)(2,1)S(1)}, bf16[24,2688]{1,0:T(8,128)(2,1)S(1)}, u32[]{:S(2)}, u32[]{:S(2)}) collective-permute-start(bf16[24,2688]{1,0:T(8,128)(2,1)S(1)} %get-tuple-element.37), channel_id=1, source_target_pairs={{0,6},{1,7},{2,4},{3,5},{4,2},{5,3},{6,0},{7,1},{8,14},{9,15},{10,... | collective-permute-start | bytes 387080 | tf_op jit(solution)/shard_map/ppermute | solution.py:381
  16.3 0.6 %collective-permute-start.5 = (bf16[24,2688]{1,0:T(8,128)(2,1)S(1)}, bf16[24,2688]{1,0:T(8,128)(2,1)S(1)}, u32[]{:S(2)}, u32[]{:S(2)}) collective-permute-start(bf16[24,2688]{1,0:T(8,128)(2,1)S(1)} %get-tuple-element.29.early_ref), channel_id=1, source_target_pairs={{0,4},{1,5},{2,6},{3,7},{4,0},{5,1},{6,2},{7,3},{8,12},{9,13},{10,... | collective-permute-start | bytes 387080 | tf_op jit(solution)/shard_map/ppermute | solution.py:381
  17.0 0.0 collective-permute-done.2.got_ref
  17.0 0.1 later_pair_sum.1
  17.0 1.4 %collective-permute-start.6 = (bf16[24,2688]{1,0:T(8,128)(2,1)S(1)}, bf16[24,2688]{1,0:T(8,128)(2,1)S(1)}, u32[]{:S(2)}, u32[]{:S(2)}) collective-permute-start(bf16[24,2688]{1,0:T(8,128)(2,1)S(1)} %get-tuple-element.38), channel_id=1, source_target_pairs={{0,2},{1,3},{2,0},{3,1},{4,6},{5,7},{6,4},{7,5},{8,10},{9,11},{10,... | collective-permute-start | bytes 387080 | tf_op jit(solution)/shard_map/ppermute | solution.py:392
  18.4 1.2 %collective-permute-start.3 = (bf16[128,384]{1,0:T(8,128)(2,1)S(1)}, bf16[128,384]{1,0:T(8,128)(2,1)S(1)}, u32[]{:S(2)}, u32[]{:S(2)}) collective-permute-start(bf16[128,384]{1,0:T(8,128)(2,1)S(1)} %get-tuple-element.35), channel_id=1, source_target_pairs={{1,0},{2,1},{3,2},{4,3},{5,4},{6,5},{7,6},{0,7},{9,8},{10,9},{11,1... | collective-permute-start | bytes 294920 | tf_op jit(solution)/shard_map/ppermute | solution.py:393
  19.6 2.4 %collective-permute-done.4.refs_0_ = bf16[24,2688]{1,0:T(8,128)(2,1)S(1)} collective-permute-done((bf16[24,2688]{1,0:T(8,128)(2,1)S(1)}, bf16[24,2688]{1,0:T(8,128)(2,1)S(1)}, u32[]{:S(2)}, u32[]{:S(2)}) %collective-permute-start.4) | collective-permute-done | bytes 129056 | tf_op jit(solution)/shard_map/ppermute | solution.py:381
  22.1 7.0 %collective-permute-done.5.refs_1_ = bf16[24,2688]{1,0:T(8,128)(2,1)S(1)} collective-permute-done((bf16[24,2688]{1,0:T(8,128)(2,1)S(1)}, bf16[24,2688]{1,0:T(8,128)(2,1)S(1)}, u32[]{:S(2)}, u32[]{:S(2)}) %collective-permute-start.5) | collective-permute-done | bytes 129056 | tf_op jit(solution)/shard_map/ppermute | solution.py:381
  29.1 0.0 collective-permute-done.6.refs_2_
  29.1 0.1 depth_sum.1.refs_0_
  29.2 2.5 %collective-permute-start.9 = (bf16[24,2688]{1,0:T(8,128)(2,1)S(1)}, bf16[24,2688]{1,0:T(8,128)(2,1)S(1)}, u32[]{:S(2)}, u32[]{:S(2)}) collective-permute-start(bf16[24,2688]{1,0:T(8,128)(2,1)S(1)} %depth_sum.1.refs_0_), channel_id=1, source_target_pairs={{0,24},{8,16},{16,8},{24,0},{1,25},{9,17},{17,9},{25,1},{2,26},{10... | collective-permute-start | bytes 387080 | tf_op jit(solution)/shard_map/ppermute | solution.py:413
  31.7 0.5 %collective-permute-start.8 = (bf16[24,2688]{1,0:T(8,128)(2,1)S(1)}, bf16[24,2688]{1,0:T(8,128)(2,1)S(1)}, u32[]{:S(2)}, u32[]{:S(2)}) collective-permute-start(bf16[24,2688]{1,0:T(8,128)(2,1)S(1)} %depth_sum.1.refs_0_), channel_id=1, source_target_pairs={{0,16},{8,24},{16,0},{24,8},{1,17},{9,25},{17,1},{25,9},{2,18},{10... | collective-permute-start | bytes 387080 | tf_op jit(solution)/shard_map/ppermute | solution.py:413
  32.2 0.5 %collective-permute-start.7 = (bf16[24,2688]{1,0:T(8,128)(2,1)S(1)}, bf16[24,2688]{1,0:T(8,128)(2,1)S(1)}, u32[]{:S(2)}, u32[]{:S(2)}) collective-permute-start(bf16[24,2688]{1,0:T(8,128)(2,1)S(1)} %depth_sum.1.refs_0_), channel_id=1, source_target_pairs={{0,8},{8,0},{16,24},{24,16},{1,9},{9,1},{17,25},{25,17},{2,10},{10... | collective-permute-start | bytes 387080 | tf_op jit(solution)/shard_map/ppermute | solution.py:413
  32.7 0.0 collective-permute-done.3.below_ref
  32.7 4.3 %input_grad.1 = bf16[8,32,3072]{2,1,0:T(8,128)(2,1)} custom-call(bf16[512,384]{1,0:T(8,128)(2,1)S(1)} %get-tuple-element.26.gp_ref, bf16[128,384]{1,0:T(8,128)(2,1)S(1)} %collective-permute-done.3.below_ref, bf16[4608,384]{1,0:T(8,128)(2,1)S(1)} %get-tuple-element.22.band), custom_call_target="tpu_custom_call" | custom-call | flops 1811939328 | bytes 8388608 | tf_op jit(solution)/shard_map/input_grad/pallas_call | solution.py:395
  37.1 0.0 collective-permute-done.9.refs_3_
  37.1 0.9 %collective-permute-done.8.refs_2_ = bf16[24,2688]{1,0:T(8,128)(2,1)S(1)} collective-permute-done((bf16[24,2688]{1,0:T(8,128)(2,1)S(1)}, bf16[24,2688]{1,0:T(8,128)(2,1)S(1)}, u32[]{:S(2)}, u32[]{:S(2)}) %collective-permute-start.8) | collective-permute-done | bytes 129056 | tf_op jit(solution)/shard_map/ppermute | solution.py:413
  38.0 0.1 collective-permute-done.7.refs_1_
  38.0 0.9 %sample_sum.1 = f32[27,24,96]{2,1,0:T(8,128)} custom-call(bf16[24,2688]{1,0:T(8,128)(2,1)S(1)} %depth_sum.1.refs_0_, bf16[24,2688]{1,0:T(8,128)(2,1)S(1)} %collective-permute-done.7.refs_1_, bf16[24,2688]{1,0:T(8,128)(2,1)S(1)} %collective-permute-done.8.refs_2_, bf16[24,2688]{1,0:T(8,128)(2,1)S(1)} %collective-permute-done.9.refs_3_), custom_call_target="tpu_custom_call" | custom-call | tf_op jit(solution)/shard_map/sample_sum/pallas_call | solution.py:414
Async XLA Ops:
  1.6 7.9 %collective-permute-start = (bf16[32,3072]{1,0:T(8,128)(2,1)S(1)}, bf16[32,3072]{1,0:T(8,128)(2,1)S(1)}, u32[]{:S(2)}, u32[]{:S(2)}) collective-permute-start(bf16[32,3072]{1,0:T(8,128)(2,1)S(1)} %edge_plane.1), channel_id=1, source_target_pairs={{0,1},{1,2},{2,3},{3,4},{4,5},{5,6},{6,7},{7,0},{8,9},{9,10},{10,1... | collective-permute-start | bytes 589832 | tf_op jit(solution)/shard_map/ppermute | solution.py:317
  11.7 2.1 %collective-permute-start.1 = (bf16[48,2688]{1,0:T(8,128)(2,1)S(1)}, bf16[48,2688]{1,0:T(8,128)(2,1)S(1)}, u32[]{:S(2)}, u32[]{:S(2)}) collective-permute-start(bf16[48,2688]{1,0:T(8,128)(2,1)S(1)} %get-tuple-element.28), channel_id=1, source_target_pairs={{0,1},{1,0},{2,3},{3,2},{4,5},{5,4},{6,7},{7,6},{8,9},{9,8},{10,11... | collective-permute-start | bytes 774152 | tf_op jit(solution)/shard_map/ppermute | solution.py:359
  13.7 3.3 %collective-permute-start.2 = (bf16[48,2688]{1,0:T(8,128)(2,1)S(1)}, bf16[48,2688]{1,0:T(8,128)(2,1)S(1)}, u32[]{:S(2)}, u32[]{:S(2)}) collective-permute-start(bf16[48,2688]{1,0:T(8,128)(2,1)S(1)} %get-tuple-element.33), channel_id=1, source_target_pairs={{0,1},{1,0},{2,3},{3,2},{4,5},{5,4},{6,7},{7,6},{8,9},{9,8},{10,11... | collective-permute-start | bytes 774152 | tf_op jit(solution)/shard_map/ppermute | solution.py:370
  13.8 8.2 %collective-permute-start.4 = (bf16[24,2688]{1,0:T(8,128)(2,1)S(1)}, bf16[24,2688]{1,0:T(8,128)(2,1)S(1)}, u32[]{:S(2)}, u32[]{:S(2)}) collective-permute-start(bf16[24,2688]{1,0:T(8,128)(2,1)S(1)} %get-tuple-element.37), channel_id=1, source_target_pairs={{0,6},{1,7},{2,4},{3,5},{4,2},{5,3},{6,0},{7,1},{8,14},{9,15},{10,... | collective-permute-start | bytes 387080 | tf_op jit(solution)/shard_map/ppermute | solution.py:381
  16.3 12.7 %collective-permute-start.5 = (bf16[24,2688]{1,0:T(8,128)(2,1)S(1)}, bf16[24,2688]{1,0:T(8,128)(2,1)S(1)}, u32[]{:S(2)}, u32[]{:S(2)}) collective-permute-start(bf16[24,2688]{1,0:T(8,128)(2,1)S(1)} %get-tuple-element.29.early_ref), channel_id=1, source_target_pairs={{0,4},{1,5},{2,6},{3,7},{4,0},{5,1},{6,2},{7,3},{8,12},{9,13},{10,... | collective-permute-start | bytes 387080 | tf_op jit(solution)/shard_map/ppermute | solution.py:381
  17.0 12.1 %collective-permute-start.6 = (bf16[24,2688]{1,0:T(8,128)(2,1)S(1)}, bf16[24,2688]{1,0:T(8,128)(2,1)S(1)}, u32[]{:S(2)}, u32[]{:S(2)}) collective-permute-start(bf16[24,2688]{1,0:T(8,128)(2,1)S(1)} %get-tuple-element.38), channel_id=1, source_target_pairs={{0,2},{1,3},{2,0},{3,1},{4,6},{5,7},{6,4},{7,5},{8,10},{9,11},{10,... | collective-permute-start | bytes 387080 | tf_op jit(solution)/shard_map/ppermute | solution.py:392
  18.4 14.3 %collective-permute-start.3 = (bf16[128,384]{1,0:T(8,128)(2,1)S(1)}, bf16[128,384]{1,0:T(8,128)(2,1)S(1)}, u32[]{:S(2)}, u32[]{:S(2)}) collective-permute-start(bf16[128,384]{1,0:T(8,128)(2,1)S(1)} %get-tuple-element.35), channel_id=1, source_target_pairs={{1,0},{2,1},{3,2},{4,3},{5,4},{6,5},{7,6},{0,7},{9,8},{10,9},{11,1... | collective-permute-start | bytes 294920 | tf_op jit(solution)/shard_map/ppermute | solution.py:393
  29.2 7.9 %collective-permute-start.9 = (bf16[24,2688]{1,0:T(8,128)(2,1)S(1)}, bf16[24,2688]{1,0:T(8,128)(2,1)S(1)}, u32[]{:S(2)}, u32[]{:S(2)}) collective-permute-start(bf16[24,2688]{1,0:T(8,128)(2,1)S(1)} %depth_sum.1.refs_0_), channel_id=1, source_target_pairs={{0,24},{8,16},{16,8},{24,0},{1,25},{9,17},{17,9},{25,1},{2,26},{10... | collective-permute-start | bytes 387080 | tf_op jit(solution)/shard_map/ppermute | solution.py:413
  31.7 6.3 %collective-permute-start.8 = (bf16[24,2688]{1,0:T(8,128)(2,1)S(1)}, bf16[24,2688]{1,0:T(8,128)(2,1)S(1)}, u32[]{:S(2)}, u32[]{:S(2)}) collective-permute-start(bf16[24,2688]{1,0:T(8,128)(2,1)S(1)} %depth_sum.1.refs_0_), channel_id=1, source_target_pairs={{0,16},{8,24},{16,0},{24,8},{1,17},{9,25},{17,1},{25,9},{2,18},{10... | collective-permute-start | bytes 387080 | tf_op jit(solution)/shard_map/ppermute | solution.py:413
  32.2 5.8 %collective-permute-start.7 = (bf16[24,2688]{1,0:T(8,128)(2,1)S(1)}, bf16[24,2688]{1,0:T(8,128)(2,1)S(1)}, u32[]{:S(2)}, u32[]{:S(2)}) collective-permute-start(bf16[24,2688]{1,0:T(8,128)(2,1)S(1)} %depth_sum.1.refs_0_), channel_id=1, source_target_pairs={{0,8},{8,0},{16,24},{24,16},{1,9},{9,1},{17,25},{25,17},{2,10},{10... | collective-permute-start | bytes 387080 | tf_op jit(solution)/shard_map/ppermute | solution.py:413

commit v2 on v1

--- a/solution.py
+++ b/solution.py
@@ -12,7 +12,9 @@
 BLOCK = 384
 SPAN = 512
 TAPS = 9
-TERM_TILES = -(-TAPS * 3 * CIN // 128)
+LOW = 640
+HIGH = 768
+MINE = LOW + HIGH
 F32 = jnp.float32
 BF16 = jnp.bfloat16
 VMEM_LIMIT = 12 * 1024 * 1024
@@ -120,15 +122,9 @@
         terms[:, base : base + BLOCK] += (even + odd)[:, :BLOCK]
 
 
-def share(terms, send_ref, keep_ref):
-    rows = send_ref.shape[0]
-    send_ref[...] = terms[:rows].astype(BF16)
-    keep_ref[...] = terms[rows:]
-
-
 def halo_kernel(
     width, above_ref, wide, band, pre_ref, cot_ref,
-    act_ref, gp_ref, first_ref, turned_ref, edge, send_ref, keep_ref, terms,
+    act_ref, gp_ref, first_ref, turned_ref, edge, send_ref, terms,
 ):
     outs = cot_ref.shape[0]
     cells = cot_ref.shape[2] // BLOCK
@@ -161,36 +157,33 @@
                 first_ref[at : at + 16] = grad
 
     rows = send_ref.shape[0]
-    half = lax.axis_size("space") // 4
-    high = rows // half
-    shape = (8 * rows, 2 * COUT)
+    steps = lax.axis_size("space") // 2
+    high = rows // steps
+    shape = (4 * rows, 2 * COUT)
     inner = iota(shape, 0)
-    later = inner >= 4 * rows
-    inner = inner - jnp.where(later, 4 * rows, 0)
-    odd = inner >= 2 * rows
-    inner = inner - jnp.where(odd, 2 * rows, 0)
-    kept = inner >= rows
-    inner = inner - jnp.where(kept, rows, 0)
+    kept = inner >= 2 * rows
+    inner = inner - jnp.where(kept, 2 * rows, 0)
+    odd = inner >= rows
+    inner = inner - jnp.where(odd, rows, 0)
     source = jnp.where(kept, core, 1 - core) * width + jnp.where(odd, COUT, 0)
-    for k in range(half):
+    for k in range(steps):
         channel = inner - k * high
         inside = (channel >= 0) & (channel < width)
-        target = jnp.where(later, chip ^ k, chip ^ (k + half)) * 2 * width
-        source = source + jnp.where(inside, channel + target, 0)
+        source = source + jnp.where(inside, channel + (chip ^ k) * 2 * width, 0)
         if high != width:
             source = jnp.where((channel >= width) & (channel < high), -1, source)
     order = jnp.where(iota(shape, 1) == source, 1.0, 0.0).astype(BF16)
     turned_ref[...] = dot_nt(order, gp_ref[...]).astype(BF16)
-    add_terms(turned_ref[: 4 * rows], edge, wide, terms)
-    share(terms, send_ref, keep_ref)
-
-
-def later_kernel(turned_ref, edge, wide, send_ref, keep_ref, terms):
-    add_terms(turned_ref[4 * send_ref.shape[0] :], edge, wide, terms)
-    share(terms, send_ref, keep_ref)
-
-
-def input_kernel(gp_ref, below_ref, band, out_ref):
+    add_terms(turned_ref[: 2 * rows], edge, wide, terms)
+    send_ref[...] = terms[...].astype(BF16)
+
+
+def keep_kernel(turned_ref, edge, wide, keep_ref):
+    add_terms(turned_ref[2 * keep_ref.shape[0] :], edge, wide, keep_ref)
+
+
+def input_kernel(gp_ref, below_ref, band, out_ref, done_ref):
+    done_ref[...] = jnp.zeros_like(done_ref)
     per_out = below_ref.shape[0]
     cells = per_out // 16
     here = gp_ref[...]
@@ -242,32 +235,64 @@
                 out_ref[2 * i + pd, :, m * BLOCK : (m + 1) * BLOCK] = mixed
 
 
-def early_pair_kernel(keep_ref, got_ref, *out_refs):
-    total = keep_ref[...] + got_ref[...].astype(F32)
-    high = out_refs[0].shape[0]
-    for k, ref in enumerate(out_refs):
-        ref[...] = total[k * high : (k + 1) * high].astype(ref.dtype)
-
-
-def later_pair_kernel(early_ref, keep_ref, got_ref, first_ref, passed_ref, *out_refs):
-    del early_ref
-    passed_ref[...] = first_ref[...]
-    early_pair_kernel(keep_ref, got_ref, *out_refs)
-
-
-def depth_kernel(own_ref, *refs):
+def sample_bits():
+    at = lax.axis_index("sample")
+    return at % 2, at // (lax.axis_size("sample") // 2)
+
+
+def pair_kernel(keep_ref, got_ref, mine_ref, low_ref, high_ref):
+    def total(start, lanes):
+        lanes = pl.ds(pl.multiple_of(start, 128), lanes)
+        return keep_ref[:, lanes] + got_ref[:, lanes].astype(F32)
+
+    low, high = sample_bits()
+    low_ref[...] = total((1 - low) * LOW, LOW).astype(BF16)
+    high_ref[...] = total(2 * LOW + (1 - high) * HIGH, HIGH).astype(BF16)
+    mine_ref[:, :LOW] = total(low * LOW, LOW)
+    mine_ref[:, LOW:] = total(2 * LOW + high * HIGH, HIGH)
+
+
+def cross_kernel(mine_ref, low_ref, high_ref, *out_refs):
+    for lanes, ref in ((slice(0, LOW), low_ref), (slice(LOW, MINE), high_ref)):
+        total = mine_ref[:, lanes] + ref[...].astype(F32)
+        high = out_refs[0].shape[0]
+        for k, out_ref in enumerate(out_refs):
+            out_ref[:, lanes] = total[k * high : (k + 1) * high].astype(out_ref.dtype)
+
+
+def depth_kernel(done_ref, own_ref, *refs):
+    del done_ref
     total = own_ref[...]
     for ref in refs[:-1]:
         total = total + ref[...].astype(F32)
     refs[-1][...] = total.astype(BF16)
 
 
+def tree(parts):
+    while len(parts) > 1:
+        parts = [parts[n] + parts[n + 1] for n in range(0, len(parts), 2)]
+    return parts[0]
+
+
 def sample_kernel(scale, *refs):
     out_ref = refs[-1]
-    parts = [ref[...].astype(F32) for ref in refs[:-1]]
-    while len(parts) > 1:
-        parts = [parts[n] + parts[n + 1] for n in range(0, len(parts), 2)]
-    total = parts[0][: out_ref.shape[1]] * scale
+    width = out_ref.shape[1]
+    parts = [ref[...].astype(F32)[:width] * scale for ref in refs[:-1]]
+    half = len(parts) // 2
+    here = tree([part[:, :LOW] for part in parts[0::2]])
+    there = tree([part[:, :LOW] for part in parts[1::2]])
+    above = tree([part[:, LOW:] for part in parts[:half]])
+    below = tree([part[:, LOW:] for part in parts[half:]])
+    low, high = (bit == 0 for bit in sample_bits())
+    total = jnp.concatenate(
+        [
+            jnp.where(low, here, there),
+            jnp.where(low, there, here),
+            jnp.where(high, above, below),
+            jnp.where(high, below, above),
+        ],
+        axis=1,
+    )
     for n in range(out_ref.shape[0]):
         out_ref[n] = total[:, n * CIN : (n + 1) * CIN]
 
@@ -284,9 +309,9 @@
     depth = space // 2
     width = COUT // space
     high = -(-width // 8) * 8
-    half = depth // 2
-    part = (high, TERM_TILES * 128)
-    group = (half * high, TERM_TILES * 128)
+    kept_rows = depth * high
+    terms = (kept_rows, 2 * MINE)
+    part = (high, MINE)
     cells = lanes // BLOCK
     per_out = cells * 16
     count = outs * per_out
@@ -335,68 +360,69 @@
         name="own_planes",
     )(x, w, cot)
 
-    terms = pltpu.VMEM((2 * group[0], group[1]), F32)
-    act, grad, first, turned, halo, send, keep = pl.pallas_call(
+    act, grad, first, turned, halo, send = pl.pallas_call(
         functools.partial(halo_kernel, width),
         out_shape=(
             shape(cot.shape, BF16),
             shape((count, BLOCK), BF16),
             shape((per_out, BLOCK), BF16),
-            shape((8 * group[0], count), BF16),
+            shape((4 * kept_rows, count), BF16),
             shape((per_out, 3 * SPAN), BF16),
-            shape(group, BF16),
-            shape(group, F32),
+            shape(terms, BF16),
         ),
         in_specs=[vmem] * 5,
-        out_specs=(vmem,) * 7,
-        scratch_shapes=[terms],
+        out_specs=(vmem,) * 6,
+        scratch_shapes=[pltpu.VMEM(terms, F32)],
         compiler_params=params,
         cost_estimate=pl.CostEstimate(
             flops=flops // 2, bytes_accessed=8 << 20, transcendentals=count * BLOCK
         ),
-        name="halo_and_early_half",
+        name="halo_and_sent_half",
     )(above, wide, band, preact, cot_in)
     got = lax.ppermute(send, "space", in_chip)
-    later_send, later_keep = pl.pallas_call(
-        later_kernel,
-        out_shape=(shape(group, BF16), shape(group, F32)),
-        in_specs=[vmem] * 3,
-        out_specs=(vmem,) * 2,
-        scratch_shapes=[terms],
-        compiler_params=params,
-        cost_estimate=pl.CostEstimate(flops=flops // 2, bytes_accessed=8 << 20, transcendentals=0),
-        name="later_half",
-    )(turned, halo, wide)
-    later_got = lax.ppermute(later_send, "space", in_chip)
-
-    early = pl.pallas_call(
-        early_pair_kernel,
-        out_shape=(shape(part, BF16),) * half,
-        in_specs=[vmem] * 2,
-        out_specs=(vmem,) * half,
-        compiler_params=params,
-        name="early_pair_sum",
-    )(keep, got)
-    came = [
-        lax.ppermute(early[k - half], "space", flipped(space, 2 * k))
-        for k in reversed(range(half, depth))
-    ]
-    first, own, *later = pl.pallas_call(
-        later_pair_kernel,
-        out_shape=(shape(first.shape, BF16), shape(part, F32)) + (shape(part, BF16),) * (half - 1),
-        in_specs=[vmem] * 4,
-        out_specs=(vmem,) * (half + 1),
-        compiler_params=params,
-        name="later_pair_sum",
-    )(early[0], later_keep, later_got, first)
-    came += [lax.ppermute(later[k - 1], "space", flipped(space, 2 * k)) for k in range(1, half)]
     below = lax.ppermute(first, "space", back)
-
-    grad_in = pl.pallas_call(
-        input_kernel,
-        out_shape=shape(x.shape, BF16),
+    keep = pl.pallas_call(
+        keep_kernel,
+        out_shape=shape(terms, F32),
         in_specs=[vmem] * 3,
         out_specs=vmem,
+        compiler_params=params,
+        cost_estimate=pl.CostEstimate(flops=flops // 2, bytes_accessed=8 << 20, transcendentals=0),
+        name="kept_half",
+    )(turned, halo, wide)
+
+    mine, low, high_lanes = pl.pallas_call(
+        pair_kernel,
+        out_shape=(
+            shape((kept_rows, MINE), F32),
+            shape((kept_rows, LOW), BF16),
+            shape((kept_rows, HIGH), BF16),
+        ),
+        in_specs=[vmem] * 2,
+        out_specs=(vmem,) * 3,
+        compiler_params=params,
+        name="pair_sum",
+    )(keep, got)
+    low = lax.ppermute(low, "sample", flipped(sample, 1))
+    high_lanes = lax.ppermute(high_lanes, "sample", flipped(sample, sample // 2))
+    own, *leaving = pl.pallas_call(
+        cross_kernel,
+        out_shape=(shape(part, F32),) + (shape(part, BF16),) * (depth - 1),
+        in_specs=[vmem] * 3,
+        out_specs=(vmem,) * depth,
+        compiler_params=params,
+        name="cross_sum",
+    )(mine, low, high_lanes)
+    came = [
+        lax.ppermute(leaving[k - 1], "space", flipped(space, 2 * k))
+        for k in reversed(range(1, depth))
+    ]
+
+    grad_in, done = pl.pallas_call(
+        input_kernel,
+        out_shape=(shape(x.shape, BF16), shape((8, 128), F32)),
+        in_specs=[vmem] * 3,
+        out_specs=(vmem, vmem),
         compiler_params=params,
         cost_estimate=pl.CostEstimate(flops=flops, bytes_accessed=8 << 20, transcendentals=0),
         name="input_grad",
@@ -405,11 +431,11 @@
     total = pl.pallas_call(
         depth_kernel,
         out_shape=shape(part, BF16),
-        in_specs=[vmem] * depth,
+        in_specs=[vmem] * (depth + 1),
         out_specs=vmem,
         compiler_params=params,
         name="depth_sum",
-    )(own, *came)
+    )(done, own, *came)
     others = [lax.ppermute(total, "sample", flipped(sample, j)) for j in range(1, sample)]
     kernel_grad = pl.pallas_call(
         functools.partial(sample_kernel, 1.0 / (samples * sample)),

time: 39.1 us -> 39 us (level)
  waiting for transfers between devices: 12.4 us -> 8.53 us
  starting transfers between devices: 10.6 us -> 13.9 us
  Pallas kernels: 15.2 us -> 15.8 us
    ppermute x4 -> x5, waiting for transfers between devices: 9.43 us -> 2.35 us  [the longest x1 2.18 us: per_device(): low = lax.ppermute(low, 'sample', flipped(sample, 1))]
    ppermute x4 -> x5, starting transfers between devices: 4.6 us -> 7.8 us  [the longest x3 4.45 us: per_device(): lax.ppermute(leaving[k - 1], 'space', flipped(space, 2 * k))]
    ppermute x3, waiting for transfers between devices: 0.95 us -> 3.74 us  [per_device(): lax.ppermute(total, 'sample', flipped(sample, j))]
    pallas_call x1, Pallas kernels: 2.26 us -> 2.88 us  [per_device(): pl.pallas_call(functools.partial(halo_kernel, width), out_shape=(shape(co...]
  transfers between devices with their start and end apart: 10 -> 11, of which waited for: 5 -> 7; matrix products, arithmetic and copies ran while one was open for 0% -> 0% of each run, Pallas kernels for 29% -> 28%
where the time goes in v2:
time: 39 us; the launch traced here: 38.9 us
  Pallas kernels  15.8 us (41%)
  starting transfers between devices  13.9 us (36%)
  waiting for transfers between devices  8.53 us (22%)
  between operations  0.67 us (2%)
    pallas_call x1, Pallas kernels, per_device(): pl.pallas_call(functools.partial(own_kernel, planes), out_shape=(shape((c...  5.3 us
    ppermute x3, starting transfers between devices, per_device(): lax.ppermute(leaving[k - 1], 'space', flipped(space, 2 * k))  4.45 us
    pallas_call x1, Pallas kernels, per_device(): pl.pallas_call(input_kernel, out_shape=(shape(x.shape, BF16), shape((8, 1...  4.35 us
    ppermute x3, waiting for transfers between devices, per_device(): lax.ppermute(total, 'sample', flipped(sample, j))  3.74 us
    ppermute x3, starting transfers between devices, per_device(): lax.ppermute(total, 'sample', flipped(sample, j))  3.55 us
    pallas_call x1, Pallas kernels, per_device(): pl.pallas_call(functools.partial(halo_kernel, width), out_shape=(shape(co...  2.88 us
    ppermute x1, waiting for transfers between devices, per_device(): low = lax.ppermute(low, 'sample', flipped(sample, 1))  2.18 us
    ppermute x1, waiting for transfers between devices, per_device(): above = lax.ppermute(edge, 'space', onward)  2.08 us
  transfers between devices with their start and end apart: 11, of which 7 were waited for; matrix products, arithmetic and copies ran while one was open for 0% of the time, Pallas kernels for 28%

profile of v2, /device:TPU:0, one launch (start us, length us, event | category | flops | bytes accessed | tf_op | source)
XLA Modules:
  0.0 38.9 jit_solution(14845290701501057802)
XLA Ops:
  0.6 0.9 %edge_plane.1 = bf16[32,3072]{1,0:T(8,128)(2,1)S(1)} custom-call(bf16[8,32,3072]{2,1,0:T(8,128)(2,1)} %bitcast.8), custom_call_target="tpu_custom_call" | custom-call | tf_op jit(solution)/shard_map/edge_plane/pallas_call | solution.py:333
  1.6 0.5 %collective-permute-start = (bf16[32,3072]{1,0:T(8,128)(2,1)S(1)}, bf16[32,3072]{1,0:T(8,128)(2,1)S(1)}, u32[]{:S(2)}, u32[]{:S(2)}) collective-permute-start(bf16[32,3072]{1,0:T(8,128)(2,1)S(1)} %edge_plane.1), channel_id=1, source_target_pairs={{0,1},{1,2},{2,3},{3,4},{4,5},{5,6},{6,7},{7,0},{8,9},{9,10},{10,1... | collective-permute-start | bytes 589832 | tf_op jit(solution)/shard_map/ppermute | solution.py:342
  2.1 5.3 %own_planes.1 = (bf16[512,4608]{1,0:T(8,128)(2,1)S(1)}, bf16[4608,384]{1,0:T(8,128)(2,1)S(1)}, f32[512,384]{1,0:T(8,128)S(1)}, bf16[4,16,3072]{2,1,0:T(8,128)(2,1)S(1)}) custom-call(bf16[8,32,3072]{2,1,0:T(8,128)(2,1)} %bitcast.9, bf16[9,288,192]{2,1,0:T(8,128)(2,1)} %bitcast.11, bf16[4,16,3072]{2,1,0:T(8,128)(2,1)} %bitcast.12), custom_call_target="tpu_custom_call" | custom-call | flops 1811939328 | bytes 12582912 | tf_op jit(solution)/shard_map/own_planes/pallas_call | solution.py:343
  7.4 2.1 %collective-permute-done.above_ref = bf16[32,3072]{1,0:T(8,128)(2,1)S(1)} collective-permute-done((bf16[32,3072]{1,0:T(8,128)(2,1)S(1)}, bf16[32,3072]{1,0:T(8,128)(2,1)S(1)}, u32[]{:S(2)}, u32[]{:S(2)}) %collective-permute-start) | collective-permute-done | bytes 196640 | tf_op jit(solution)/shard_map/ppermute | solution.py:342
  9.5 2.9 %halo_and_sent_half.1 = (bf16[4,16,3072]{2,1,0:T(8,128)(2,1)}, bf16[512,384]{1,0:T(8,128)(2,1)S(1)}, bf16[128,384]{1,0:T(8,128)(2,1)S(1)}, bf16[384,512]{1,0:T(8...) custom-call(bf16[32,3072]{1,0:T(8,128)(2,1)S(1)} %collective-permute-done.above_ref, ...), custom_call_target="tpu_custom_call" | custom-call | flops 905969664 | bytes 8388608 | tf_op jit(solution)/shard_map/halo_and_sent_half/pallas_call | solution.py:363
  12.4 0.6 %collective-permute-start.2 = (bf16[96,2816]{1,0:T(8,128)(2,1)S(1)}, bf16[96,2816]{1,0:T(8,128)(2,1)S(1)}, u32[]{:S(2)}, u32[]{:S(2)}) collective-permute-start(bf16[96,2816]{1,0:T(8,128)(2,1)S(1)} %get-tuple-element.33), channel_id=1, source_target_pairs={{0,1},{1,0},{2,3},{3,2},{4,5},{5,4},{6,7},{7,6},{8,9},{9,8},{10,11... | collective-permute-start | bytes 1622024 | tf_op jit(solution)/shard_map/ppermute | solution.py:382
  13.0 1.2 %kept_half.1.keep_ref = f32[96,2816]{1,0:T(8,128)S(1)} custom-call(bf16[384,512]{1,0:T(8,128)(2,1)S(1)} %get-tuple-element.31.turned_ref, bf16[128,1536]{1,0:T(8,128)(2,1)S(1)} %get-tuple-element.32.edge, bf16[512,4608]{1,0:T(8,128)(2,1)S(1)} %get-tuple-element.22.wide), custom_call_target="tpu_custom_call" | custom-call | flops 905969664 | bytes 8388608 | tf_op jit(solution)/shard_map/kept_half/pallas_call | solution.py:384
  14.2 0.4 collective-permute-done.2.got_ref
  14.5 0.1 pair_sum.1
  14.6 1.9 %collective-permute-start.4 = (bf16[96,768]{1,0:T(8,128)(2,1)S(1)}, bf16[96,768]{1,0:T(8,128)(2,1)S(1)}, u32[]{:S(2)}, u32[]{:S(2)}) collective-permute-start(bf16[96,768]{1,0:T(8,128)(2,1)S(1)} %get-tuple-element.36), channel_id=1, source_target_pairs={{0,16},{8,24},{16,0},{24,8},{1,17},{9,25},{17,1},{25,9},{2,18},{10... | collective-permute-start | bytes 442376 | tf_op jit(solution)/shard_map/ppermute | solution.py:407
  16.5 1.5 %collective-permute-start.3 = (bf16[96,640]{1,0:T(8,128)(2,1)S(1)}, bf16[96,640]{1,0:T(8,128)(2,1)S(1)}, u32[]{:S(2)}, u32[]{:S(2)}) collective-permute-start(bf16[96,640]{1,0:T(8,128)(2,1)S(1)} %get-tuple-element.35), channel_id=1, source_target_pairs={{0,8},{8,0},{16,24},{24,16},{1,9},{9,1},{17,25},{25,17},{2,10},{10... | collective-permute-start | bytes 368648 | tf_op jit(solution)/shard_map/ppermute | solution.py:406
  18.0 1.4 %collective-permute-start.1 = (bf16[128,384]{1,0:T(8,128)(2,1)S(1)}, bf16[128,384]{1,0:T(8,128)(2,1)S(1)}, u32[]{:S(2)}, u32[]{:S(2)}) collective-permute-start(bf16[128,384]{1,0:T(8,128)(2,1)S(1)} %get-tuple-element.28), channel_id=1, source_target_pairs={{1,0},{2,1},{3,2},{4,3},{5,4},{6,5},{7,6},{0,7},{9,8},{10,9},{11,1... | collective-permute-start | bytes 294920 | tf_op jit(solution)/shard_map/ppermute | solution.py:383
  19.4 2.2 %collective-permute-done.3.low_ref = bf16[96,640]{1,0:T(8,128)(2,1)S(1)} collective-permute-done((bf16[96,640]{1,0:T(8,128)(2,1)S(1)}, bf16[96,640]{1,0:T(8,128)(2,1)S(1)}, u32[]{:S(2)}, u32[]{:S(2)}) %collective-permute-start.3) | collective-permute-done | bytes 122912 | tf_op jit(solution)/shard_map/ppermute | solution.py:406
  21.6 0.0 collective-permute-done.4.high_ref
  21.6 0.1 cross_sum.1
  21.7 2.3 %collective-permute-start.5 = (bf16[24,1408]{1,0:T(8,128)(2,1)S(1)}, bf16[24,1408]{1,0:T(8,128)(2,1)S(1)}, u32[]{:S(2)}, u32[]{:S(2)}) collective-permute-start(bf16[24,1408]{1,0:T(8,128)(2,1)S(1)} %get-tuple-element.38), channel_id=1, source_target_pairs={{0,6},{1,7},{2,4},{3,5},{4,2},{5,3},{6,0},{7,1},{8,14},{9,15},{10,... | collective-permute-start | bytes 202760 | tf_op jit(solution)/shard_map/ppermute | solution.py:417
  24.0 0.8 %collective-permute-start.6 = (bf16[24,1408]{1,0:T(8,128)(2,1)S(1)}, bf16[24,1408]{1,0:T(8,128)(2,1)S(1)}, u32[]{:S(2)}, u32[]{:S(2)}) collective-permute-start(bf16[24,1408]{1,0:T(8,128)(2,1)S(1)} %get-tuple-element.39), channel_id=1, source_target_pairs={{0,4},{1,5},{2,6},{3,7},{4,0},{5,1},{6,2},{7,3},{8,12},{9,13},{10,... | collective-permute-start | bytes 202760 | tf_op jit(solution)/shard_map/ppermute | solution.py:417
  24.7 1.4 %collective-permute-start.7 = (bf16[24,1408]{1,0:T(8,128)(2,1)S(1)}, bf16[24,1408]{1,0:T(8,128)(2,1)S(1)}, u32[]{:S(2)}, u32[]{:S(2)}) collective-permute-start(bf16[24,1408]{1,0:T(8,128)(2,1)S(1)} %get-tuple-element.40), channel_id=1, source_target_pairs={{0,2},{1,3},{2,0},{3,1},{4,6},{5,7},{6,4},{7,5},{8,10},{9,11},{10,... | collective-permute-start | bytes 202760 | tf_op jit(solution)/shard_map/ppermute | solution.py:417
  26.1 0.0 collective-permute-done.1.below_ref
  26.1 4.3 %input_grad.1 = (bf16[8,32,3072]{2,1,0:T(8,128)(2,1)}, f32[8,128]{1,0:T(8,128)S(1)}) custom-call(bf16[512,384]{1,0:T(8,128)(2,1)S(1)} %get-tuple-element.27.gp_ref, bf16[128,384]{1,0:T(8,128)(2,1)S(1)} %collective-permute-done.1.below_ref, bf16[4608,384]{1,0:T(8,128)(2,1)S(1)} %get-tuple-element.23.band), custom_call_target="tpu_custom_call" | custom-call | flops 1811939328 | bytes 8388608 | tf_op jit(solution)/shard_map/input_grad/pallas_call | solution.py:421
  30.5 0.0 collective-permute-done.5.refs_0_
  30.5 0.2 collective-permute-done.6.refs_1_
  30.6 0.0 collective-permute-done.7.refs_2_
  30.7 1.8 %collective-permute-start.10 = (bf16[24,1408]{1,0:T(8,128)(2,1)S(1)}, bf16[24,1408]{1,0:T(8,128)(2,1)S(1)}, u32[]{:S(2)}, u32[]{:S(2)}) collective-permute-start(bf16[24,1408]{1,0:T(8,128)(2,1)S(1)} %depth_sum.1.refs_0_), channel_id=1, source_target_pairs={{0,24},{8,16},{16,8},{24,0},{1,25},{9,17},{17,9},{25,1},{2,26},{10... | collective-permute-start | bytes 202760 | tf_op jit(solution)/shard_map/ppermute | solution.py:439
  32.5 1.2 %collective-permute-start.9 = (bf16[24,1408]{1,0:T(8,128)(2,1)S(1)}, bf16[24,1408]{1,0:T(8,128)(2,1)S(1)}, u32[]{:S(2)}, u32[]{:S(2)}) collective-permute-start(bf16[24,1408]{1,0:T(8,128)(2,1)S(1)} %depth_sum.1.refs_0_), channel_id=1, source_target_pairs={{0,16},{8,24},{16,0},{24,8},{1,17},{9,25},{17,1},{25,9},{2,18},{10... | collective-permute-start | bytes 202760 | tf_op jit(solution)/shard_map/ppermute | solution.py:439
  33.7 0.5 %collective-permute-start.8 = (bf16[24,1408]{1,0:T(8,128)(2,1)S(1)}, bf16[24,1408]{1,0:T(8,128)(2,1)S(1)}, u32[]{:S(2)}, u32[]{:S(2)}) collective-permute-start(bf16[24,1408]{1,0:T(8,128)(2,1)S(1)} %depth_sum.1.refs_0_), channel_id=1, source_target_pairs={{0,8},{8,0},{16,24},{24,16},{1,9},{9,1},{17,25},{25,17},{2,10},{10... | collective-permute-start | bytes 202760 | tf_op jit(solution)/shard_map/ppermute | solution.py:439
  34.2 2.0 %collective-permute-done.10.refs_3_ = bf16[24,1408]{1,0:T(8,128)(2,1)S(1)} collective-permute-done((bf16[24,1408]{1,0:T(8,128)(2,1)S(1)}, bf16[24,1408]{1,0:T(8,128)(2,1)S(1)}, u32[]{:S(2)}, u32[]{:S(2)}) %collective-permute-start.10) | collective-permute-done | bytes 67616 | tf_op jit(solution)/shard_map/ppermute | solution.py:439
  36.3 0.6 %collective-permute-done.9.refs_2_ = bf16[24,1408]{1,0:T(8,128)(2,1)S(1)} collective-permute-done((bf16[24,1408]{1,0:T(8,128)(2,1)S(1)}, bf16[24,1408]{1,0:T(8,128)(2,1)S(1)}, u32[]{:S(2)}, u32[]{:S(2)}) %collective-permute-start.9) | collective-permute-done | bytes 67616 | tf_op jit(solution)/shard_map/ppermute | solution.py:439
  36.9 1.1 %collective-permute-done.8.refs_1_ = bf16[24,1408]{1,0:T(8,128)(2,1)S(1)} collective-permute-done((bf16[24,1408]{1,0:T(8,128)(2,1)S(1)}, bf16[24,1408]{1,0:T(8,128)(2,1)S(1)}, u32[]{:S(2)}, u32[]{:S(2)}) %collective-permute-start.8) | collective-permute-done | bytes 67616 | tf_op jit(solution)/shard_map/ppermute | solution.py:439
  38.0 0.9 %sample_sum.1 = f32[27,24,96]{2,1,0:T(8,128)} custom-call(bf16[24,1408]{1,0:T(8,128)(2,1)S(1)} %depth_sum.1.refs_0_, bf16[24,1408]{1,0:T(8,128)(2,1)S(1)} %collective-permute-done.8.refs_1_, bf16[24,1408]{1,0:T(8,128)(2,1)S(1)} %collective-permute-done.9.refs_2_, bf16[24,1408]{1,0:T(8,128)(2,1)S(1)} %collective-permute-done.10.refs_3_), custom_call_target="tpu_custom_call" | custom-call | tf_op jit(solution)/shard_map/sample_sum/pallas_call | solution.py:440
  (1 shorter events, 0.0 us)
Async XLA Ops:
  1.6 7.9 %collective-permute-start = (bf16[32,3072]{1,0:T(8,128)(2,1)S(1)}, bf16[32,3072]{1,0:T(8,128)(2,1)S(1)}, u32[]{:S(2)}, u32[]{:S(2)}) collective-permute-start(bf16[32,3072]{1,0:T(8,128)(2,1)S(1)} %edge_plane.1), channel_id=1, source_target_pairs={{0,1},{1,2},{2,3},{3,4},{4,5},{5,6},{6,7},{7,0},{8,9},{9,10},{10,1... | collective-permute-start | bytes 589832 | tf_op jit(solution)/shard_map/ppermute | solution.py:342
  12.4 2.2 %collective-permute-start.2 = (bf16[96,2816]{1,0:T(8,128)(2,1)S(1)}, bf16[96,2816]{1,0:T(8,128)(2,1)S(1)}, u32[]{:S(2)}, u32[]{:S(2)}) collective-permute-start(bf16[96,2816]{1,0:T(8,128)(2,1)S(1)} %get-tuple-element.33), channel_id=1, source_target_pairs={{0,1},{1,0},{2,3},{3,2},{4,5},{5,4},{6,7},{7,6},{8,9},{9,8},{10,11... | collective-permute-start | bytes 1622024 | tf_op jit(solution)/shard_map/ppermute | solution.py:382
  14.6 6.9 %collective-permute-start.4 = (bf16[96,768]{1,0:T(8,128)(2,1)S(1)}, bf16[96,768]{1,0:T(8,128)(2,1)S(1)}, u32[]{:S(2)}, u32[]{:S(2)}) collective-permute-start(bf16[96,768]{1,0:T(8,128)(2,1)S(1)} %get-tuple-element.36), channel_id=1, source_target_pairs={{0,16},{8,24},{16,0},{24,8},{1,17},{9,25},{17,1},{25,9},{2,18},{10... | collective-permute-start | bytes 442376 | tf_op jit(solution)/shard_map/ppermute | solution.py:407
  16.5 5.1 %collective-permute-start.3 = (bf16[96,640]{1,0:T(8,128)(2,1)S(1)}, bf16[96,640]{1,0:T(8,128)(2,1)S(1)}, u32[]{:S(2)}, u32[]{:S(2)}) collective-permute-start(bf16[96,640]{1,0:T(8,128)(2,1)S(1)} %get-tuple-element.35), channel_id=1, source_target_pairs={{0,8},{8,0},{16,24},{24,16},{1,9},{9,1},{17,25},{25,17},{2,10},{10... | collective-permute-start | bytes 368648 | tf_op jit(solution)/shard_map/ppermute | solution.py:406
  18.0 8.1 %collective-permute-start.1 = (bf16[128,384]{1,0:T(8,128)(2,1)S(1)}, bf16[128,384]{1,0:T(8,128)(2,1)S(1)}, u32[]{:S(2)}, u32[]{:S(2)}) collective-permute-start(bf16[128,384]{1,0:T(8,128)(2,1)S(1)} %get-tuple-element.28), channel_id=1, source_target_pairs={{1,0},{2,1},{3,2},{4,3},{5,4},{6,5},{7,6},{0,7},{9,8},{10,9},{11,1... | collective-permute-start | bytes 294920 | tf_op jit(solution)/shard_map/ppermute | solution.py:383
  21.7 8.8 %collective-permute-start.5 = (bf16[24,1408]{1,0:T(8,128)(2,1)S(1)}, bf16[24,1408]{1,0:T(8,128)(2,1)S(1)}, u32[]{:S(2)}, u32[]{:S(2)}) collective-permute-start(bf16[24,1408]{1,0:T(8,128)(2,1)S(1)} %get-tuple-element.38), channel_id=1, source_target_pairs={{0,6},{1,7},{2,4},{3,5},{4,2},{5,3},{6,0},{7,1},{8,14},{9,15},{10,... | collective-permute-start | bytes 202760 | tf_op jit(solution)/shard_map/ppermute | solution.py:417
  24.0 6.7 %collective-permute-start.6 = (bf16[24,1408]{1,0:T(8,128)(2,1)S(1)}, bf16[24,1408]{1,0:T(8,128)(2,1)S(1)}, u32[]{:S(2)}, u32[]{:S(2)}) collective-permute-start(bf16[24,1408]{1,0:T(8,128)(2,1)S(1)} %get-tuple-element.39), channel_id=1, source_target_pairs={{0,4},{1,5},{2,6},{3,7},{4,0},{5,1},{6,2},{7,3},{8,12},{9,13},{10,... | collective-permute-start | bytes 202760 | tf_op jit(solution)/shard_map/ppermute | solution.py:417
  24.7 5.9 %collective-permute-start.7 = (bf16[24,1408]{1,0:T(8,128)(2,1)S(1)}, bf16[24,1408]{1,0:T(8,128)(2,1)S(1)}, u32[]{:S(2)}, u32[]{:S(2)}) collective-permute-start(bf16[24,1408]{1,0:T(8,128)(2,1)S(1)} %get-tuple-element.40), channel_id=1, source_target_pairs={{0,2},{1,3},{2,0},{3,1},{4,6},{5,7},{6,4},{7,5},{8,10},{9,11},{10,... | collective-permute-start | bytes 202760 | tf_op jit(solution)/shard_map/ppermute | solution.py:417
  30.7 5.6 %collective-permute-start.10 = (bf16[24,1408]{1,0:T(8,128)(2,1)S(1)}, bf16[24,1408]{1,0:T(8,128)(2,1)S(1)}, u32[]{:S(2)}, u32[]{:S(2)}) collective-permute-start(bf16[24,1408]{1,0:T(8,128)(2,1)S(1)} %depth_sum.1.refs_0_), channel_id=1, source_target_pairs={{0,24},{8,16},{16,8},{24,0},{1,25},{9,17},{17,9},{25,1},{2,26},{10... | collective-permute-start | bytes 202760 | tf_op jit(solution)/shard_map/ppermute | solution.py:439
  32.5 4.4 %collective-permute-start.9 = (bf16[24,1408]{1,0:T(8,128)(2,1)S(1)}, bf16[24,1408]{1,0:T(8,128)(2,1)S(1)}, u32[]{:S(2)}, u32[]{:S(2)}) collective-permute-start(bf16[24,1408]{1,0:T(8,128)(2,1)S(1)} %depth_sum.1.refs_0_), channel_id=1, source_target_pairs={{0,16},{8,24},{16,0},{24,8},{1,17},{9,25},{17,1},{25,9},{2,18},{10... | collective-permute-start | bytes 202760 | tf_op jit(solution)/shard_map/ppermute | solution.py:439
  33.7 4.3 %collective-permute-start.8 = (bf16[24,1408]{1,0:T(8,128)(2,1)S(1)}, bf16[24,1408]{1,0:T(8,128)(2,1)S(1)}, u32[]{:S(2)}, u32[]{:S(2)}) collective-permute-start(bf16[24,1408]{1,0:T(8,128)(2,1)S(1)} %depth_sum.1.refs_0_), channel_id=1, source_target_pairs={{0,8},{8,0},{16,24},{24,16},{1,9},{9,1},{17,25},{25,17},{2,10},{10... | collective-permute-start | bytes 202760 | tf_op jit(solution)/shard_map/ppermute | solution.py:439

commit v3 on v2

--- a/solution.py
+++ b/solution.py
@@ -56,27 +56,50 @@
         wide[at : at + 16, tap * SPAN : tap * SPAN + 128] = jnp.zeros((16, 128), BF16)
 
 
-def edge_kernel(x_hbm, edge_ref, sem):
+def edge_kernel(width, x_hbm, edge_ref, split_ref, order_ref, sem):
     copy = pltpu.make_async_copy(x_hbm.at[x_hbm.shape[0] - 1], edge_ref, sem)
     copy.start()
+    split_ref[...] = row_split(x_hbm.shape[0])
+    at = lax.axis_index("space")
+    core = at % 2
+    chip = at // 2
+    steps = lax.axis_size("space") // 2
+    shape = order_ref.shape
+    rows = shape[0] // 4
+    high = rows // steps
+    inner = iota(shape, 0)
+    kept = inner >= 2 * rows
+    inner = inner - jnp.where(kept, 2 * rows, 0)
+    odd = inner >= rows
+    inner = inner - jnp.where(odd, rows, 0)
+    source = jnp.where(kept, core, 1 - core) * width + jnp.where(odd, COUT, 0)
+    for k in range(steps):
+        channel = inner - k * high
+        inside = (channel >= 0) & (channel < width)
+        source = source + jnp.where(inside, channel + (chip ^ k) * 2 * width, 0)
+        if high != width:
+            source = jnp.where((channel >= width) & (channel < high), -1, source)
+    order_ref[...] = jnp.where(iota(shape, 1) == source, 1.0, 0.0).astype(BF16)
     copy.wait()
 
 
-def own_kernel(
-    planes, x_hbm, w_hbm, cot_hbm, wide, band, preact, cot_ref, x_ref, w_ref, sems
-):
+def by_parity(wide, even_band, odd_band, taps):
+    sides = []
+    for start, band in ((0, even_band), (SPAN - BLOCK, odd_band)):
+        windows = [wide[:, tap * SPAN + start : tap * SPAN + start + BLOCK] for tap in range(taps)]
+        sides.append(dot(jnp.concatenate(windows, axis=1), band[: taps * BLOCK]))
+    return sides
+
+
+def own_kernel(x_ref, split_ref, w_hbm, wide, even_band, odd_band, preact, w_ref, sem):
+    planes = x_ref.shape[0]
     outs = planes // 2
     cells = x_ref.shape[2] // BLOCK
     per_out = cells * 16
-    x_copy = pltpu.make_async_copy(x_hbm, x_ref, sems.at[0])
-    w_copy = pltpu.make_async_copy(w_hbm, w_ref, sems.at[1])
-    cot_copy = pltpu.make_async_copy(cot_hbm, cot_ref, sems.at[2])
-    x_copy.start()
-    w_copy.start()
-    cot_copy.start()
-    split = row_split(planes)
+    copy = pltpu.make_async_copy(w_hbm, w_ref, sem)
+    copy.start()
+    split = split_ref[...]
     wide[0:per_out, 0 : 3 * SPAN] = jnp.zeros((per_out, 3 * SPAN), BF16)
-    x_copy.wait()
     x = x_ref[...].reshape(planes * 32, x_ref.shape[2])
     for m in range(cells):
         rows = dot(split, x[:, m * BLOCK : (m + 1) * BLOCK]).astype(BF16)
@@ -89,14 +112,17 @@
                     put(wide, per_out, cells, p // 2, m, 6 + b, piece)
                     if p // 2 + 1 < outs:
                         put(wide, per_out, cells, p // 2 + 1, m, b, piece)
-    w_copy.wait()
+    copy.wait()
     for tap in range(TAPS):
-        w = w_ref[tap]
-        even = jnp.concatenate([blank(32, COUT), w, blank(192, COUT)], axis=0)
-        odd = jnp.concatenate([blank(224, COUT), w], axis=0)
-        band[tap * SPAN : (tap + 1) * SPAN] = jnp.concatenate([even, odd], axis=1)
-    preact[...] = dot(wide[...], band[...])
-    cot_copy.wait()
+        at = tap * BLOCK
+        even_band[at : at + 32] = blank(32, COUT)
+        even_band[at + 32 : at + 320] = w_ref[tap]
+        even_band[at + 320 : at + BLOCK] = blank(64, COUT)
+        odd_band[at : at + 96] = blank(96, COUT)
+        odd_band[at + 96 : at + BLOCK] = w_ref[tap]
+    even, odd = by_parity(wide, even_band, odd_band, TAPS)
+    preact[:, :COUT] = even
+    preact[:, COUT:] = odd
 
 
 def add_terms(turned, edge, wide, terms):
@@ -123,24 +149,22 @@
 
 
 def halo_kernel(
-    width, above_ref, wide, band, pre_ref, cot_ref,
+    above_ref, order_ref, wide, even_band, odd_band, pre_ref, cot_ref,
     act_ref, gp_ref, first_ref, turned_ref, edge, send_ref, terms,
 ):
     outs = cot_ref.shape[0]
     cells = cot_ref.shape[2] // BLOCK
     per_out = cells * 16
-    at = lax.axis_index("space")
-    core = at % 2
-    chip = at // 2
+    top = lax.axis_index("space") == 0
     split_one = row_split(1)
     for m in range(cells):
         lanes = slice(m * BLOCK, (m + 1) * BLOCK)
         plane = above_ref[:, lanes]
-        plane = jnp.where(core + chip == 0, jnp.zeros_like(plane), plane)
+        plane = jnp.where(top, jnp.zeros_like(plane), plane)
         above = dot(split_one, plane).astype(BF16)
         for b in range(3):
             put(edge, per_out, cells, 0, m, b, above[b * 16 : b * 16 + 16])
-    added = dot(edge[...], band[: 3 * SPAN])
+    added = jnp.concatenate(by_parity(edge, even_band, odd_band, 3), axis=1)
     for i in range(outs):
         for m in range(cells):
             lanes = slice(m * BLOCK, (m + 1) * BLOCK)
@@ -156,25 +180,8 @@
             if i == 0:
                 first_ref[at : at + 16] = grad
 
-    rows = send_ref.shape[0]
-    steps = lax.axis_size("space") // 2
-    high = rows // steps
-    shape = (4 * rows, 2 * COUT)
-    inner = iota(shape, 0)
-    kept = inner >= 2 * rows
-    inner = inner - jnp.where(kept, 2 * rows, 0)
-    odd = inner >= rows
-    inner = inner - jnp.where(odd, rows, 0)
-    source = jnp.where(kept, core, 1 - core) * width + jnp.where(odd, COUT, 0)
-    for k in range(steps):
-        channel = inner - k * high
-        inside = (channel >= 0) & (channel < width)
-        source = source + jnp.where(inside, channel + (chip ^ k) * 2 * width, 0)
-        if high != width:
-            source = jnp.where((channel >= width) & (channel < high), -1, source)
-    order = jnp.where(iota(shape, 1) == source, 1.0, 0.0).astype(BF16)
-    turned_ref[...] = dot_nt(order, gp_ref[...]).astype(BF16)
-    add_terms(turned_ref[: 2 * rows], edge, wide, terms)
+    turned_ref[...] = dot_nt(order_ref[...], gp_ref[...]).astype(BF16)
+    add_terms(turned_ref[: 2 * send_ref.shape[0]], edge, wide, terms)
     send_ref[...] = terms[...].astype(BF16)
 
 
@@ -182,8 +189,13 @@
     add_terms(turned_ref[2 * keep_ref.shape[0] :], edge, wide, keep_ref)
 
 
-def input_kernel(gp_ref, below_ref, band, out_ref, done_ref):
+def input_kernel(gp_ref, below_ref, w_ref, out_ref, done_ref, band):
     done_ref[...] = jnp.zeros_like(done_ref)
+    for tap in range(TAPS):
+        w = w_ref[tap]
+        even = jnp.concatenate([blank(32, COUT), w, blank(192, COUT)], axis=0)
+        odd = jnp.concatenate([blank(224, COUT), w], axis=0)
+        band[tap * SPAN : (tap + 1) * SPAN] = jnp.concatenate([even, odd], axis=1)
     per_out = below_ref.shape[0]
     cells = per_out // 16
     here = gp_ref[...]
@@ -268,6 +280,17 @@
     refs[-1][...] = total.astype(BF16)
 
 
+def store_kernel(total_ref, *refs):
+    del total_ref
+    count = (len(refs) - 1) // 2
+    sems = refs[-1]
+    copies = [pltpu.make_async_copy(refs[n], refs[count + n], sems.at[n]) for n in range(count)]
+    for copy in copies:
+        copy.start()
+    for copy in copies:
+        copy.wait()
+
+
 def tree(parts):
     while len(parts) > 1:
         parts = [parts[n] + parts[n + 1] for n in range(0, len(parts), 2)]
@@ -323,45 +346,46 @@
     x = slabs.reshape(planes, rows, lanes)
     cot = cotangent.reshape(outs, rows // 2, lanes)
     w = weight.reshape(TAPS, 3 * CIN, COUT)
-    x, cot, w = (pltpu.with_memory_space_constraint(array, pltpu.HBM) for array in (x, cot, w))
     vmem = pl.BlockSpec(memory_space=pltpu.VMEM)
     hbm = pl.BlockSpec(memory_space=pltpu.HBM)
     params = pltpu.CompilerParams(vmem_limit_bytes=VMEM_LIMIT)
     shape = jax.ShapeDtypeStruct
     flops = 2 * count * TAPS * SPAN * BLOCK
 
-    edge = pl.pallas_call(
-        edge_kernel,
-        out_shape=shape((rows, lanes), BF16),
+    edge, split, order = pl.pallas_call(
+        functools.partial(edge_kernel, width),
+        out_shape=(
+            shape((rows, lanes), BF16),
+            shape((3 * planes * 16, planes * 32), BF16),
+            shape((4 * kept_rows, 2 * COUT), BF16),
+        ),
         in_specs=[hbm],
-        out_specs=vmem,
+        out_specs=(vmem,) * 3,
         scratch_shapes=[pltpu.SemaphoreType.DMA(())],
         compiler_params=params,
+        cost_estimate=pl.CostEstimate(flops=0, bytes_accessed=10 << 20, transcendentals=0),
         name="edge_plane",
-    )(x)
+    )(pltpu.with_memory_space_constraint(x, pltpu.HBM))
     above = lax.ppermute(edge, "space", onward)
-    wide, band, preact, cot_in = pl.pallas_call(
-        functools.partial(own_kernel, planes),
+    wide, even_band, odd_band, preact, w_in = pl.pallas_call(
+        own_kernel,
         out_shape=(
             shape((count, TAPS * SPAN), BF16),
-            shape((TAPS * SPAN, BLOCK), BF16),
+            shape((TAPS * BLOCK, COUT), BF16),
+            shape((TAPS * BLOCK, COUT), BF16),
             shape((count, BLOCK), F32),
-            shape(cot.shape, BF16),
-        ),
-        in_specs=[hbm] * 3,
-        out_specs=(vmem,) * 4,
-        scratch_shapes=[
-            pltpu.VMEM(x.shape, BF16),
-            pltpu.VMEM(w.shape, BF16),
-            pltpu.SemaphoreType.DMA((3,)),
-        ],
+            shape(w.shape, BF16),
+        ),
+        in_specs=[vmem, vmem, hbm],
+        out_specs=(vmem,) * 5,
+        scratch_shapes=[pltpu.SemaphoreType.DMA(())],
         compiler_params=params,
         cost_estimate=pl.CostEstimate(flops=flops, bytes_accessed=12 << 20, transcendentals=0),
         name="own_planes",
-    )(x, w, cot)
+    )(x, split, pltpu.with_memory_space_constraint(w, pltpu.HBM))
 
     act, grad, first, turned, halo, send = pl.pallas_call(
-        functools.partial(halo_kernel, width),
+        halo_kernel,
         out_shape=(
             shape(cot.shape, BF16),
             shape((count, BLOCK), BF16),
@@ -370,7 +394,7 @@
             shape((per_out, 3 * SPAN), BF16),
             shape(terms, BF16),
         ),
-        in_specs=[vmem] * 5,
+        in_specs=[vmem] * 7,
         out_specs=(vmem,) * 6,
         scratch_shapes=[pltpu.VMEM(terms, F32)],
         compiler_params=params,
@@ -378,7 +402,7 @@
             flops=flops // 2, bytes_accessed=8 << 20, transcendentals=count * BLOCK
         ),
         name="halo_and_sent_half",
-    )(above, wide, band, preact, cot_in)
+    )(above, order, wide, even_band, odd_band, preact, cot)
     got = lax.ppermute(send, "space", in_chip)
     below = lax.ppermute(first, "space", back)
     keep = pl.pallas_call(
@@ -423,10 +447,11 @@
         out_shape=(shape(x.shape, BF16), shape((8, 128), F32)),
         in_specs=[vmem] * 3,
         out_specs=(vmem, vmem),
+        scratch_shapes=[pltpu.VMEM((TAPS * SPAN, BLOCK), BF16)],
         compiler_params=params,
         cost_estimate=pl.CostEstimate(flops=flops, bytes_accessed=8 << 20, transcendentals=0),
         name="input_grad",
-    )(grad, below, band)
+    )(grad, below, w_in)
 
     total = pl.pallas_call(
         depth_kernel,
@@ -436,6 +461,15 @@
         compiler_params=params,
         name="depth_sum",
     )(done, own, *came)
+    act, grad_in = pl.pallas_call(
+        store_kernel,
+        out_shape=(shape(cot.shape, BF16), shape(x.shape, BF16)),
+        in_specs=[vmem] * 3,
+        out_specs=(hbm, hbm),
+        scratch_shapes=[pltpu.SemaphoreType.DMA((2,))],
+        compiler_params=params,
+        name="store",
+    )(total, act, grad_in)
     others = [lax.ppermute(total, "sample", flipped(sample, j)) for j in range(1, sample)]
     kernel_grad = pl.pallas_call(
         functools.partial(sample_kernel, 1.0 / (samples * sample)),

time: 39 us -> 37.6 us (0.964)
  Pallas kernels: 15.8 us -> 13.8 us
  waiting for transfers between devices: 8.53 us -> 9.78 us
  starting transfers between devices: 13.9 us -> 13.1 us
    ppermute x1, waiting for transfers between devices: 2.08 us -> 3.68 us  [per_device(): above = lax.ppermute(edge, 'space', onward)]
    ppermute x3, waiting for transfers between devices: 3.74 us -> 2.45 us  [per_device(): lax.ppermute(total, 'sample', flipped(sample, j))]
    pallas_call x1, Pallas kernels: 4.35 us -> 3.32 us  [per_device(): pl.pallas_call(input_kernel, out_shape=(shape(x.shape, BF16), shape((8, 1...]
    pallas_call x3 -> x4, Pallas kernels: 9.12 us -> 8.11 us  [the longest x1 3.69 us: per_device(): pl.pallas_call(own_kernel, out_shape=(shape((count, TAPS * SPAN), BF16),...]
    ppermute x1, starting transfers between devices: 0.62 us -> 0.07 us  [per_device(): got = lax.ppermute(send, 'space', in_chip)]
    ppermute x1, starting transfers between devices: 1.42 us -> 0.98 us  [per_device(): below = lax.ppermute(first, 'space', back)]
    ppermute x1, waiting for transfers between devices: 2.18 us -> 2.61 us  [per_device(): low = lax.ppermute(low, 'sample', flipped(sample, 1))]
  transfers between devices with their start and end apart: 11 -> 11, of which waited for: 7 -> 7; matrix products, arithmetic and copies ran while one was open for 0% -> 0% of each run, Pallas kernels for 28% -> 26%
where the time goes in v3:
time: 37.6 us; the launch traced here: 37.4 us
  Pallas kernels  13.8 us (37%)
  starting transfers between devices  13.1 us (35%)
  waiting for transfers between devices  9.78 us (26%)
  between operations  0.72 us (2%)
    ppermute x3, starting transfers between devices, per_device(): lax.ppermute(leaving[k - 1], 'space', flipped(space, 2 * k))  4.45 us
    pallas_call x1, Pallas kernels, per_device(): pl.pallas_call(own_kernel, out_shape=(shape((count, TAPS * SPAN), BF16),...  3.69 us
    ppermute x1, waiting for transfers between devices, per_device(): above = lax.ppermute(edge, 'space', onward)  3.68 us
    ppermute x3, starting transfers between devices, per_device(): lax.ppermute(total, 'sample', flipped(sample, j))  3.55 us
    pallas_call x1, Pallas kernels, per_device(): pl.pallas_call(input_kernel, out_shape=(shape(x.shape, BF16), shape((8, 1...  3.32 us
    ppermute x1, waiting for transfers between devices, per_device(): low = lax.ppermute(low, 'sample', flipped(sample, 1))  2.61 us
    ppermute x3, waiting for transfers between devices, per_device(): lax.ppermute(total, 'sample', flipped(sample, j))  2.45 us
    ppermute x1, starting transfers between devices, per_device(): lax.ppermute(high_lanes, 'sample', flipped(sample, sample // 2))  2.09 us
  transfers between devices with their start and end apart: 11, of which 7 were waited for; matrix products, arithmetic and copies ran while one was open for 0% of the time, Pallas kernels for 26%

profile of v3, /device:TPU:0, one launch (start us, length us, event | category | flops | bytes accessed | tf_op | source)
XLA Modules:
  0.0 37.4 jit_solution(5045968454261582997)
XLA Ops:
  0.6 0.0 copy-start
  0.6 1.1 %edge_plane.1 = (bf16[32,3072]{1,0:T(8,128)(2,1)S(1)}, bf16[384,256]{1,0:T(8,128)(2,1)S(1)}, bf16[384,384]{1,0:T(8,128)(2,1)S(1)}) custom-call(bf16[8,32,3072]{2,1,0:T(8,128)(2,1)} %bitcast.8), custom_call_target="tpu_custom_call" | custom-call | bytes 10485760 | tf_op jit(solution)/shard_map/edge_plane/pallas_call | solution.py:355
  1.7 0.5 %collective-permute-start = (bf16[32,3072]{1,0:T(8,128)(2,1)S(1)}, bf16[32,3072]{1,0:T(8,128)(2,1)S(1)}, u32[]{:S(2)}, u32[]{:S(2)}) collective-permute-start(bf16[32,3072]{1,0:T(8,128)(2,1)S(1)} %get-tuple-element.28), channel_id=1, source_target_pairs={{0,1},{1,2},{2,3},{3,4},{4,5},{5,6},{6,7},{7,0},{8,9},{9,10},{10,1... | collective-permute-start | bytes 589832 | tf_op jit(solution)/shard_map/ppermute | solution.py:369
  2.2 3.7 %own_planes.1 = (bf16[512,4608]{1,0:T(8,128)(2,1)S(1)}, bf16[3456,192]{1,0:T(8,128)(2,1)S(1)}, bf16[3456,192]{1,0:T(8,128)(2,1)S(1)}, f32[512,384]{1,0:T(8,128)S(1)}, bf16[9,288,192]{2,1,0:T(8,128)(2,1)S(1)}) custom-call(bf16[8,32,3072]{2,1,0:T(8,128)(2,1)S(1)} %bitcast.9, bf16[384,256]{1,0:T(8,128)(2,1)S(1)} %get-tuple-element.30.split_ref, ...), custom_call_target="tpu_custom_call" | custom-call | flops 1811939328 | bytes 12582912 | tf_op jit(solution)/shard_map/own_planes/pallas_call | solution.py:370
  5.9 3.7 %collective-permute-done.above_ref = bf16[32,3072]{1,0:T(8,128)(2,1)S(1)} collective-permute-done((bf16[32,3072]{1,0:T(8,128)(2,1)S(1)}, bf16[32,3072]{1,0:T(8,128)(2,1)S(1)}, u32[]{:S(2)}, u32[]{:S(2)}) %collective-permute-start) | collective-permute-done | bytes 196640 | tf_op jit(solution)/shard_map/ppermute | solution.py:369
  9.6 2.1 %halo_and_sent_half.1 = (bf16[4,16,3072]{2,1,0:T(8,128)(2,1)S(1)}, bf16[512,384]{1,0:T(8,128)(2,1)S(1)}, bf16[128,384]{1,0:T(8,128)(2,1)S(1)}, bf16[384,512]{1,0...) custom-call(bf16[32,3072]{1,0:T(8,128)(2,1)S(1)} %collective-permute-done.above_ref, ...), custom_call_target="tpu_custom_call" | custom-call | flops 905969664 | bytes 8388608 | tf_op jit(solution)/shard_map/halo_and_sent_half/pallas_call | solution.py:387
  11.7 0.1 collective-permute-start.2
  11.8 1.2 %kept_half.1.keep_ref = f32[96,2816]{1,0:T(8,128)S(1)} custom-call(bf16[384,512]{1,0:T(8,128)(2,1)S(1)} %get-tuple-element.39.turned_ref, bf16[128,1536]{1,0:T(8,128)(2,1)S(1)} %get-tuple-element.40.edge, bf16[512,4608]{1,0:T(8,128)(2,1)S(1)} %get-tuple-element.31.wide), custom_call_target="tpu_custom_call" | custom-call | flops 905969664 | bytes 8388608 | tf_op jit(solution)/shard_map/kept_half/pallas_call | solution.py:408
  13.0 0.7 %collective-permute-done.2.got_ref = bf16[96,2816]{1,0:T(8,128)(2,1)S(1)} collective-permute-done((bf16[96,2816]{1,0:T(8,128)(2,1)S(1)}, bf16[96,2816]{1,0:T(8,128)(2,1)S(1)}, u32[]{:S(2)}, u32[]{:S(2)}) %collective-permute-start.2) | collective-permute-done | bytes 540704 | tf_op jit(solution)/shard_map/ppermute | solution.py:406
  13.7 0.1 pair_sum.1
  13.8 2.1 %collective-permute-start.4 = (bf16[96,768]{1,0:T(8,128)(2,1)S(1)}, bf16[96,768]{1,0:T(8,128)(2,1)S(1)}, u32[]{:S(2)}, u32[]{:S(2)}) collective-permute-start(bf16[96,768]{1,0:T(8,128)(2,1)S(1)} %get-tuple-element.44), channel_id=1, source_target_pairs={{0,16},{8,24},{16,0},{24,8},{1,17},{9,25},{17,1},{25,9},{2,18},{10... | collective-permute-start | bytes 442376 | tf_op jit(solution)/shard_map/ppermute | solution.py:431
  15.9 1.5 %collective-permute-start.3 = (bf16[96,640]{1,0:T(8,128)(2,1)S(1)}, bf16[96,640]{1,0:T(8,128)(2,1)S(1)}, u32[]{:S(2)}, u32[]{:S(2)}) collective-permute-start(bf16[96,640]{1,0:T(8,128)(2,1)S(1)} %get-tuple-element.43), channel_id=1, source_target_pairs={{0,8},{8,0},{16,24},{24,16},{1,9},{9,1},{17,25},{25,17},{2,10},{10... | collective-permute-start | bytes 368648 | tf_op jit(solution)/shard_map/ppermute | solution.py:430
  17.4 1.0 %collective-permute-start.1 = (bf16[128,384]{1,0:T(8,128)(2,1)S(1)}, bf16[128,384]{1,0:T(8,128)(2,1)S(1)}, u32[]{:S(2)}, u32[]{:S(2)}) collective-permute-start(bf16[128,384]{1,0:T(8,128)(2,1)S(1)} %get-tuple-element.36), channel_id=1, source_target_pairs={{1,0},{2,1},{3,2},{4,3},{5,4},{6,5},{7,6},{0,7},{9,8},{10,9},{11,1... | collective-permute-start | bytes 294920 | tf_op jit(solution)/shard_map/ppermute | solution.py:407
  18.4 2.6 %collective-permute-done.3.low_ref = bf16[96,640]{1,0:T(8,128)(2,1)S(1)} collective-permute-done((bf16[96,640]{1,0:T(8,128)(2,1)S(1)}, bf16[96,640]{1,0:T(8,128)(2,1)S(1)}, u32[]{:S(2)}, u32[]{:S(2)}) %collective-permute-start.3) | collective-permute-done | bytes 122912 | tf_op jit(solution)/shard_map/ppermute | solution.py:430
  21.0 0.0 collective-permute-done.4.high_ref
  21.0 0.1 cross_sum.1
  21.0 1.9 %collective-permute-start.5 = (bf16[24,1408]{1,0:T(8,128)(2,1)S(1)}, bf16[24,1408]{1,0:T(8,128)(2,1)S(1)}, u32[]{:S(2)}, u32[]{:S(2)}) collective-permute-start(bf16[24,1408]{1,0:T(8,128)(2,1)S(1)} %get-tuple-element.46), channel_id=1, source_target_pairs={{0,6},{1,7},{2,4},{3,5},{4,2},{5,3},{6,0},{7,1},{8,14},{9,15},{10,... | collective-permute-start | bytes 202760 | tf_op jit(solution)/shard_map/ppermute | solution.py:441
  22.9 0.0 collective-permute-start.6
  22.9 2.6 %collective-permute-start.7 = (bf16[24,1408]{1,0:T(8,128)(2,1)S(1)}, bf16[24,1408]{1,0:T(8,128)(2,1)S(1)}, u32[]{:S(2)}, u32[]{:S(2)}) collective-permute-start(bf16[24,1408]{1,0:T(8,128)(2,1)S(1)} %get-tuple-element.48), channel_id=1, source_target_pairs={{0,2},{1,3},{2,0},{3,1},{4,6},{5,7},{6,4},{7,5},{8,10},{9,11},{10,... | collective-permute-start | bytes 202760 | tf_op jit(solution)/shard_map/ppermute | solution.py:441
  25.5 0.0 collective-permute-done.1.below_ref
  25.5 3.3 %input_grad.1 = (bf16[8,32,3072]{2,1,0:T(8,128)(2,1)S(1)}, f32[8,128]{1,0:T(8,128)S(1)}) custom-call(bf16[512,384]{1,0:T(8,128)(2,1)S(1)} %get-tuple-element.35.gp_ref, bf16[128,384]{1,0:T(8,128)(2,1)S(1)} %collective-permute-done.1.below_ref, bf16[9,288,192]{2,1,0:T(8,128)(2,1)S(1)} %get-tuple-element.37.w_ref), custom_call_target="tpu_custom_call" | custom-call | flops 1811939328 | bytes 8388608 | tf_op jit(solution)/shard_map/input_grad/pallas_call | solution.py:445
  28.8 0.0 collective-permute-done.5.refs_0_
  28.8 0.3 collective-permute-done.6.refs_1_
  29.1 0.0 collective-permute-done.7.refs_2_
  29.2 1.8 %collective-permute-start.10 = (bf16[24,1408]{1,0:T(8,128)(2,1)S(1)}, bf16[24,1408]{1,0:T(8,128)(2,1)S(1)}, u32[]{:S(2)}, u32[]{:S(2)}) collective-permute-start(bf16[24,1408]{1,0:T(8,128)(2,1)S(1)} %depth_sum.1.total_ref.refs_0_), channel_id=1, source_target_pairs={{0,24},{8,16},{16,8},{24,0},{1,25},{9,17},{17,9},{25,1},{2,26},{10... | collective-permute-start | bytes 202760 | tf_op jit(solution)/shard_map/ppermute | solution.py:473
  31.0 1.2 %collective-permute-start.9 = (bf16[24,1408]{1,0:T(8,128)(2,1)S(1)}, bf16[24,1408]{1,0:T(8,128)(2,1)S(1)}, u32[]{:S(2)}, u32[]{:S(2)}) collective-permute-start(bf16[24,1408]{1,0:T(8,128)(2,1)S(1)} %depth_sum.1.total_ref.refs_0_), channel_id=1, source_target_pairs={{0,16},{8,24},{16,0},{24,8},{1,17},{9,25},{17,1},{25,9},{2,18},{10... | collective-permute-start | bytes 202760 | tf_op jit(solution)/shard_map/ppermute | solution.py:473
  32.2 0.5 %collective-permute-start.8 = (bf16[24,1408]{1,0:T(8,128)(2,1)S(1)}, bf16[24,1408]{1,0:T(8,128)(2,1)S(1)}, u32[]{:S(2)}, u32[]{:S(2)}) collective-permute-start(bf16[24,1408]{1,0:T(8,128)(2,1)S(1)} %depth_sum.1.total_ref.refs_0_), channel_id=1, source_target_pairs={{0,8},{8,0},{16,24},{24,16},{1,9},{9,1},{17,25},{25,17},{2,10},{10... | collective-permute-start | bytes 202760 | tf_op jit(solution)/shard_map/ppermute | solution.py:473
  32.7 1.3 %store.1 = (bf16[4,16,3072]{2,1,0:T(8,128)(2,1)}, bf16[8,32,3072]{2,1,0:T(8,128)(2,1)}) custom-call(bf16[24,1408]{1,0:T(8,128)(2,1)S(1)} %depth_sum.1.total_ref.refs_0_, bf16[4,16,3072]{2,1,0:T(8,128)(2,1)S(1)} %get-tuple-element.49.refs_0_, bf16[8,32,3072]{2,1,0:T(8,128)(2,1)S(1)} %get-tuple-element.50.refs_1_), custom_call_target="tpu_custom_call" | custom-call | tf_op jit(solution)/shard_map/store/pallas_call | solution.py:464
  34.0 0.6 %collective-permute-done.10.refs_3_ = bf16[24,1408]{1,0:T(8,128)(2,1)S(1)} collective-permute-done((bf16[24,1408]{1,0:T(8,128)(2,1)S(1)}, bf16[24,1408]{1,0:T(8,128)(2,1)S(1)}, u32[]{:S(2)}, u32[]{:S(2)}) %collective-permute-start.10) | collective-permute-done | bytes 67616 | tf_op jit(solution)/shard_map/ppermute | solution.py:473
  34.7 0.7 %collective-permute-done.9.refs_2_ = bf16[24,1408]{1,0:T(8,128)(2,1)S(1)} collective-permute-done((bf16[24,1408]{1,0:T(8,128)(2,1)S(1)}, bf16[24,1408]{1,0:T(8,128)(2,1)S(1)}, u32[]{:S(2)}, u32[]{:S(2)}) %collective-permute-start.9) | collective-permute-done | bytes 67616 | tf_op jit(solution)/shard_map/ppermute | solution.py:473
  35.4 1.1 %collective-permute-done.8.refs_1_ = bf16[24,1408]{1,0:T(8,128)(2,1)S(1)} collective-permute-done((bf16[24,1408]{1,0:T(8,128)(2,1)S(1)}, bf16[24,1408]{1,0:T(8,128)(2,1)S(1)}, u32[]{:S(2)}, u32[]{:S(2)}) %collective-permute-start.8) | collective-permute-done | bytes 67616 | tf_op jit(solution)/shard_map/ppermute | solution.py:473
  36.5 0.9 %sample_sum.1 = f32[27,24,96]{2,1,0:T(8,128)} custom-call(bf16[24,1408]{1,0:T(8,128)(2,1)S(1)} %depth_sum.1.total_ref.refs_0_, bf16[24,1408]{1,0:T(8,128)(2,1)S(1)} %collective-permute-done.8.refs_1_, bf16[24,1408]{1,0:T(8,128)(2,1)S(1)} %collective-permute-done.9.refs_2_, bf16[24,1408]{1,0:T(8,128)(2,1)S(1)} %collective-permute-done.10.refs_3_), custom_call_target="tpu_custom_call" | custom-call | tf_op jit(solution)/shard_map/sample_sum/pallas_call | solution.py:474
  (4 shorter events, 0.0 us)
Async XLA Ops:
  0.6 1.6 %copy-start = (bf16[1,8,32,3072]{3,2,1,0:T(8,128)(2,1)S(1)}, bf16[1,8,32,3072]{3,2,1,0:T(8,128)(2,1)}, u32[]{:S(2)}) copy-start(bf16[1,8,32,3072]{3,2,1,0:T(8,128)(2,1)} %param.3) | copy-start | bytes 4718596
  1.7 7.9 %collective-permute-start = (bf16[32,3072]{1,0:T(8,128)(2,1)S(1)}, bf16[32,3072]{1,0:T(8,128)(2,1)S(1)}, u32[]{:S(2)}, u32[]{:S(2)}) collective-permute-start(bf16[32,3072]{1,0:T(8,128)(2,1)S(1)} %get-tuple-element.28), channel_id=1, source_target_pairs={{0,1},{1,2},{2,3},{3,4},{4,5},{5,6},{6,7},{7,0},{8,9},{9,10},{10,1... | collective-permute-start | bytes 589832 | tf_op jit(solution)/shard_map/ppermute | solution.py:369
  2.2 7.4 %copy-start.1 = (bf16[1,4,16,3072]{3,2,1,0:T(8,128)(2,1)S(1)}, bf16[1,4,16,3072]{3,2,1,0:T(8,128)(2,1)}, u32[]{:S(2)}) copy-start(bf16[1,4,16,3072]{3,2,1,0:T(8,128)(2,1)} %param.5) | copy-start | bytes 1179652
  11.7 2.0 %collective-permute-start.2 = (bf16[96,2816]{1,0:T(8,128)(2,1)S(1)}, bf16[96,2816]{1,0:T(8,128)(2,1)S(1)}, u32[]{:S(2)}, u32[]{:S(2)}) collective-permute-start(bf16[96,2816]{1,0:T(8,128)(2,1)S(1)} %get-tuple-element.41), channel_id=1, source_target_pairs={{0,1},{1,0},{2,3},{3,2},{4,5},{5,4},{6,7},{7,6},{8,9},{9,8},{10,11... | collective-permute-start | bytes 1622024 | tf_op jit(solution)/shard_map/ppermute | solution.py:406
  13.8 7.2 %collective-permute-start.4 = (bf16[96,768]{1,0:T(8,128)(2,1)S(1)}, bf16[96,768]{1,0:T(8,128)(2,1)S(1)}, u32[]{:S(2)}, u32[]{:S(2)}) collective-permute-start(bf16[96,768]{1,0:T(8,128)(2,1)S(1)} %get-tuple-element.44), channel_id=1, source_target_pairs={{0,16},{8,24},{16,0},{24,8},{1,17},{9,25},{17,1},{25,9},{2,18},{10... | collective-permute-start | bytes 442376 | tf_op jit(solution)/shard_map/ppermute | solution.py:431
  15.9 5.1 %collective-permute-start.3 = (bf16[96,640]{1,0:T(8,128)(2,1)S(1)}, bf16[96,640]{1,0:T(8,128)(2,1)S(1)}, u32[]{:S(2)}, u32[]{:S(2)}) collective-permute-start(bf16[96,640]{1,0:T(8,128)(2,1)S(1)} %get-tuple-element.43), channel_id=1, source_target_pairs={{0,8},{8,0},{16,24},{24,16},{1,9},{9,1},{17,25},{25,17},{2,10},{10... | collective-permute-start | bytes 368648 | tf_op jit(solution)/shard_map/ppermute | solution.py:430
  17.4 8.1 %collective-permute-start.1 = (bf16[128,384]{1,0:T(8,128)(2,1)S(1)}, bf16[128,384]{1,0:T(8,128)(2,1)S(1)}, u32[]{:S(2)}, u32[]{:S(2)}) collective-permute-start(bf16[128,384]{1,0:T(8,128)(2,1)S(1)} %get-tuple-element.36), channel_id=1, source_target_pairs={{1,0},{2,1},{3,2},{4,3},{5,4},{6,5},{7,6},{0,7},{9,8},{10,9},{11,1... | collective-permute-start | bytes 294920 | tf_op jit(solution)/shard_map/ppermute | solution.py:407
  21.0 7.8 %collective-permute-start.5 = (bf16[24,1408]{1,0:T(8,128)(2,1)S(1)}, bf16[24,1408]{1,0:T(8,128)(2,1)S(1)}, u32[]{:S(2)}, u32[]{:S(2)}) collective-permute-start(bf16[24,1408]{1,0:T(8,128)(2,1)S(1)} %get-tuple-element.46), channel_id=1, source_target_pairs={{0,6},{1,7},{2,4},{3,5},{4,2},{5,3},{6,0},{7,1},{8,14},{9,15},{10,... | collective-permute-start | bytes 202760 | tf_op jit(solution)/shard_map/ppermute | solution.py:441
  22.9 6.2 %collective-permute-start.6 = (bf16[24,1408]{1,0:T(8,128)(2,1)S(1)}, bf16[24,1408]{1,0:T(8,128)(2,1)S(1)}, u32[]{:S(2)}, u32[]{:S(2)}) collective-permute-start(bf16[24,1408]{1,0:T(8,128)(2,1)S(1)} %get-tuple-element.47), channel_id=1, source_target_pairs={{0,4},{1,5},{2,6},{3,7},{4,0},{5,1},{6,2},{7,3},{8,12},{9,13},{10,... | collective-permute-start | bytes 202760 | tf_op jit(solution)/shard_map/ppermute | solution.py:441
  22.9 6.2 %collective-permute-start.7 = (bf16[24,1408]{1,0:T(8,128)(2,1)S(1)}, bf16[24,1408]{1,0:T(8,128)(2,1)S(1)}, u32[]{:S(2)}, u32[]{:S(2)}) collective-permute-start(bf16[24,1408]{1,0:T(8,128)(2,1)S(1)} %get-tuple-element.48), channel_id=1, source_target_pairs={{0,2},{1,3},{2,0},{3,1},{4,6},{5,7},{6,4},{7,5},{8,10},{9,11},{10,... | collective-permute-start | bytes 202760 | tf_op jit(solution)/shard_map/ppermute | solution.py:441
  29.2 5.5 %collective-permute-start.10 = (bf16[24,1408]{1,0:T(8,128)(2,1)S(1)}, bf16[24,1408]{1,0:T(8,128)(2,1)S(1)}, u32[]{:S(2)}, u32[]{:S(2)}) collective-permute-start(bf16[24,1408]{1,0:T(8,128)(2,1)S(1)} %depth_sum.1.total_ref.refs_0_), channel_id=1, source_target_pairs={{0,24},{8,16},{16,8},{24,0},{1,25},{9,17},{17,9},{25,1},{2,26},{10... | collective-permute-start | bytes 202760 | tf_op jit(solution)/shard_map/ppermute | solution.py:473
  31.0 4.4 %collective-permute-start.9 = (bf16[24,1408]{1,0:T(8,128)(2,1)S(1)}, bf16[24,1408]{1,0:T(8,128)(2,1)S(1)}, u32[]{:S(2)}, u32[]{:S(2)}) collective-permute-start(bf16[24,1408]{1,0:T(8,128)(2,1)S(1)} %depth_sum.1.total_ref.refs_0_), channel_id=1, source_target_pairs={{0,16},{8,24},{16,0},{24,8},{1,17},{9,25},{17,1},{25,9},{2,18},{10... | collective-permute-start | bytes 202760 | tf_op jit(solution)/shard_map/ppermute | solution.py:473
  32.2 4.3 %collective-permute-start.8 = (bf16[24,1408]{1,0:T(8,128)(2,1)S(1)}, bf16[24,1408]{1,0:T(8,128)(2,1)S(1)}, u32[]{:S(2)}, u32[]{:S(2)}) collective-permute-start(bf16[24,1408]{1,0:T(8,128)(2,1)S(1)} %depth_sum.1.total_ref.refs_0_), channel_id=1, source_target_pairs={{0,8},{8,0},{16,24},{24,16},{1,9},{9,1},{17,25},{25,17},{2,10},{10... | collective-permute-start | bytes 202760 | tf_op jit(solution)/shard_map/ppermute | solution.py:473

commit v4 on v3

--- a/solution.py
+++ b/solution.py
@@ -91,13 +91,25 @@
     return sides
 
 
-def own_kernel(x_ref, split_ref, w_hbm, wide, even_band, odd_band, preact, w_ref, sem):
+def activate(value, cot):
+    sig = jax.nn.sigmoid(value)
+    grad = cot.astype(F32) * (sig * (1.0 + value * (1.0 - sig)))
+    return (value * sig).astype(BF16), grad.astype(BF16)
+
+
+def own_kernel(
+    x_ref, split_ref, order_ref, w_hbm, cot_hbm,
+    wide, even_band, odd_band, pre_ref, act_ref, gp_ref, turned_ref, cot_ref, w_ref,
+    preact, sems,
+):
     planes = x_ref.shape[0]
     outs = planes // 2
     cells = x_ref.shape[2] // BLOCK
     per_out = cells * 16
-    copy = pltpu.make_async_copy(w_hbm, w_ref, sem)
-    copy.start()
+    w_copy = pltpu.make_async_copy(w_hbm, w_ref, sems.at[0])
+    cot_copy = pltpu.make_async_copy(cot_hbm, cot_ref, sems.at[1])
+    w_copy.start()
+    cot_copy.start()
     split = split_ref[...]
     wide[0:per_out, 0 : 3 * SPAN] = jnp.zeros((per_out, 3 * SPAN), BF16)
     x = x_ref[...].reshape(planes * 32, x_ref.shape[2])
@@ -112,7 +124,7 @@
                     put(wide, per_out, cells, p // 2, m, 6 + b, piece)
                     if p // 2 + 1 < outs:
                         put(wide, per_out, cells, p // 2 + 1, m, b, piece)
-    copy.wait()
+    w_copy.wait()
     for tap in range(TAPS):
         at = tap * BLOCK
         even_band[at : at + 32] = blank(32, COUT)
@@ -123,6 +135,16 @@
     even, odd = by_parity(wide, even_band, odd_band, TAPS)
     preact[:, :COUT] = even
     preact[:, COUT:] = odd
+    pre_ref[...] = preact[:per_out]
+    cot_copy.wait()
+    for i in range(1, outs):
+        for m in range(cells):
+            lanes = slice(m * BLOCK, (m + 1) * BLOCK)
+            at = i * per_out + m * 16
+            act, grad = activate(preact[at : at + 16], cot_ref[i, :, lanes])
+            act_ref[i - 1, :, lanes] = act
+            gp_ref[at - per_out : at - per_out + 16] = grad
+    turned_ref[...] = dot_nt(order_ref[...], gp_ref[...]).astype(BF16)
 
 
 def add_terms(turned, edge, wide, terms):
@@ -149,10 +171,9 @@
 
 
 def halo_kernel(
-    above_ref, order_ref, wide, even_band, odd_band, pre_ref, cot_ref,
-    act_ref, gp_ref, first_ref, turned_ref, edge, send_ref, terms,
+    above_ref, order_ref, wide, even_band, odd_band, pre_ref, cot_ref, rest_ref,
+    act_ref, gp_ref, turned_ref, edge, send_ref, terms,
 ):
-    outs = cot_ref.shape[0]
     cells = cot_ref.shape[2] // BLOCK
     per_out = cells * 16
     top = lax.axis_index("space") == 0
@@ -164,23 +185,13 @@
         above = dot(split_one, plane).astype(BF16)
         for b in range(3):
             put(edge, per_out, cells, 0, m, b, above[b * 16 : b * 16 + 16])
-    added = jnp.concatenate(by_parity(edge, even_band, odd_band, 3), axis=1)
-    for i in range(outs):
-        for m in range(cells):
-            lanes = slice(m * BLOCK, (m + 1) * BLOCK)
-            at = i * per_out + m * 16
-            value = pre_ref[at : at + 16]
-            if i == 0:
-                value = value + added[at : at + 16]
-            sig = jax.nn.sigmoid(value)
-            act_ref[i, :, lanes] = (value * sig).astype(BF16)
-            grad = cot_ref[i, :, lanes].astype(F32) * (sig * (1.0 + value * (1.0 - sig)))
-            grad = grad.astype(BF16)
-            gp_ref[at : at + 16] = grad
-            if i == 0:
-                first_ref[at : at + 16] = grad
-
-    turned_ref[...] = dot_nt(order_ref[...], gp_ref[...]).astype(BF16)
+    value = pre_ref[...] + jnp.concatenate(by_parity(edge, even_band, odd_band, 3), axis=1)
+    for m in range(cells):
+        lanes = slice(m * BLOCK, (m + 1) * BLOCK)
+        rows = slice(m * 16, m * 16 + 16)
+        act_ref[:, lanes], gp_ref[rows] = activate(value[rows], cot_ref[0, :, lanes])
+    turned_ref[:, :per_out] = dot_nt(order_ref[...], gp_ref[...]).astype(BF16)
+    turned_ref[:, per_out:] = rest_ref[...]
     add_terms(turned_ref[: 2 * send_ref.shape[0]], edge, wide, terms)
     send_ref[...] = terms[...].astype(BF16)
 
@@ -189,7 +200,7 @@
     add_terms(turned_ref[2 * keep_ref.shape[0] :], edge, wide, keep_ref)
 
 
-def input_kernel(gp_ref, below_ref, w_ref, out_ref, done_ref, band):
+def input_kernel(gp_ref, rest_ref, below_ref, w_ref, out_ref, done_ref, band):
     done_ref[...] = jnp.zeros_like(done_ref)
     for tap in range(TAPS):
         w = w_ref[tap]
@@ -198,12 +209,12 @@
         band[tap * SPAN : (tap + 1) * SPAN] = jnp.concatenate([even, odd], axis=1)
     per_out = below_ref.shape[0]
     cells = per_out // 16
-    here = gp_ref[...]
+    here = jnp.concatenate([gp_ref[...], rest_ref[...]], axis=0)
     following = below_ref[...]
     last = lax.axis_index("space") == lax.axis_size("space") - 1
     following = jnp.where(last, jnp.zeros_like(following), following)
     there = jnp.concatenate([here[per_out:], following], axis=0)
-    count = gp_ref.shape[0]
+    count = here.shape[0]
     outs = count // per_out
     shape = (128, 128)
     row = iota(shape, 0)
@@ -280,11 +291,18 @@
     refs[-1][...] = total.astype(BF16)
 
 
-def store_kernel(total_ref, *refs):
+def store_kernel(total_ref, first_ref, rest_ref, grad_ref, act_hbm, grad_hbm, sems):
     del total_ref
-    count = (len(refs) - 1) // 2
-    sems = refs[-1]
-    copies = [pltpu.make_async_copy(refs[n], refs[count + n], sems.at[n]) for n in range(count)]
+    copies = [
+        pltpu.make_async_copy(source, target, sems.at[n])
+        for n, (source, target) in enumerate(
+            (
+                (grad_ref, grad_hbm),
+                (rest_ref, act_hbm.at[pl.ds(1, rest_ref.shape[0])]),
+                (first_ref, act_hbm.at[0]),
+            )
+        )
+    ]
     for copy in copies:
         copy.start()
     for copy in copies:
@@ -367,42 +385,53 @@
         name="edge_plane",
     )(pltpu.with_memory_space_constraint(x, pltpu.HBM))
     above = lax.ppermute(edge, "space", onward)
-    wide, even_band, odd_band, preact, w_in = pl.pallas_call(
+    wide, even_band, odd_band, preact, act, grad, rest, cot_in, w_in = pl.pallas_call(
         own_kernel,
         out_shape=(
             shape((count, TAPS * SPAN), BF16),
             shape((TAPS * BLOCK, COUT), BF16),
             shape((TAPS * BLOCK, COUT), BF16),
-            shape((count, BLOCK), F32),
+            shape((per_out, BLOCK), F32),
+            shape((outs - 1,) + cot.shape[1:], BF16),
+            shape((count - per_out, BLOCK), BF16),
+            shape((4 * kept_rows, count - per_out), BF16),
+            shape(cot.shape, BF16),
             shape(w.shape, BF16),
         ),
-        in_specs=[vmem, vmem, hbm],
-        out_specs=(vmem,) * 5,
-        scratch_shapes=[pltpu.SemaphoreType.DMA(())],
-        compiler_params=params,
-        cost_estimate=pl.CostEstimate(flops=flops, bytes_accessed=12 << 20, transcendentals=0),
+        in_specs=[vmem] * 3 + [hbm] * 2,
+        out_specs=(vmem,) * 9,
+        scratch_shapes=[pltpu.VMEM((count, BLOCK), F32), pltpu.SemaphoreType.DMA((2,))],
+        compiler_params=params,
+        cost_estimate=pl.CostEstimate(
+            flops=flops, bytes_accessed=12 << 20, transcendentals=count * BLOCK
+        ),
         name="own_planes",
-    )(x, split, pltpu.with_memory_space_constraint(w, pltpu.HBM))
-
-    act, grad, first, turned, halo, send = pl.pallas_call(
+    )(
+        x,
+        split,
+        order,
+        pltpu.with_memory_space_constraint(w, pltpu.HBM),
+        pltpu.with_memory_space_constraint(cot, pltpu.HBM),
+    )
+
+    act_first, first, turned, halo, send = pl.pallas_call(
         halo_kernel,
         out_shape=(
-            shape(cot.shape, BF16),
-            shape((count, BLOCK), BF16),
+            shape(cot.shape[1:], BF16),
             shape((per_out, BLOCK), BF16),
             shape((4 * kept_rows, count), BF16),
             shape((per_out, 3 * SPAN), BF16),
             shape(terms, BF16),
         ),
-        in_specs=[vmem] * 7,
-        out_specs=(vmem,) * 6,
+        in_specs=[vmem] * 8,
+        out_specs=(vmem,) * 5,
         scratch_shapes=[pltpu.VMEM(terms, F32)],
         compiler_params=params,
         cost_estimate=pl.CostEstimate(
-            flops=flops // 2, bytes_accessed=8 << 20, transcendentals=count * BLOCK
+            flops=flops // 2, bytes_accessed=8 << 20, transcendentals=per_out * BLOCK
         ),
         name="halo_and_sent_half",
-    )(above, order, wide, even_band, odd_band, preact, cot)
+    )(above, order, wide, even_band, odd_band, preact, cot_in, rest)
     got = lax.ppermute(send, "space", in_chip)
     below = lax.ppermute(first, "space", back)
     keep = pl.pallas_call(
@@ -439,19 +468,19 @@
     )(mine, low, high_lanes)
     came = [
         lax.ppermute(leaving[k - 1], "space", flipped(space, 2 * k))
-        for k in reversed(range(1, depth))
+        for k in [*range(depth // 2, depth), *range(1, depth // 2)]
     ]
 
     grad_in, done = pl.pallas_call(
         input_kernel,
         out_shape=(shape(x.shape, BF16), shape((8, 128), F32)),
-        in_specs=[vmem] * 3,
+        in_specs=[vmem] * 4,
         out_specs=(vmem, vmem),
         scratch_shapes=[pltpu.VMEM((TAPS * SPAN, BLOCK), BF16)],
         compiler_params=params,
         cost_estimate=pl.CostEstimate(flops=flops, bytes_accessed=8 << 20, transcendentals=0),
         name="input_grad",
-    )(grad, below, w_in)
+    )(first, grad, below, w_in)
 
     total = pl.pallas_call(
         depth_kernel,
@@ -464,12 +493,12 @@
     act, grad_in = pl.pallas_call(
         store_kernel,
         out_shape=(shape(cot.shape, BF16), shape(x.shape, BF16)),
-        in_specs=[vmem] * 3,
+        in_specs=[vmem] * 4,
         out_specs=(hbm, hbm),
-        scratch_shapes=[pltpu.SemaphoreType.DMA((2,))],
+        scratch_shapes=[pltpu.SemaphoreType.DMA((3,))],
         compiler_params=params,
         name="store",
-    )(total, act, grad_in)
+    )(total, act_first, act, grad_in)
     others = [lax.ppermute(total, "sample", flipped(sample, j)) for j in range(1, sample)]
     kernel_grad = pl.pallas_call(
         functools.partial(sample_kernel, 1.0 / (samples * sample)),

time: 37.6 us -> 37.7 us (level)
  starting transfers between devices: 13.1 us -> 12.3 us
  waiting for transfers between devices: 9.78 us -> 10.5 us
    ppermute x3, waiting for transfers between devices: 0.31 us -> 1.45 us  [per_device(): lax.ppermute(leaving[k - 1], 'space', flipped(space, 2 * k))]
    ppermute x3, starting transfers between devices: 4.45 us -> 3.55 us  [per_device(): lax.ppermute(leaving[k - 1], 'space', flipped(space, 2 * k))]
    pallas_call x1, Pallas kernels: 3.69 us -> 4.15 us  [per_device(): pl.pallas_call(own_kernel, out_shape=(shape((count, TAPS * SPAN), BF16),...]
    ppermute x1, waiting for transfers between devices: 3.68 us -> 3.23 us  [per_device(): above = lax.ppermute(edge, 'space', onward)]
  transfers between devices with their start and end apart: 11 -> 11, of which waited for: 7 -> 9; matrix products, arithmetic and copies ran while one was open for 0% -> 0% of each run, Pallas kernels for 26% -> 27%
where the time goes in v4:
time: 37.7 us; the launch traced here: 37.5 us
  Pallas kernels  14.1 us (37%)
  starting transfers between devices  12.3 us (33%)
  waiting for transfers between devices  10.5 us (28%)
  between operations  0.71 us (2%)
    pallas_call x1, Pallas kernels, per_device(): pl.pallas_call(own_kernel, out_shape=(shape((count, TAPS * SPAN), BF16),...  4.15 us
    ppermute x3, starting transfers between devices, per_device(): lax.ppermute(leaving[k - 1], 'space', flipped(space, 2 * k))  3.55 us
    ppermute x3, starting transfers between devices, per_device(): lax.ppermute(total, 'sample', flipped(sample, j))  3.55 us
    pallas_call x1, Pallas kernels, per_device(): pl.pallas_call(input_kernel, out_shape=(shape(x.shape, BF16), shape((8, 1...  3.32 us
    ppermute x1, waiting for transfers between devices, per_device(): above = lax.ppermute(edge, 'space', onward)  3.23 us
    ppermute x1, waiting for transfers between devices, per_device(): low = lax.ppermute(low, 'sample', flipped(sample, 1))  2.61 us
    ppermute x3, waiting for transfers between devices, per_device(): lax.ppermute(total, 'sample', flipped(sample, j))  2.46 us
    ppermute x1, starting transfers between devices, per_device(): lax.ppermute(high_lanes, 'sample', flipped(sample, sample // 2))  2.1 us
  transfers between devices with their start and end apart: 11, of which 9 were waited for; matrix products, arithmetic and copies ran while one was open for 0% of the time, Pallas kernels for 27%

profile of v4, /device:TPU:0, one launch (start us, length us, event | category | flops | bytes accessed | tf_op | source)
XLA Modules:
  0.0 37.5 jit_solution(3663208884019785020)
XLA Ops:
  0.6 0.0 copy-start
  0.6 1.1 %edge_plane.1 = (bf16[32,3072]{1,0:T(8,128)(2,1)S(1)}, bf16[384,256]{1,0:T(8,128)(2,1)S(1)}, bf16[384,384]{1,0:T(8,128)(2,1)S(1)}) custom-call(bf16[8,32,3072]{2,1,0:T(8,128)(2,1)} %bitcast.8), custom_call_target="tpu_custom_call" | custom-call | bytes 10485760 | tf_op jit(solution)/shard_map/edge_plane/pallas_call | solution.py:373
  1.7 0.5 %collective-permute-start = (bf16[32,3072]{1,0:T(8,128)(2,1)S(1)}, bf16[32,3072]{1,0:T(8,128)(2,1)S(1)}, u32[]{:S(2)}, u32[]{:S(2)}) collective-permute-start(bf16[32,3072]{1,0:T(8,128)(2,1)S(1)} %get-tuple-element.31), channel_id=1, source_target_pairs={{0,1},{1,2},{2,3},{3,4},{4,5},{5,6},{6,7},{7,0},{8,9},{9,10},{10,1... | collective-permute-start | bytes 589832 | tf_op jit(solution)/shard_map/ppermute | solution.py:387
  2.2 4.2 %own_planes.1 = (bf16[512,4608]{1,0:T(8,128)(2,1)S(1)}, bf16[3456,192]{1,0:T(8,128)(2,1)S(1)}, bf16[3456,192]{1,0:T(8,128)(2,1)S(1)}, f32[128,384]{1,0:T(8,128)S...) custom-call(bf16[8,32,3072]{2,1,0:T(8,128)(2,1)S(1)} %bitcast.9, ...), custom_call_target="tpu_custom_call" | custom-call | flops 1811939328 | bytes 12582912 | tf_op jit(solution)/shard_map/own_planes/pallas_call | solution.py:388
  6.4 3.2 %collective-permute-done.above_ref = bf16[32,3072]{1,0:T(8,128)(2,1)S(1)} collective-permute-done((bf16[32,3072]{1,0:T(8,128)(2,1)S(1)}, bf16[32,3072]{1,0:T(8,128)(2,1)S(1)}, u32[]{:S(2)}, u32[]{:S(2)}) %collective-permute-start) | collective-permute-done | bytes 196640 | tf_op jit(solution)/shard_map/ppermute | solution.py:387
  9.6 2.0 %halo_and_sent_half.1 = (bf16[16,3072]{1,0:T(8,128)(2,1)S(1)}, bf16[128,384]{1,0:T(8,128)(2,1)S(1)}, bf16[384,512]{1,0:T(8,128)(2,1)S(1)}, bf16[128,1536]{1,0:T(8,128)(2,1)S(1)}, bf16[96,2816]{1,0:T(8,128)(2,1)S(1)}) custom-call(bf16[32,3072]{1,0:T(8,128)(2,1)S(1)} %collective-permute-done.above_ref, bf16[384,384]{1,0:T(8,128)(2,1)S(1)} %get-tuple-element.32.order_ref, ...), custom_call_target="tpu_custom_call" | custom-call | flops 905969664 | bytes 8388608 | tf_op jit(solution)/shard_map/halo_and_sent_half/pallas_call | solution.py:417
  11.6 0.1 collective-permute-start.2
  11.7 1.2 %kept_half.1.keep_ref = f32[96,2816]{1,0:T(8,128)S(1)} custom-call(bf16[384,512]{1,0:T(8,128)(2,1)S(1)} %get-tuple-element.44.turned_ref, bf16[128,1536]{1,0:T(8,128)(2,1)S(1)} %get-tuple-element.45.edge, bf16[512,4608]{1,0:T(8,128)(2,1)S(1)} %get-tuple-element.34.wide), custom_call_target="tpu_custom_call" | custom-call | flops 905969664 | bytes 8388608 | tf_op jit(solution)/shard_map/kept_half/pallas_call | solution.py:437
  12.9 0.7 %collective-permute-done.2.got_ref = bf16[96,2816]{1,0:T(8,128)(2,1)S(1)} collective-permute-done((bf16[96,2816]{1,0:T(8,128)(2,1)S(1)}, bf16[96,2816]{1,0:T(8,128)(2,1)S(1)}, u32[]{:S(2)}, u32[]{:S(2)}) %collective-permute-start.2) | collective-permute-done | bytes 540704 | tf_op jit(solution)/shard_map/ppermute | solution.py:435
  13.6 0.1 pair_sum.1
  13.7 2.1 %collective-permute-start.4 = (bf16[96,768]{1,0:T(8,128)(2,1)S(1)}, bf16[96,768]{1,0:T(8,128)(2,1)S(1)}, u32[]{:S(2)}, u32[]{:S(2)}) collective-permute-start(bf16[96,768]{1,0:T(8,128)(2,1)S(1)} %get-tuple-element.49), channel_id=1, source_target_pairs={{0,16},{8,24},{16,0},{24,8},{1,17},{9,25},{17,1},{25,9},{2,18},{10... | collective-permute-start | bytes 442376 | tf_op jit(solution)/shard_map/ppermute | solution.py:460
  15.8 1.5 %collective-permute-start.3 = (bf16[96,640]{1,0:T(8,128)(2,1)S(1)}, bf16[96,640]{1,0:T(8,128)(2,1)S(1)}, u32[]{:S(2)}, u32[]{:S(2)}) collective-permute-start(bf16[96,640]{1,0:T(8,128)(2,1)S(1)} %get-tuple-element.48), channel_id=1, source_target_pairs={{0,8},{8,0},{16,24},{24,16},{1,9},{9,1},{17,25},{25,17},{2,10},{10... | collective-permute-start | bytes 368648 | tf_op jit(solution)/shard_map/ppermute | solution.py:459
  17.3 1.0 %collective-permute-start.1 = (bf16[128,384]{1,0:T(8,128)(2,1)S(1)}, bf16[128,384]{1,0:T(8,128)(2,1)S(1)}, u32[]{:S(2)}, u32[]{:S(2)}) collective-permute-start(bf16[128,384]{1,0:T(8,128)(2,1)S(1)} %get-tuple-element.40.gp_ref), channel_id=1, source_target_pairs={{1,0},{2,1},{3,2},{4,3},{5,4},{6,5},{7,6},{0,7},{9,8},{10,9},{11,1... | collective-permute-start | bytes 294920 | tf_op jit(solution)/shard_map/ppermute | solution.py:436
  18.3 2.6 %collective-permute-done.3.low_ref = bf16[96,640]{1,0:T(8,128)(2,1)S(1)} collective-permute-done((bf16[96,640]{1,0:T(8,128)(2,1)S(1)}, bf16[96,640]{1,0:T(8,128)(2,1)S(1)}, u32[]{:S(2)}, u32[]{:S(2)}) %collective-permute-start.3) | collective-permute-done | bytes 122912 | tf_op jit(solution)/shard_map/ppermute | solution.py:459
  20.9 0.0 collective-permute-done.4.high_ref
  20.9 0.1 cross_sum.1
  20.9 1.5 %collective-permute-start.5 = (bf16[24,1408]{1,0:T(8,128)(2,1)S(1)}, bf16[24,1408]{1,0:T(8,128)(2,1)S(1)}, u32[]{:S(2)}, u32[]{:S(2)}) collective-permute-start(bf16[24,1408]{1,0:T(8,128)(2,1)S(1)} %get-tuple-element.51), channel_id=1, source_target_pairs={{0,4},{1,5},{2,6},{3,7},{4,0},{5,1},{6,2},{7,3},{8,12},{9,13},{10,... | collective-permute-start | bytes 202760 | tf_op jit(solution)/shard_map/ppermute | solution.py:470
  22.4 1.3 %collective-permute-start.6 = (bf16[24,1408]{1,0:T(8,128)(2,1)S(1)}, bf16[24,1408]{1,0:T(8,128)(2,1)S(1)}, u32[]{:S(2)}, u32[]{:S(2)}) collective-permute-start(bf16[24,1408]{1,0:T(8,128)(2,1)S(1)} %get-tuple-element.52), channel_id=1, source_target_pairs={{0,6},{1,7},{2,4},{3,5},{4,2},{5,3},{6,0},{7,1},{8,14},{9,15},{10,... | collective-permute-start | bytes 202760 | tf_op jit(solution)/shard_map/ppermute | solution.py:470
  23.8 0.7 %collective-permute-start.7 = (bf16[24,1408]{1,0:T(8,128)(2,1)S(1)}, bf16[24,1408]{1,0:T(8,128)(2,1)S(1)}, u32[]{:S(2)}, u32[]{:S(2)}) collective-permute-start(bf16[24,1408]{1,0:T(8,128)(2,1)S(1)} %get-tuple-element.53), channel_id=1, source_target_pairs={{0,2},{1,3},{2,0},{3,1},{4,6},{5,7},{6,4},{7,5},{8,10},{9,11},{10,... | collective-permute-start | bytes 202760 | tf_op jit(solution)/shard_map/ppermute | solution.py:470
  24.5 0.0 collective-permute-done.1.below_ref
  24.5 3.3 %input_grad.1 = (bf16[8,32,3072]{2,1,0:T(8,128)(2,1)S(1)}, f32[8,128]{1,0:T(8,128)S(1)}) custom-call(bf16[128,384]{1,0:T(8,128)(2,1)S(1)} %get-tuple-element.40.gp_ref, bf16[384,384]{1,0:T(8,128)(2,1)S(1)} %get-tuple-element.41.rest_ref, bf16[128,384]{1,0:T(8,128)(2,1)S(1)} %collective-permute-done.1.below_ref, bf16[9,288,192]{2,1,0:T(8,128)(2,1)S(1)} %get-tuple-element.42.w_ref), custom_call_target="tpu_custom_call" | custom-call | flops 1811939328 | bytes 8388608 | tf_op jit(solution)/shard_map/input_grad/pallas_call | solution.py:474
  27.8 0.1 collective-permute-done.5.refs_0_
  27.9 0.8 %collective-permute-done.6.refs_1_ = bf16[24,1408]{1,0:T(8,128)(2,1)S(1)} collective-permute-done((bf16[24,1408]{1,0:T(8,128)(2,1)S(1)}, bf16[24,1408]{1,0:T(8,128)(2,1)S(1)}, u32[]{:S(2)}, u32[]{:S(2)}) %collective-permute-start.6) | collective-permute-done | bytes 67616 | tf_op jit(solution)/shard_map/ppermute | solution.py:470
  28.7 0.6 %collective-permute-done.7.refs_2_ = bf16[24,1408]{1,0:T(8,128)(2,1)S(1)} collective-permute-done((bf16[24,1408]{1,0:T(8,128)(2,1)S(1)}, bf16[24,1408]{1,0:T(8,128)(2,1)S(1)}, u32[]{:S(2)}, u32[]{:S(2)}) %collective-permute-start.7) | collective-permute-done | bytes 67616 | tf_op jit(solution)/shard_map/ppermute | solution.py:470
  29.3 1.8 %collective-permute-start.10 = (bf16[24,1408]{1,0:T(8,128)(2,1)S(1)}, bf16[24,1408]{1,0:T(8,128)(2,1)S(1)}, u32[]{:S(2)}, u32[]{:S(2)}) collective-permute-start(bf16[24,1408]{1,0:T(8,128)(2,1)S(1)} %depth_sum.1.total_ref.refs_0_), channel_id=1, source_target_pairs={{0,24},{8,16},{16,8},{24,0},{1,25},{9,17},{17,9},{25,1},{2,26},{10... | collective-permute-start | bytes 202760 | tf_op jit(solution)/shard_map/ppermute | solution.py:502
  31.1 1.2 %collective-permute-start.9 = (bf16[24,1408]{1,0:T(8,128)(2,1)S(1)}, bf16[24,1408]{1,0:T(8,128)(2,1)S(1)}, u32[]{:S(2)}, u32[]{:S(2)}) collective-permute-start(bf16[24,1408]{1,0:T(8,128)(2,1)S(1)} %depth_sum.1.total_ref.refs_0_), channel_id=1, source_target_pairs={{0,16},{8,24},{16,0},{24,8},{1,17},{9,25},{17,1},{25,9},{2,18},{10... | collective-permute-start | bytes 202760 | tf_op jit(solution)/shard_map/ppermute | solution.py:502
  32.3 0.5 %collective-permute-start.8 = (bf16[24,1408]{1,0:T(8,128)(2,1)S(1)}, bf16[24,1408]{1,0:T(8,128)(2,1)S(1)}, u32[]{:S(2)}, u32[]{:S(2)}) collective-permute-start(bf16[24,1408]{1,0:T(8,128)(2,1)S(1)} %depth_sum.1.total_ref.refs_0_), channel_id=1, source_target_pairs={{0,8},{8,0},{16,24},{24,16},{1,9},{9,1},{17,25},{25,17},{2,10},{10... | collective-permute-start | bytes 202760 | tf_op jit(solution)/shard_map/ppermute | solution.py:502
  32.9 1.3 %store.1 = (bf16[4,16,3072]{2,1,0:T(8,128)(2,1)}, bf16[8,32,3072]{2,1,0:T(8,128)(2,1)}) custom-call(bf16[24,1408]{1,0:T(8,128)(2,1)S(1)} %depth_sum.1.total_ref.refs_0_, bf16[16,3072]{1,0:T(8,128)(2,1)S(1)} %get-tuple-element.54.first_ref, bf16[3,16,3072]{2,1,0:T(8,128)(2,1)S(1)} %get-tuple-element.55.rest_ref, ...), custom_call_target="tpu_custom_call" | custom-call | tf_op jit(solution)/shard_map/store/pallas_call | solution.py:493
  34.2 0.4 %collective-permute-done.10.refs_3_ = bf16[24,1408]{1,0:T(8,128)(2,1)S(1)} collective-permute-done((bf16[24,1408]{1,0:T(8,128)(2,1)S(1)}, bf16[24,1408]{1,0:T(8,128)(2,1)S(1)}, u32[]{:S(2)}, u32[]{:S(2)}) %collective-permute-start.10) | collective-permute-done | bytes 67616 | tf_op jit(solution)/shard_map/ppermute | solution.py:502
  34.6 0.9 %collective-permute-done.9.refs_2_ = bf16[24,1408]{1,0:T(8,128)(2,1)S(1)} collective-permute-done((bf16[24,1408]{1,0:T(8,128)(2,1)S(1)}, bf16[24,1408]{1,0:T(8,128)(2,1)S(1)}, u32[]{:S(2)}, u32[]{:S(2)}) %collective-permute-start.9) | collective-permute-done | bytes 67616 | tf_op jit(solution)/shard_map/ppermute | solution.py:502
  35.4 1.2 %collective-permute-done.8.refs_1_ = bf16[24,1408]{1,0:T(8,128)(2,1)S(1)} collective-permute-done((bf16[24,1408]{1,0:T(8,128)(2,1)S(1)}, bf16[24,1408]{1,0:T(8,128)(2,1)S(1)}, u32[]{:S(2)}, u32[]{:S(2)}) %collective-permute-start.8) | collective-permute-done | bytes 67616 | tf_op jit(solution)/shard_map/ppermute | solution.py:502
  36.6 0.9 %sample_sum.1 = f32[27,24,96]{2,1,0:T(8,128)} custom-call(bf16[24,1408]{1,0:T(8,128)(2,1)S(1)} %depth_sum.1.total_ref.refs_0_, bf16[24,1408]{1,0:T(8,128)(2,1)S(1)} %collective-permute-done.8.refs_1_, bf16[24,1408]{1,0:T(8,128)(2,1)S(1)} %collective-permute-done.9.refs_2_, bf16[24,1408]{1,0:T(8,128)(2,1)S(1)} %collective-permute-done.10.refs_3_), custom_call_target="tpu_custom_call" | custom-call | tf_op jit(solution)/shard_map/sample_sum/pallas_call | solution.py:503
  (2 shorter events, 0.0 us)
Async XLA Ops:
  0.6 1.6 %copy-start = (bf16[1,8,32,3072]{3,2,1,0:T(8,128)(2,1)S(1)}, bf16[1,8,32,3072]{3,2,1,0:T(8,128)(2,1)}, u32[]{:S(2)}) copy-start(bf16[1,8,32,3072]{3,2,1,0:T(8,128)(2,1)} %param.3) | copy-start | bytes 4718596
  1.7 7.9 %collective-permute-start = (bf16[32,3072]{1,0:T(8,128)(2,1)S(1)}, bf16[32,3072]{1,0:T(8,128)(2,1)S(1)}, u32[]{:S(2)}, u32[]{:S(2)}) collective-permute-start(bf16[32,3072]{1,0:T(8,128)(2,1)S(1)} %get-tuple-element.31), channel_id=1, source_target_pairs={{0,1},{1,2},{2,3},{3,4},{4,5},{5,6},{6,7},{7,0},{8,9},{9,10},{10,1... | collective-permute-start | bytes 589832 | tf_op jit(solution)/shard_map/ppermute | solution.py:387
  11.6 2.0 %collective-permute-start.2 = (bf16[96,2816]{1,0:T(8,128)(2,1)S(1)}, bf16[96,2816]{1,0:T(8,128)(2,1)S(1)}, u32[]{:S(2)}, u32[]{:S(2)}) collective-permute-start(bf16[96,2816]{1,0:T(8,128)(2,1)S(1)} %get-tuple-element.46), channel_id=1, source_target_pairs={{0,1},{1,0},{2,3},{3,2},{4,5},{5,4},{6,7},{7,6},{8,9},{9,8},{10,11... | collective-permute-start | bytes 1622024 | tf_op jit(solution)/shard_map/ppermute | solution.py:435
  13.7 7.2 %collective-permute-start.4 = (bf16[96,768]{1,0:T(8,128)(2,1)S(1)}, bf16[96,768]{1,0:T(8,128)(2,1)S(1)}, u32[]{:S(2)}, u32[]{:S(2)}) collective-permute-start(bf16[96,768]{1,0:T(8,128)(2,1)S(1)} %get-tuple-element.49), channel_id=1, source_target_pairs={{0,16},{8,24},{16,0},{24,8},{1,17},{9,25},{17,1},{25,9},{2,18},{10... | collective-permute-start | bytes 442376 | tf_op jit(solution)/shard_map/ppermute | solution.py:460
  15.8 5.1 %collective-permute-start.3 = (bf16[96,640]{1,0:T(8,128)(2,1)S(1)}, bf16[96,640]{1,0:T(8,128)(2,1)S(1)}, u32[]{:S(2)}, u32[]{:S(2)}) collective-permute-start(bf16[96,640]{1,0:T(8,128)(2,1)S(1)} %get-tuple-element.48), channel_id=1, source_target_pairs={{0,8},{8,0},{16,24},{24,16},{1,9},{9,1},{17,25},{25,17},{2,10},{10... | collective-permute-start | bytes 368648 | tf_op jit(solution)/shard_map/ppermute | solution.py:459
  17.3 7.2 %collective-permute-start.1 = (bf16[128,384]{1,0:T(8,128)(2,1)S(1)}, bf16[128,384]{1,0:T(8,128)(2,1)S(1)}, u32[]{:S(2)}, u32[]{:S(2)}) collective-permute-start(bf16[128,384]{1,0:T(8,128)(2,1)S(1)} %get-tuple-element.40.gp_ref), channel_id=1, source_target_pairs={{1,0},{2,1},{3,2},{4,3},{5,4},{6,5},{7,6},{0,7},{9,8},{10,9},{11,1... | collective-permute-start | bytes 294920 | tf_op jit(solution)/shard_map/ppermute | solution.py:436
  20.9 6.9 %collective-permute-start.5 = (bf16[24,1408]{1,0:T(8,128)(2,1)S(1)}, bf16[24,1408]{1,0:T(8,128)(2,1)S(1)}, u32[]{:S(2)}, u32[]{:S(2)}) collective-permute-start(bf16[24,1408]{1,0:T(8,128)(2,1)S(1)} %get-tuple-element.51), channel_id=1, source_target_pairs={{0,4},{1,5},{2,6},{3,7},{4,0},{5,1},{6,2},{7,3},{8,12},{9,13},{10,... | collective-permute-start | bytes 202760 | tf_op jit(solution)/shard_map/ppermute | solution.py:470
  22.4 6.2 %collective-permute-start.6 = (bf16[24,1408]{1,0:T(8,128)(2,1)S(1)}, bf16[24,1408]{1,0:T(8,128)(2,1)S(1)}, u32[]{:S(2)}, u32[]{:S(2)}) collective-permute-start(bf16[24,1408]{1,0:T(8,128)(2,1)S(1)} %get-tuple-element.52), channel_id=1, source_target_pairs={{0,6},{1,7},{2,4},{3,5},{4,2},{5,3},{6,0},{7,1},{8,14},{9,15},{10,... | collective-permute-start | bytes 202760 | tf_op jit(solution)/shard_map/ppermute | solution.py:470
  23.8 5.5 %collective-permute-start.7 = (bf16[24,1408]{1,0:T(8,128)(2,1)S(1)}, bf16[24,1408]{1,0:T(8,128)(2,1)S(1)}, u32[]{:S(2)}, u32[]{:S(2)}) collective-permute-start(bf16[24,1408]{1,0:T(8,128)(2,1)S(1)} %get-tuple-element.53), channel_id=1, source_target_pairs={{0,2},{1,3},{2,0},{3,1},{4,6},{5,7},{6,4},{7,5},{8,10},{9,11},{10,... | collective-permute-start | bytes 202760 | tf_op jit(solution)/shard_map/ppermute | solution.py:470
  29.3 5.3 %collective-permute-start.10 = (bf16[24,1408]{1,0:T(8,128)(2,1)S(1)}, bf16[24,1408]{1,0:T(8,128)(2,1)S(1)}, u32[]{:S(2)}, u32[]{:S(2)}) collective-permute-start(bf16[24,1408]{1,0:T(8,128)(2,1)S(1)} %depth_sum.1.total_ref.refs_0_), channel_id=1, source_target_pairs={{0,24},{8,16},{16,8},{24,0},{1,25},{9,17},{17,9},{25,1},{2,26},{10... | collective-permute-start | bytes 202760 | tf_op jit(solution)/shard_map/ppermute | solution.py:502
  31.1 4.3 %collective-permute-start.9 = (bf16[24,1408]{1,0:T(8,128)(2,1)S(1)}, bf16[24,1408]{1,0:T(8,128)(2,1)S(1)}, u32[]{:S(2)}, u32[]{:S(2)}) collective-permute-start(bf16[24,1408]{1,0:T(8,128)(2,1)S(1)} %depth_sum.1.total_ref.refs_0_), channel_id=1, source_target_pairs={{0,16},{8,24},{16,0},{24,8},{1,17},{9,25},{17,1},{25,9},{2,18},{10... | collective-permute-start | bytes 202760 | tf_op jit(solution)/shard_map/ppermute | solution.py:502
  32.3 4.3 %collective-permute-start.8 = (bf16[24,1408]{1,0:T(8,128)(2,1)S(1)}, bf16[24,1408]{1,0:T(8,128)(2,1)S(1)}, u32[]{:S(2)}, u32[]{:S(2)}) collective-permute-start(bf16[24,1408]{1,0:T(8,128)(2,1)S(1)} %depth_sum.1.total_ref.refs_0_), channel_id=1, source_target_pairs={{0,8},{8,0},{16,24},{24,16},{1,9},{9,1},{17,25},{25,17},{2,10},{10... | collective-permute-start | bytes 202760 | tf_op jit(solution)/shard_map/ppermute | solution.py:502

commit v5 on v3

--- a/solution.py
+++ b/solution.py
@@ -12,9 +12,10 @@
 BLOCK = 384
 SPAN = 512
 TAPS = 9
-LOW = 640
-HIGH = 768
-MINE = LOW + HIGH
+SIDE = 640
+REST = 4 * SIDE
+TERMS = REST + 128
+LEFT = TAPS * 3 * CIN - REST
 F32 = jnp.float32
 BF16 = jnp.bfloat16
 VMEM_LIMIT = 12 * 1024 * 1024
@@ -252,24 +253,65 @@
     return at % 2, at // (lax.axis_size("sample") // 2)
 
 
+def listed(block):
+    rows, lanes = block.shape
+    return jnp.concatenate(
+        [block[r : r + 8, t : t + 128] for r in range(0, rows, 8) for t in range(0, lanes, 128)],
+        axis=0,
+    )
+
+
+def unlisted(tiles, rows):
+    across = tiles.shape[0] // rows
+    return jnp.concatenate(
+        [
+            jnp.concatenate(
+                [tiles[(r * across + t) * 8 : (r * across + t) * 8 + 8] for t in range(across)], axis=1
+            )
+            for r in range(rows // 8)
+        ],
+        axis=0,
+    )
+
+
 def pair_kernel(keep_ref, got_ref, mine_ref, low_ref, high_ref):
+    low, high = sample_bits()
+    steps, side = low_ref.shape[:2]
+    rows = keep_ref.shape[0] // steps
+
     def total(start, lanes):
         lanes = pl.ds(pl.multiple_of(start, 128), lanes)
         return keep_ref[:, lanes] + got_ref[:, lanes].astype(F32)
 
-    low, high = sample_bits()
-    low_ref[...] = total((1 - low) * LOW, LOW).astype(BF16)
-    high_ref[...] = total(2 * LOW + (1 - high) * HIGH, HIGH).astype(BF16)
-    mine_ref[:, :LOW] = total(low * LOW, LOW)
-    mine_ref[:, LOW:] = total(2 * LOW + high * HIGH, HIGH)
+    sent = total((1 - low) * SIDE, SIDE), total((3 - high) * SIDE, SIDE)
+    kept = total(low * SIDE, SIDE), total((2 + high) * SIDE, SIDE)
+    last = keep_ref[:, REST:] + got_ref[:, REST:].astype(F32)
+    lane = iota((8, 128), 1)
+    for k in range(steps):
+        at = slice(k * rows, (k + 1) * rows)
+        low_ref[k] = listed(sent[0][at]).astype(BF16)
+        high_ref[k] = listed(sent[1][at]).astype(BF16)
+        mine_ref[k, :side] = listed(kept[0][at])
+        mine_ref[k, side : 2 * side] = listed(kept[1][at])
+        packed = jnp.zeros((8, 128), F32)
+        for r in range(rows // 8):
+            tile = last[k * rows + r * 8 : k * rows + r * 8 + 8]
+            packed = packed + pltpu.roll(jnp.where(lane < LEFT, tile, 0.0), r * LEFT, 1)
+        mine_ref[k, 2 * side :] = packed
 
 
 def cross_kernel(mine_ref, low_ref, high_ref, *out_refs):
-    for lanes, ref in ((slice(0, LOW), low_ref), (slice(LOW, MINE), high_ref)):
-        total = mine_ref[:, lanes] + ref[...].astype(F32)
-        high = out_refs[0].shape[0]
-        for k, out_ref in enumerate(out_refs):
-            out_ref[:, lanes] = total[k * high : (k + 1) * high].astype(out_ref.dtype)
+    side = low_ref.shape[1]
+    for k, out_ref in enumerate(out_refs):
+        total = jnp.concatenate(
+            [
+                mine_ref[k, :side] + low_ref[k].astype(F32),
+                mine_ref[k, side : 2 * side] + high_ref[k].astype(F32),
+                mine_ref[k, 2 * side :],
+            ],
+            axis=0,
+        )
+        out_ref[...] = total.astype(out_ref.dtype)
 
 
 def depth_kernel(done_ref, own_ref, *refs):
@@ -300,22 +342,27 @@
 def sample_kernel(scale, *refs):
     out_ref = refs[-1]
     width = out_ref.shape[1]
-    parts = [ref[...].astype(F32)[:width] * scale for ref in refs[:-1]]
+    rows = -(-width // 8) * 8
+    side = rows * SIDE // 128
+    parts = [ref[...].astype(F32) * scale for ref in refs[:-1]]
     half = len(parts) // 2
-    here = tree([part[:, :LOW] for part in parts[0::2]])
-    there = tree([part[:, :LOW] for part in parts[1::2]])
-    above = tree([part[:, LOW:] for part in parts[:half]])
-    below = tree([part[:, LOW:] for part in parts[half:]])
+    here = tree([part[:side] for part in parts[0::2]])
+    there = tree([part[:side] for part in parts[1::2]])
+    above = tree([part[side : 2 * side] for part in parts[:half]])
+    below = tree([part[side : 2 * side] for part in parts[half:]])
+    packed = tree([part[2 * side :] for part in parts])
     low, high = (bit == 0 for bit in sample_bits())
+    quarters = (
+        jnp.where(low, here, there),
+        jnp.where(low, there, here),
+        jnp.where(high, above, below),
+        jnp.where(high, below, above),
+    )
+    last = [pltpu.roll(packed, (128 - r * LEFT) % 128, 1) for r in range(rows // 8)]
     total = jnp.concatenate(
-        [
-            jnp.where(low, here, there),
-            jnp.where(low, there, here),
-            jnp.where(high, above, below),
-            jnp.where(high, below, above),
-        ],
-        axis=1,
+        [unlisted(quarter, rows) for quarter in quarters] + [jnp.concatenate(last, axis=0)], axis=1
     )
+    total = total[:width]
     for n in range(out_ref.shape[0]):
         out_ref[n] = total[:, n * CIN : (n + 1) * CIN]
 
@@ -333,8 +380,9 @@
     width = COUT // space
     high = -(-width // 8) * 8
     kept_rows = depth * high
-    terms = (kept_rows, 2 * MINE)
-    part = (high, MINE)
+    terms = (kept_rows, TERMS)
+    side = high * SIDE // 128
+    part = (2 * side + 8, 128)
     cells = lanes // BLOCK
     per_out = cells * 16
     count = outs * per_out
@@ -418,9 +466,9 @@
     mine, low, high_lanes = pl.pallas_call(
         pair_kernel,
         out_shape=(
-            shape((kept_rows, MINE), F32),
-            shape((kept_rows, LOW), BF16),
-            shape((kept_rows, HIGH), BF16),
+            shape((depth,) + part, F32),
+            shape((depth, side, 128), BF16),
+            shape((depth, side, 128), BF16),
         ),
         in_specs=[vmem] * 2,
         out_specs=(vmem,) * 3,
@@ -439,7 +487,7 @@
     )(mine, low, high_lanes)
     came = [
         lax.ppermute(leaving[k - 1], "space", flipped(space, 2 * k))
-        for k in reversed(range(1, depth))
+        for k in [*range(depth // 2, depth), *range(1, depth // 2)]
     ]
 
     grad_in, done = pl.pallas_call(

time: 37.6 us -> 36.1 us (0.960)
  starting transfers between devices: 13.1 us -> 12.2 us
  waiting for transfers between devices: 9.78 us -> 9.19 us
    ppermute x1, waiting for transfers between devices: 2.61 us -> 1.13 us  [per_device(): low = lax.ppermute(low, 'sample', flipped(sample, 1))]
    ppermute x1, waiting for transfers between devices: 0.01 us -> 1.46 us  [per_device(): lax.ppermute(high_lanes, 'sample', flipped(sample, sample // 2))]
    ppermute x3, waiting for transfers between devices: 2.45 us -> 1.52 us  [per_device(): lax.ppermute(total, 'sample', flipped(sample, j))]
    ppermute x3, starting transfers between devices: 4.45 us -> 3.55 us  [per_device(): lax.ppermute(leaving[k - 1], 'space', flipped(space, 2 * k))]
    ppermute x1, starting transfers between devices: 2.09 us -> 1.52 us  [per_device(): lax.ppermute(high_lanes, 'sample', flipped(sample, sample // 2))]
    ppermute x1, starting transfers between devices: 1.5 us -> 2.06 us  [per_device(): low = lax.ppermute(low, 'sample', flipped(sample, 1))]
    ppermute x3, waiting for transfers between devices: 0.31 us -> 0.7 us  [per_device(): lax.ppermute(leaving[k - 1], 'space', flipped(space, 2 * k))]
  transfers between devices with their start and end apart: 11 -> 11, of which waited for: 7 -> 9; matrix products, arithmetic and copies ran while one was open for 0% -> 0% of each run, Pallas kernels for 26% -> 27%
where the time goes in v5:
time: 36.1 us; the launch traced here: 35.9 us
  Pallas kernels  13.8 us (38%)
  starting transfers between devices  12.2 us (34%)
  waiting for transfers between devices  9.19 us (25%)
  between operations  0.72 us (2%)
    pallas_call x1, Pallas kernels, per_device(): pl.pallas_call(own_kernel, out_shape=(shape((count, TAPS * SPAN), BF16),...  3.69 us
    ppermute x1, waiting for transfers between devices, per_device(): above = lax.ppermute(edge, 'space', onward)  3.68 us
    ppermute x3, starting transfers between devices, per_device(): lax.ppermute(leaving[k - 1], 'space', flipped(space, 2 * k))  3.55 us
    ppermute x3, starting transfers between devices, per_device(): lax.ppermute(total, 'sample', flipped(sample, j))  3.55 us
    pallas_call x1, Pallas kernels, per_device(): pl.pallas_call(input_kernel, out_shape=(shape(x.shape, BF16), shape((8, 1...  3.32 us
    pallas_call x1, Pallas kernels, per_device(): pl.pallas_call(halo_kernel, out_shape=(shape(cot.shape, BF16), shape((cou...  2.07 us
    ppermute x1, starting transfers between devices, per_device(): low = lax.ppermute(low, 'sample', flipped(sample, 1))  2.06 us
    ppermute x3, waiting for transfers between devices, per_device(): lax.ppermute(total, 'sample', flipped(sample, j))  1.52 us
  transfers between devices with their start and end apart: 11, of which 9 were waited for; matrix products, arithmetic and copies ran while one was open for 0% of the time, Pallas kernels for 27%

profile of v5, /device:TPU:0, one launch (start us, length us, event | category | flops | bytes accessed | tf_op | source)
XLA Modules:
  0.0 35.9 jit_solution(15314769047870636673)
XLA Ops:
  0.6 0.0 copy-start
  0.6 1.1 %edge_plane.1 = (bf16[32,3072]{1,0:T(8,128)(2,1)S(1)}, bf16[384,256]{1,0:T(8,128)(2,1)S(1)}, bf16[384,384]{1,0:T(8,128)(2,1)S(1)}) custom-call(bf16[8,32,3072]{2,1,0:T(8,128)(2,1)} %bitcast.8), custom_call_target="tpu_custom_call" | custom-call | bytes 10485760 | tf_op jit(solution)/shard_map/edge_plane/pallas_call | solution.py:403
  1.7 0.5 %collective-permute-start = (bf16[32,3072]{1,0:T(8,128)(2,1)S(1)}, bf16[32,3072]{1,0:T(8,128)(2,1)S(1)}, u32[]{:S(2)}, u32[]{:S(2)}) collective-permute-start(bf16[32,3072]{1,0:T(8,128)(2,1)S(1)} %get-tuple-element.28), channel_id=1, source_target_pairs={{0,1},{1,2},{2,3},{3,4},{4,5},{5,6},{6,7},{7,0},{8,9},{9,10},{10,1... | collective-permute-start | bytes 589832 | tf_op jit(solution)/shard_map/ppermute | solution.py:417
  2.2 3.7 %own_planes.1 = (bf16[512,4608]{1,0:T(8,128)(2,1)S(1)}, bf16[3456,192]{1,0:T(8,128)(2,1)S(1)}, bf16[3456,192]{1,0:T(8,128)(2,1)S(1)}, f32[512,384]{1,0:T(8,128)S(1)}, bf16[9,288,192]{2,1,0:T(8,128)(2,1)S(1)}) custom-call(bf16[8,32,3072]{2,1,0:T(8,128)(2,1)S(1)} %bitcast.9, bf16[384,256]{1,0:T(8,128)(2,1)S(1)} %get-tuple-element.30.split_ref, ...), custom_call_target="tpu_custom_call" | custom-call | flops 1811939328 | bytes 12582912 | tf_op jit(solution)/shard_map/own_planes/pallas_call | solution.py:418
  5.9 3.7 %collective-permute-done.above_ref = bf16[32,3072]{1,0:T(8,128)(2,1)S(1)} collective-permute-done((bf16[32,3072]{1,0:T(8,128)(2,1)S(1)}, bf16[32,3072]{1,0:T(8,128)(2,1)S(1)}, u32[]{:S(2)}, u32[]{:S(2)}) %collective-permute-start) | collective-permute-done | bytes 196640 | tf_op jit(solution)/shard_map/ppermute | solution.py:417
  9.6 2.1 %halo_and_sent_half.1 = (bf16[4,16,3072]{2,1,0:T(8,128)(2,1)S(1)}, bf16[512,384]{1,0:T(8,128)(2,1)S(1)}, bf16[128,384]{1,0:T(8,128)(2,1)S(1)}, bf16[384,512]{1,0...) custom-call(bf16[32,3072]{1,0:T(8,128)(2,1)S(1)} %collective-permute-done.above_ref, ...), custom_call_target="tpu_custom_call" | custom-call | flops 905969664 | bytes 8388608 | tf_op jit(solution)/shard_map/halo_and_sent_half/pallas_call | solution.py:435
  11.7 0.1 collective-permute-start.2
  11.8 1.2 %kept_half.1.keep_ref = f32[96,2688]{1,0:T(8,128)S(1)} custom-call(bf16[384,512]{1,0:T(8,128)(2,1)S(1)} %get-tuple-element.39.turned_ref, bf16[128,1536]{1,0:T(8,128)(2,1)S(1)} %get-tuple-element.40.edge, bf16[512,4608]{1,0:T(8,128)(2,1)S(1)} %get-tuple-element.31.wide), custom_call_target="tpu_custom_call" | custom-call | flops 905969664 | bytes 8388608 | tf_op jit(solution)/shard_map/kept_half/pallas_call | solution.py:456
  13.0 0.7 %collective-permute-done.2.got_ref = bf16[96,2688]{1,0:T(8,128)(2,1)S(1)} collective-permute-done((bf16[96,2688]{1,0:T(8,128)(2,1)S(1)}, bf16[96,2688]{1,0:T(8,128)(2,1)S(1)}, u32[]{:S(2)}, u32[]{:S(2)}) %collective-permute-start.2) | collective-permute-done | bytes 516128 | tf_op jit(solution)/shard_map/ppermute | solution.py:454
  13.6 0.1 pair_sum.1
  13.8 2.1 %collective-permute-start.3 = (bf16[4,120,128]{2,1,0:T(8,128)(2,1)S(1)}, bf16[4,120,128]{2,1,0:T(8,128)(2,1)S(1)}, u32[]{:S(2)}, u32[]{:S(2)}) collective-permute-start(bf16[4,120,128]{2,1,0:T(8,128)(2,1)S(1)} %get-tuple-element.43), channel_id=1, source_target_pairs={{0,8},{8,0},{16,24},{24,16},{1,9},{9,1},{17,25},{25,17},{2,10},{10... | collective-permute-start | bytes 368648 | tf_op jit(solution)/shard_map/ppermute | solution.py:478
  15.8 1.5 %collective-permute-start.4 = (bf16[4,120,128]{2,1,0:T(8,128)(2,1)S(1)}, bf16[4,120,128]{2,1,0:T(8,128)(2,1)S(1)}, u32[]{:S(2)}, u32[]{:S(2)}) collective-permute-start(bf16[4,120,128]{2,1,0:T(8,128)(2,1)S(1)} %get-tuple-element.44), channel_id=1, source_target_pairs={{0,16},{8,24},{16,0},{24,8},{1,17},{9,25},{17,1},{25,9},{2,18},{10... | collective-permute-start | bytes 368648 | tf_op jit(solution)/shard_map/ppermute | solution.py:479
  17.4 1.0 %collective-permute-start.1 = (bf16[128,384]{1,0:T(8,128)(2,1)S(1)}, bf16[128,384]{1,0:T(8,128)(2,1)S(1)}, u32[]{:S(2)}, u32[]{:S(2)}) collective-permute-start(bf16[128,384]{1,0:T(8,128)(2,1)S(1)} %get-tuple-element.36), channel_id=1, source_target_pairs={{1,0},{2,1},{3,2},{4,3},{5,4},{6,5},{7,6},{0,7},{9,8},{10,9},{11,1... | collective-permute-start | bytes 294920 | tf_op jit(solution)/shard_map/ppermute | solution.py:455
  18.3 1.1 %collective-permute-done.3.low_ref = bf16[4,120,128]{2,1,0:T(8,128)(2,1)S(1)} collective-permute-done((bf16[4,120,128]{2,1,0:T(8,128)(2,1)S(1)}, bf16[4,120,128]{2,1,0:T(8,128)(2,1)S(1)}, u32[]{:S(2)}, u32[]{:S(2)}) %collective-permute-start.3) | collective-permute-done | bytes 122912 | tf_op jit(solution)/shard_map/ppermute | solution.py:478
  19.5 1.5 %collective-permute-done.4.high_ref = bf16[4,120,128]{2,1,0:T(8,128)(2,1)S(1)} collective-permute-done((bf16[4,120,128]{2,1,0:T(8,128)(2,1)S(1)}, bf16[4,120,128]{2,1,0:T(8,128)(2,1)S(1)}, u32[]{:S(2)}, u32[]{:S(2)}) %collective-permute-start.4) | collective-permute-done | bytes 122912 | tf_op jit(solution)/shard_map/ppermute | solution.py:479
  20.9 0.1 cross_sum.1
  21.0 1.0 %collective-permute-start.5 = (bf16[248,128]{1,0:T(8,128)(2,1)S(1)}, bf16[248,128]{1,0:T(8,128)(2,1)S(1)}, u32[]{:S(2)}, u32[]{:S(2)}) collective-permute-start(bf16[248,128]{1,0:T(8,128)(2,1)S(1)} %get-tuple-element.46), channel_id=1, source_target_pairs={{0,4},{1,5},{2,6},{3,7},{4,0},{5,1},{6,2},{7,3},{8,12},{9,13},{10,... | collective-permute-start | bytes 190472 | tf_op jit(solution)/shard_map/ppermute | solution.py:489
  22.0 1.3 %collective-permute-start.6 = (bf16[248,128]{1,0:T(8,128)(2,1)S(1)}, bf16[248,128]{1,0:T(8,128)(2,1)S(1)}, u32[]{:S(2)}, u32[]{:S(2)}) collective-permute-start(bf16[248,128]{1,0:T(8,128)(2,1)S(1)} %get-tuple-element.47), channel_id=1, source_target_pairs={{0,6},{1,7},{2,4},{3,5},{4,2},{5,3},{6,0},{7,1},{8,14},{9,15},{10,... | collective-permute-start | bytes 190472 | tf_op jit(solution)/shard_map/ppermute | solution.py:489
  23.4 1.2 %collective-permute-start.7 = (bf16[248,128]{1,0:T(8,128)(2,1)S(1)}, bf16[248,128]{1,0:T(8,128)(2,1)S(1)}, u32[]{:S(2)}, u32[]{:S(2)}) collective-permute-start(bf16[248,128]{1,0:T(8,128)(2,1)S(1)} %get-tuple-element.48), channel_id=1, source_target_pairs={{0,2},{1,3},{2,0},{3,1},{4,6},{5,7},{6,4},{7,5},{8,10},{9,11},{10,... | collective-permute-start | bytes 190472 | tf_op jit(solution)/shard_map/ppermute | solution.py:489
  24.5 0.0 collective-permute-done.1.below_ref
  24.5 3.3 %input_grad.1 = (bf16[8,32,3072]{2,1,0:T(8,128)(2,1)S(1)}, f32[8,128]{1,0:T(8,128)S(1)}) custom-call(bf16[512,384]{1,0:T(8,128)(2,1)S(1)} %get-tuple-element.35.gp_ref, bf16[128,384]{1,0:T(8,128)(2,1)S(1)} %collective-permute-done.1.below_ref, bf16[9,288,192]{2,1,0:T(8,128)(2,1)S(1)} %get-tuple-element.37.w_ref), custom_call_target="tpu_custom_call" | custom-call | flops 1811939328 | bytes 8388608 | tf_op jit(solution)/shard_map/input_grad/pallas_call | solution.py:493
  27.9 0.0 collective-permute-done.5.refs_0_
  27.9 0.3 collective-permute-done.6.refs_1_
  28.2 0.4 collective-permute-done.7.refs_2_
  28.6 1.6 %collective-permute-start.10 = (bf16[248,128]{1,0:T(8,128)(2,1)S(1)}, bf16[248,128]{1,0:T(8,128)(2,1)S(1)}, u32[]{:S(2)}, u32[]{:S(2)}) collective-permute-start(bf16[248,128]{1,0:T(8,128)(2,1)S(1)} %depth_sum.1.total_ref.refs_0_), channel_id=1, source_target_pairs={{0,24},{8,16},{16,8},{24,0},{1,25},{9,17},{17,9},{25,1},{2,26},{10... | collective-permute-start | bytes 190472 | tf_op jit(solution)/shard_map/ppermute | solution.py:521
  30.2 0.5 %collective-permute-start.9 = (bf16[248,128]{1,0:T(8,128)(2,1)S(1)}, bf16[248,128]{1,0:T(8,128)(2,1)S(1)}, u32[]{:S(2)}, u32[]{:S(2)}) collective-permute-start(bf16[248,128]{1,0:T(8,128)(2,1)S(1)} %depth_sum.1.total_ref.refs_0_), channel_id=1, source_target_pairs={{0,16},{8,24},{16,0},{24,8},{1,17},{9,25},{17,1},{25,9},{2,18},{10... | collective-permute-start | bytes 190472 | tf_op jit(solution)/shard_map/ppermute | solution.py:521
  30.7 1.4 %collective-permute-start.8 = (bf16[248,128]{1,0:T(8,128)(2,1)S(1)}, bf16[248,128]{1,0:T(8,128)(2,1)S(1)}, u32[]{:S(2)}, u32[]{:S(2)}) collective-permute-start(bf16[248,128]{1,0:T(8,128)(2,1)S(1)} %depth_sum.1.total_ref.refs_0_), channel_id=1, source_target_pairs={{0,8},{8,0},{16,24},{24,16},{1,9},{9,1},{17,25},{25,17},{2,10},{10... | collective-permute-start | bytes 190472 | tf_op jit(solution)/shard_map/ppermute | solution.py:521
  32.2 1.3 %store.1 = (bf16[4,16,3072]{2,1,0:T(8,128)(2,1)}, bf16[8,32,3072]{2,1,0:T(8,128)(2,1)}) custom-call(bf16[248,128]{1,0:T(8,128)(2,1)S(1)} %depth_sum.1.total_ref.refs_0_, bf16[4,16,3072]{2,1,0:T(8,128)(2,1)S(1)} %get-tuple-element.49.refs_0_, bf16[8,32,3072]{2,1,0:T(8,128)(2,1)S(1)} %get-tuple-element.50.refs_1_), custom_call_target="tpu_custom_call" | custom-call | tf_op jit(solution)/shard_map/store/pallas_call | solution.py:512
  33.5 0.4 collective-permute-done.10.refs_3_
  33.8 0.7 %collective-permute-done.9.refs_2_ = bf16[248,128]{1,0:T(8,128)(2,1)S(1)} collective-permute-done((bf16[248,128]{1,0:T(8,128)(2,1)S(1)}, bf16[248,128]{1,0:T(8,128)(2,1)S(1)}, u32[]{:S(2)}, u32[]{:S(2)}) %collective-permute-start.9) | collective-permute-done | bytes 63520 | tf_op jit(solution)/shard_map/ppermute | solution.py:521
  34.5 0.5 %collective-permute-done.8.refs_1_ = bf16[248,128]{1,0:T(8,128)(2,1)S(1)} collective-permute-done((bf16[248,128]{1,0:T(8,128)(2,1)S(1)}, bf16[248,128]{1,0:T(8,128)(2,1)S(1)}, u32[]{:S(2)}, u32[]{:S(2)}) %collective-permute-start.8) | collective-permute-done | bytes 63520 | tf_op jit(solution)/shard_map/ppermute | solution.py:521
  35.0 0.9 %sample_sum.1 = f32[27,24,96]{2,1,0:T(8,128)} custom-call(bf16[248,128]{1,0:T(8,128)(2,1)S(1)} %depth_sum.1.total_ref.refs_0_, bf16[248,128]{1,0:T(8,128)(2,1)S(1)} %collective-permute-done.8.refs_1_, bf16[248,128]{1,0:T(8,128)(2,1)S(1)} %collective-permute-done.9.refs_2_, bf16[248,128]{1,0:T(8,128)(2,1)S(1)} %collective-permute-done.10.refs_3_), custom_call_target="tpu_custom_call" | custom-call | tf_op jit(solution)/shard_map/sample_sum/pallas_call | solution.py:522
  (4 shorter events, 0.0 us)
Async XLA Ops:
  0.6 1.6 %copy-start = (bf16[1,8,32,3072]{3,2,1,0:T(8,128)(2,1)S(1)}, bf16[1,8,32,3072]{3,2,1,0:T(8,128)(2,1)}, u32[]{:S(2)}) copy-start(bf16[1,8,32,3072]{3,2,1,0:T(8,128)(2,1)} %param.3) | copy-start | bytes 4718596
  1.7 7.9 %collective-permute-start = (bf16[32,3072]{1,0:T(8,128)(2,1)S(1)}, bf16[32,3072]{1,0:T(8,128)(2,1)S(1)}, u32[]{:S(2)}, u32[]{:S(2)}) collective-permute-start(bf16[32,3072]{1,0:T(8,128)(2,1)S(1)} %get-tuple-element.28), channel_id=1, source_target_pairs={{0,1},{1,2},{2,3},{3,4},{4,5},{5,6},{6,7},{7,0},{8,9},{9,10},{10,1... | collective-permute-start | bytes 589832 | tf_op jit(solution)/shard_map/ppermute | solution.py:417
  2.2 7.4 %copy-start.1 = (bf16[1,4,16,3072]{3,2,1,0:T(8,128)(2,1)S(1)}, bf16[1,4,16,3072]{3,2,1,0:T(8,128)(2,1)}, u32[]{:S(2)}) copy-start(bf16[1,4,16,3072]{3,2,1,0:T(8,128)(2,1)} %param.5) | copy-start | bytes 1179652
  11.7 2.0 %collective-permute-start.2 = (bf16[96,2688]{1,0:T(8,128)(2,1)S(1)}, bf16[96,2688]{1,0:T(8,128)(2,1)S(1)}, u32[]{:S(2)}, u32[]{:S(2)}) collective-permute-start(bf16[96,2688]{1,0:T(8,128)(2,1)S(1)} %get-tuple-element.41), channel_id=1, source_target_pairs={{0,1},{1,0},{2,3},{3,2},{4,5},{5,4},{6,7},{7,6},{8,9},{9,8},{10,11... | collective-permute-start | bytes 1548296 | tf_op jit(solution)/shard_map/ppermute | solution.py:454
  13.8 5.7 %collective-permute-start.3 = (bf16[4,120,128]{2,1,0:T(8,128)(2,1)S(1)}, bf16[4,120,128]{2,1,0:T(8,128)(2,1)S(1)}, u32[]{:S(2)}, u32[]{:S(2)}) collective-permute-start(bf16[4,120,128]{2,1,0:T(8,128)(2,1)S(1)} %get-tuple-element.43), channel_id=1, source_target_pairs={{0,8},{8,0},{16,24},{24,16},{1,9},{9,1},{17,25},{25,17},{2,10},{10... | collective-permute-start | bytes 368648 | tf_op jit(solution)/shard_map/ppermute | solution.py:478
  15.8 5.1 %collective-permute-start.4 = (bf16[4,120,128]{2,1,0:T(8,128)(2,1)S(1)}, bf16[4,120,128]{2,1,0:T(8,128)(2,1)S(1)}, u32[]{:S(2)}, u32[]{:S(2)}) collective-permute-start(bf16[4,120,128]{2,1,0:T(8,128)(2,1)S(1)} %get-tuple-element.44), channel_id=1, source_target_pairs={{0,16},{8,24},{16,0},{24,8},{1,17},{9,25},{17,1},{25,9},{2,18},{10... | collective-permute-start | bytes 368648 | tf_op jit(solution)/shard_map/ppermute | solution.py:479
  17.4 7.2 %collective-permute-start.1 = (bf16[128,384]{1,0:T(8,128)(2,1)S(1)}, bf16[128,384]{1,0:T(8,128)(2,1)S(1)}, u32[]{:S(2)}, u32[]{:S(2)}) collective-permute-start(bf16[128,384]{1,0:T(8,128)(2,1)S(1)} %get-tuple-element.36), channel_id=1, source_target_pairs={{1,0},{2,1},{3,2},{4,3},{5,4},{6,5},{7,6},{0,7},{9,8},{10,9},{11,1... | collective-permute-start | bytes 294920 | tf_op jit(solution)/shard_map/ppermute | solution.py:455
  21.0 6.9 %collective-permute-start.5 = (bf16[248,128]{1,0:T(8,128)(2,1)S(1)}, bf16[248,128]{1,0:T(8,128)(2,1)S(1)}, u32[]{:S(2)}, u32[]{:S(2)}) collective-permute-start(bf16[248,128]{1,0:T(8,128)(2,1)S(1)} %get-tuple-element.46), channel_id=1, source_target_pairs={{0,4},{1,5},{2,6},{3,7},{4,0},{5,1},{6,2},{7,3},{8,12},{9,13},{10,... | collective-permute-start | bytes 190472 | tf_op jit(solution)/shard_map/ppermute | solution.py:489
  22.0 6.2 %collective-permute-start.6 = (bf16[248,128]{1,0:T(8,128)(2,1)S(1)}, bf16[248,128]{1,0:T(8,128)(2,1)S(1)}, u32[]{:S(2)}, u32[]{:S(2)}) collective-permute-start(bf16[248,128]{1,0:T(8,128)(2,1)S(1)} %get-tuple-element.47), channel_id=1, source_target_pairs={{0,6},{1,7},{2,4},{3,5},{4,2},{5,3},{6,0},{7,1},{8,14},{9,15},{10,... | collective-permute-start | bytes 190472 | tf_op jit(solution)/shard_map/ppermute | solution.py:489
  23.4 5.2 %collective-permute-start.7 = (bf16[248,128]{1,0:T(8,128)(2,1)S(1)}, bf16[248,128]{1,0:T(8,128)(2,1)S(1)}, u32[]{:S(2)}, u32[]{:S(2)}) collective-permute-start(bf16[248,128]{1,0:T(8,128)(2,1)S(1)} %get-tuple-element.48), channel_id=1, source_target_pairs={{0,2},{1,3},{2,0},{3,1},{4,6},{5,7},{6,4},{7,5},{8,10},{9,11},{10,... | collective-permute-start | bytes 190472 | tf_op jit(solution)/shard_map/ppermute | solution.py:489
  28.6 5.2 %collective-permute-start.10 = (bf16[248,128]{1,0:T(8,128)(2,1)S(1)}, bf16[248,128]{1,0:T(8,128)(2,1)S(1)}, u32[]{:S(2)}, u32[]{:S(2)}) collective-permute-start(bf16[248,128]{1,0:T(8,128)(2,1)S(1)} %depth_sum.1.total_ref.refs_0_), channel_id=1, source_target_pairs={{0,24},{8,16},{16,8},{24,0},{1,25},{9,17},{17,9},{25,1},{2,26},{10... | collective-permute-start | bytes 190472 | tf_op jit(solution)/shard_map/ppermute | solution.py:521
  30.2 4.3 %collective-permute-start.9 = (bf16[248,128]{1,0:T(8,128)(2,1)S(1)}, bf16[248,128]{1,0:T(8,128)(2,1)S(1)}, u32[]{:S(2)}, u32[]{:S(2)}) collective-permute-start(bf16[248,128]{1,0:T(8,128)(2,1)S(1)} %depth_sum.1.total_ref.refs_0_), channel_id=1, source_target_pairs={{0,16},{8,24},{16,0},{24,8},{1,17},{9,25},{17,1},{25,9},{2,18},{10... | collective-permute-start | bytes 190472 | tf_op jit(solution)/shard_map/ppermute | solution.py:521
  30.7 4.2 %collective-permute-start.8 = (bf16[248,128]{1,0:T(8,128)(2,1)S(1)}, bf16[248,128]{1,0:T(8,128)(2,1)S(1)}, u32[]{:S(2)}, u32[]{:S(2)}) collective-permute-start(bf16[248,128]{1,0:T(8,128)(2,1)S(1)} %depth_sum.1.total_ref.refs_0_), channel_id=1, source_target_pairs={{0,8},{8,0},{16,24},{24,16},{1,9},{9,1},{17,25},{25,17},{2,10},{10... | collective-permute-start | bytes 190472 | tf_op jit(solution)/shard_map/ppermute | solution.py:521

commit v6 on v5

--- a/solution.py
+++ b/solution.py
@@ -274,10 +274,10 @@
     )
 
 
-def pair_kernel(keep_ref, got_ref, mine_ref, low_ref, high_ref):
+def pair_kernel(keep_ref, got_ref, *refs):
     low, high = sample_bits()
-    steps, side = low_ref.shape[:2]
-    rows = keep_ref.shape[0] // steps
+    half, side = refs[1].shape[:2]
+    rows = keep_ref.shape[0] // (2 * half)
 
     def total(start, lanes):
         lanes = pl.ds(pl.multiple_of(start, 128), lanes)
@@ -287,17 +287,19 @@
     kept = total(low * SIDE, SIDE), total((2 + high) * SIDE, SIDE)
     last = keep_ref[:, REST:] + got_ref[:, REST:].astype(F32)
     lane = iota((8, 128), 1)
-    for k in range(steps):
+    for k in range(2 * half):
+        mine_ref, low_ref, high_ref = refs[:3] if k >= half else refs[3:]
         at = slice(k * rows, (k + 1) * rows)
-        low_ref[k] = listed(sent[0][at]).astype(BF16)
-        high_ref[k] = listed(sent[1][at]).astype(BF16)
-        mine_ref[k, :side] = listed(kept[0][at])
-        mine_ref[k, side : 2 * side] = listed(kept[1][at])
+        to = k % half
+        low_ref[to] = listed(sent[0][at]).astype(BF16)
+        high_ref[to] = listed(sent[1][at]).astype(BF16)
+        mine_ref[to, :side] = listed(kept[0][at])
+        mine_ref[to, side : 2 * side] = listed(kept[1][at])
         packed = jnp.zeros((8, 128), F32)
         for r in range(rows // 8):
             tile = last[k * rows + r * 8 : k * rows + r * 8 + 8]
             packed = packed + pltpu.roll(jnp.where(lane < LEFT, tile, 0.0), r * LEFT, 1)
-        mine_ref[k, 2 * side :] = packed
+        mine_ref[to, 2 * side :] = packed
 
 
 def cross_kernel(mine_ref, low_ref, high_ref, *out_refs):
@@ -312,6 +314,10 @@
             axis=0,
         )
         out_ref[...] = total.astype(out_ref.dtype)
+
+
+def later_cross_kernel(early, *refs):
+    cross_kernel(*refs[early:])
 
 
 def depth_kernel(done_ref, own_ref, *refs):
@@ -463,32 +469,49 @@
         name="kept_half",
     )(turned, halo, wide)
 
-    mine, low, high_lanes = pl.pallas_call(
+    half = depth // 2
+    batch = (
+        shape((half,) + part, F32),
+        shape((half, side, 128), BF16),
+        shape((half, side, 128), BF16),
+    )
+    early_mine, early_low, early_high, later_mine, later_low, later_high = pl.pallas_call(
         pair_kernel,
-        out_shape=(
-            shape((depth,) + part, F32),
-            shape((depth, side, 128), BF16),
-            shape((depth, side, 128), BF16),
-        ),
+        out_shape=batch * 2,
         in_specs=[vmem] * 2,
-        out_specs=(vmem,) * 3,
+        out_specs=(vmem,) * 6,
         compiler_params=params,
         name="pair_sum",
     )(keep, got)
-    low = lax.ppermute(low, "sample", flipped(sample, 1))
-    high_lanes = lax.ppermute(high_lanes, "sample", flipped(sample, sample // 2))
+
+    def crossed(low_half, high_half):
+        return (
+            lax.ppermute(low_half, "sample", flipped(sample, 1)),
+            lax.ppermute(high_half, "sample", flipped(sample, sample // 2)),
+        )
+
+    early = crossed(early_low, early_high)
+    later = crossed(later_low, later_high)
+    leaving = pl.pallas_call(
+        cross_kernel,
+        out_shape=(shape(part, BF16),) * half,
+        in_specs=[vmem] * 3,
+        out_specs=(vmem,) * half,
+        compiler_params=params,
+        name="early_cross_sum",
+    )(early_mine, *early)
+    came = [
+        lax.ppermute(leaving[k - half], "space", flipped(space, 2 * k)) for k in range(half, depth)
+    ]
     own, *leaving = pl.pallas_call(
-        cross_kernel,
-        out_shape=(shape(part, F32),) + (shape(part, BF16),) * (depth - 1),
-        in_specs=[vmem] * 3,
-        out_specs=(vmem,) * depth,
-        compiler_params=params,
-        name="cross_sum",
-    )(mine, low, high_lanes)
-    came = [
-        lax.ppermute(leaving[k - 1], "space", flipped(space, 2 * k))
-        for k in [*range(depth // 2, depth), *range(1, depth // 2)]
-    ]
+        functools.partial(later_cross_kernel, half),
+        out_shape=(shape(part, F32),) + (shape(part, BF16),) * (half - 1),
+        in_specs=[vmem] * (half + 3),
+        out_specs=(vmem,) * half,
+        compiler_params=params,
+        name="later_cross_sum",
+    )(*leaving, later_mine, *later)
+    came += [lax.ppermute(leaving[k - 1], "space", flipped(space, 2 * k)) for k in range(1, half)]
 
     grad_in, done = pl.pallas_call(
         input_kernel,

time: 36.1 us -> 36.3 us (level)
  starting transfers between devices: 12.2 us -> 14.3 us
  waiting for transfers between devices: 9.19 us -> 7.39 us
    ppermute x2 -> x6, starting transfers between devices: 3.58 us -> 6.77 us  [the longest x2 2.65 us: per_device(): lax.ppermute(leaving[k - half], 'space', flipped(space, 2 * k))]
    ppermute x3 -> x1, starting transfers between devices: 3.55 us -> 0.96 us  [per_device(): lax.ppermute(leaving[k - 1], 'space', flipped(space, 2 * k))]
    ppermute x1, starting transfers between devices: 0.98 us -> 2.4 us  [per_device(): below = lax.ppermute(first, 'space', back)]
    ppermute x2 -> x6, waiting for transfers between devices: 2.59 us -> 1.66 us  [the longest x2 1.12 us: crossed(): lax.ppermute(high_half, 'sample', flipped(sample, sample // 2))]
    ppermute x3 -> x1, waiting for transfers between devices: 0.7 us -> 0.01 us  [per_device(): lax.ppermute(leaving[k - 1], 'space', flipped(space, 2 * k))]
    ppermute x1, waiting for transfers between devices: 0.69 us -> 0.01 us  [per_device(): got = lax.ppermute(send, 'space', in_chip)]
    ppermute x3, waiting for transfers between devices: 1.52 us -> 2.02 us  [per_device(): lax.ppermute(total, 'sample', flipped(sample, j))]
  transfers between devices with their start and end apart: 11 -> 13, of which waited for: 9 -> 6; matrix products, arithmetic and copies ran while one was open for 0% -> 0% of each run, Pallas kernels for 27% -> 27%
where the time goes in v6:
time: 36.3 us; the launch traced here: 36.2 us
  starting transfers between devices  14.3 us (39%)
  Pallas kernels  13.8 us (38%)
  waiting for transfers between devices  7.39 us (20%)
  between operations  0.75 us (2%)
    pallas_call x1, Pallas kernels, per_device(): pl.pallas_call(own_kernel, out_shape=(shape((count, TAPS * SPAN), BF16),...  3.69 us
    ppermute x1, waiting for transfers between devices, per_device(): above = lax.ppermute(edge, 'space', onward)  3.68 us
    ppermute x3, starting transfers between devices, per_device(): lax.ppermute(total, 'sample', flipped(sample, j))  3.55 us
    pallas_call x1, Pallas kernels, per_device(): pl.pallas_call(input_kernel, out_shape=(shape(x.shape, BF16), shape((8, 1...  3.32 us
    ppermute x2, starting transfers between devices, per_device(): lax.ppermute(leaving[k - half], 'space', flipped(space, 2 * k))  2.65 us
    ppermute x1, starting transfers between devices, per_device(): below = lax.ppermute(first, 'space', back)  2.4 us
    ppermute x2, starting transfers between devices, crossed(): lax.ppermute(low_half, 'sample', flipped(sample, 1))  2.09 us
    pallas_call x1, Pallas kernels, per_device(): pl.pallas_call(halo_kernel, out_shape=(shape(cot.shape, BF16), shape((cou...  2.07 us
  transfers between devices with their start and end apart: 13, of which 6 were waited for; matrix products, arithmetic and copies ran while one was open for 0% of the time, Pallas kernels for 27%

profile of v6, /device:TPU:0, one launch (start us, length us, event | category | flops | bytes accessed | tf_op | source)
XLA Modules:
  0.0 36.2 jit_solution(1552821597010574392)
XLA Ops:
  0.6 1.1 %edge_plane.1 = (bf16[32,3072]{1,0:T(8,128)(2,1)S(1)}, bf16[384,256]{1,0:T(8,128)(2,1)S(1)}, bf16[384,384]{1,0:T(8,128)(2,1)S(1)}) custom-call(bf16[8,32,3072]{2,1,0:T(8,128)(2,1)} %bitcast.8), custom_call_target="tpu_custom_call" | custom-call | bytes 10485760 | tf_op jit(solution)/shard_map/edge_plane/pallas_call | solution.py:409
  1.7 0.5 %collective-permute-start = (bf16[32,3072]{1,0:T(8,128)(2,1)S(1)}, bf16[32,3072]{1,0:T(8,128)(2,1)S(1)}, u32[]{:S(2)}, u32[]{:S(2)}) collective-permute-start(bf16[32,3072]{1,0:T(8,128)(2,1)S(1)} %get-tuple-element.31), channel_id=1, source_target_pairs={{0,1},{1,2},{2,3},{3,4},{4,5},{5,6},{6,7},{7,0},{8,9},{9,10},{10,1... | collective-permute-start | bytes 589832 | tf_op jit(solution)/shard_map/ppermute | solution.py:423
  2.2 3.7 %own_planes.1 = (bf16[512,4608]{1,0:T(8,128)(2,1)S(1)}, bf16[3456,192]{1,0:T(8,128)(2,1)S(1)}, bf16[3456,192]{1,0:T(8,128)(2,1)S(1)}, f32[512,384]{1,0:T(8,128)S(1)}, bf16[9,288,192]{2,1,0:T(8,128)(2,1)S(1)}) custom-call(bf16[8,32,3072]{2,1,0:T(8,128)(2,1)S(1)} %bitcast.9, bf16[384,256]{1,0:T(8,128)(2,1)S(1)} %get-tuple-element.33.split_ref, ...), custom_call_target="tpu_custom_call" | custom-call | flops 1811939328 | bytes 12582912 | tf_op jit(solution)/shard_map/own_planes/pallas_call | solution.py:424
  5.9 3.7 %collective-permute-done.above_ref = bf16[32,3072]{1,0:T(8,128)(2,1)S(1)} collective-permute-done((bf16[32,3072]{1,0:T(8,128)(2,1)S(1)}, bf16[32,3072]{1,0:T(8,128)(2,1)S(1)}, u32[]{:S(2)}, u32[]{:S(2)}) %collective-permute-start) | collective-permute-done | bytes 196640 | tf_op jit(solution)/shard_map/ppermute | solution.py:423
  9.6 2.1 %halo_and_sent_half.1 = (bf16[4,16,3072]{2,1,0:T(8,128)(2,1)S(1)}, bf16[512,384]{1,0:T(8,128)(2,1)S(1)}, bf16[128,384]{1,0:T(8,128)(2,1)S(1)}, bf16[384,512]{1,0...) custom-call(bf16[32,3072]{1,0:T(8,128)(2,1)S(1)} %collective-permute-done.above_ref, ...), custom_call_target="tpu_custom_call" | custom-call | flops 905969664 | bytes 8388608 | tf_op jit(solution)/shard_map/halo_and_sent_half/pallas_call | solution.py:441
  11.7 0.1 collective-permute-start.2
  11.8 2.4 %collective-permute-start.1 = (bf16[128,384]{1,0:T(8,128)(2,1)S(1)}, bf16[128,384]{1,0:T(8,128)(2,1)S(1)}, u32[]{:S(2)}, u32[]{:S(2)}) collective-permute-start(bf16[128,384]{1,0:T(8,128)(2,1)S(1)} %get-tuple-element.39), channel_id=1, source_target_pairs={{1,0},{2,1},{3,2},{4,3},{5,4},{6,5},{7,6},{0,7},{9,8},{10,9},{11,1... | collective-permute-start | bytes 294920 | tf_op jit(solution)/shard_map/ppermute | solution.py:461
  14.2 1.2 %kept_half.1.keep_ref = f32[96,2688]{1,0:T(8,128)S(1)} custom-call(bf16[384,512]{1,0:T(8,128)(2,1)S(1)} %get-tuple-element.42.turned_ref, bf16[128,1536]{1,0:T(8,128)(2,1)S(1)} %get-tuple-element.43.edge, bf16[512,4608]{1,0:T(8,128)(2,1)S(1)} %get-tuple-element.34.wide), custom_call_target="tpu_custom_call" | custom-call | flops 905969664 | bytes 8388608 | tf_op jit(solution)/shard_map/kept_half/pallas_call | solution.py:462
  15.4 0.0 collective-permute-done.2.got_ref
  15.4 0.1 pair_sum.1
  15.5 1.5 %collective-permute-start.3 = (bf16[2,120,128]{2,1,0:T(8,128)(2,1)S(1)}, bf16[2,120,128]{2,1,0:T(8,128)(2,1)S(1)}, u32[]{:S(2)}, u32[]{:S(2)}) collective-permute-start(bf16[2,120,128]{2,1,0:T(8,128)(2,1)S(1)} %get-tuple-element.46), channel_id=1, source_target_pairs={{0,8},{8,0},{16,24},{24,16},{1,9},{9,1},{17,25},{25,17},{2,10},{10... | collective-permute-start | bytes 184328 | tf_op jit(solution)/shard_map/ppermute | solution.py:489
  17.1 1.5 %collective-permute-start.4 = (bf16[2,120,128]{2,1,0:T(8,128)(2,1)S(1)}, bf16[2,120,128]{2,1,0:T(8,128)(2,1)S(1)}, u32[]{:S(2)}, u32[]{:S(2)}) collective-permute-start(bf16[2,120,128]{2,1,0:T(8,128)(2,1)S(1)} %get-tuple-element.47), channel_id=1, source_target_pairs={{0,16},{8,24},{16,0},{24,8},{1,17},{9,25},{17,1},{25,9},{2,18},{10... | collective-permute-start | bytes 184328 | tf_op jit(solution)/shard_map/ppermute | solution.py:490
  18.6 0.5 %collective-permute-start.5 = (bf16[2,120,128]{2,1,0:T(8,128)(2,1)S(1)}, bf16[2,120,128]{2,1,0:T(8,128)(2,1)S(1)}, u32[]{:S(2)}, u32[]{:S(2)}) collective-permute-start(bf16[2,120,128]{2,1,0:T(8,128)(2,1)S(1)} %get-tuple-element.51), channel_id=1, source_target_pairs={{0,8},{8,0},{16,24},{24,16},{1,9},{9,1},{17,25},{25,17},{2,10},{10... | collective-permute-start | bytes 184328 | tf_op jit(solution)/shard_map/ppermute | solution.py:489
  19.1 0.5 %collective-permute-start.6 = (bf16[2,120,128]{2,1,0:T(8,128)(2,1)S(1)}, bf16[2,120,128]{2,1,0:T(8,128)(2,1)S(1)}, u32[]{:S(2)}, u32[]{:S(2)}) collective-permute-start(bf16[2,120,128]{2,1,0:T(8,128)(2,1)S(1)} %get-tuple-element.52), channel_id=1, source_target_pairs={{0,16},{8,24},{16,0},{24,8},{1,17},{9,25},{17,1},{25,9},{2,18},{10... | collective-permute-start | bytes 184328 | tf_op jit(solution)/shard_map/ppermute | solution.py:490
  19.6 0.5 %collective-permute-done.3.low_ref = bf16[2,120,128]{2,1,0:T(8,128)(2,1)S(1)} collective-permute-done((bf16[2,120,128]{2,1,0:T(8,128)(2,1)S(1)}, bf16[2,120,128]{2,1,0:T(8,128)(2,1)S(1)}, u32[]{:S(2)}, u32[]{:S(2)}) %collective-permute-start.3) | collective-permute-done | bytes 61472 | tf_op jit(solution)/shard_map/ppermute | solution.py:489
  20.2 1.1 %collective-permute-done.4.high_ref = bf16[2,120,128]{2,1,0:T(8,128)(2,1)S(1)} collective-permute-done((bf16[2,120,128]{2,1,0:T(8,128)(2,1)S(1)}, bf16[2,120,128]{2,1,0:T(8,128)(2,1)S(1)}, u32[]{:S(2)}, u32[]{:S(2)}) %collective-permute-start.4) | collective-permute-done | bytes 61472 | tf_op jit(solution)/shard_map/ppermute | solution.py:490
  21.3 0.1 collective-permute-start.7
  21.4 2.6 %collective-permute-start.8 = (bf16[248,128]{1,0:T(8,128)(2,1)S(1)}, bf16[248,128]{1,0:T(8,128)(2,1)S(1)}, u32[]{:S(2)}, u32[]{:S(2)}) collective-permute-start(bf16[248,128]{1,0:T(8,128)(2,1)S(1)} %get-tuple-element.49.refs_1_), channel_id=1, source_target_pairs={{0,6},{1,7},{2,4},{3,5},{4,2},{5,3},{6,0},{7,1},{8,14},{9,15},{10,... | collective-permute-start | bytes 190472 | tf_op jit(solution)/shard_map/ppermute | solution.py:504
  24.0 0.0 collective-permute-done.5.refs_3_
  24.0 0.0 collective-permute-done.6.refs_4_
  24.0 1.0 %collective-permute-start.9 = (bf16[248,128]{1,0:T(8,128)(2,1)S(1)}, bf16[248,128]{1,0:T(8,128)(2,1)S(1)}, u32[]{:S(2)}, u32[]{:S(2)}) collective-permute-start(bf16[248,128]{1,0:T(8,128)(2,1)S(1)} %get-tuple-element.54), channel_id=1, source_target_pairs={{0,2},{1,3},{2,0},{3,1},{4,6},{5,7},{6,4},{7,5},{8,10},{9,11},{10,... | collective-permute-start | bytes 190472 | tf_op jit(solution)/shard_map/ppermute | solution.py:514
  25.0 3.3 %input_grad.1 = (bf16[8,32,3072]{2,1,0:T(8,128)(2,1)S(1)}, f32[8,128]{1,0:T(8,128)S(1)}) custom-call(bf16[512,384]{1,0:T(8,128)(2,1)S(1)} %get-tuple-element.38.gp_ref, bf16[128,384]{1,0:T(8,128)(2,1)S(1)} %collective-permute-done.1.below_ref, bf16[9,288,192]{2,1,0:T(8,128)(2,1)S(1)} %get-tuple-element.40.w_ref), custom_call_target="tpu_custom_call" | custom-call | flops 1811939328 | bytes 8388608 | tf_op jit(solution)/shard_map/input_grad/pallas_call | solution.py:516
  28.3 0.0 collective-permute-done.9.refs_2_
  28.3 0.0 collective-permute-done.8.refs_1_
  28.4 1.6 %collective-permute-start.12 = (bf16[248,128]{1,0:T(8,128)(2,1)S(1)}, bf16[248,128]{1,0:T(8,128)(2,1)S(1)}, u32[]{:S(2)}, u32[]{:S(2)}) collective-permute-start(bf16[248,128]{1,0:T(8,128)(2,1)S(1)} %depth_sum.1.total_ref.refs_0_), channel_id=1, source_target_pairs={{0,24},{8,16},{16,8},{24,0},{1,25},{9,17},{17,9},{25,1},{2,26},{10... | collective-permute-start | bytes 190472 | tf_op jit(solution)/shard_map/ppermute | solution.py:544
  29.9 1.1 %collective-permute-start.11 = (bf16[248,128]{1,0:T(8,128)(2,1)S(1)}, bf16[248,128]{1,0:T(8,128)(2,1)S(1)}, u32[]{:S(2)}, u32[]{:S(2)}) collective-permute-start(bf16[248,128]{1,0:T(8,128)(2,1)S(1)} %depth_sum.1.total_ref.refs_0_), channel_id=1, source_target_pairs={{0,16},{8,24},{16,0},{24,8},{1,17},{9,25},{17,1},{25,9},{2,18},{10... | collective-permute-start | bytes 190472 | tf_op jit(solution)/shard_map/ppermute | solution.py:544
  31.0 0.9 %collective-permute-start.10 = (bf16[248,128]{1,0:T(8,128)(2,1)S(1)}, bf16[248,128]{1,0:T(8,128)(2,1)S(1)}, u32[]{:S(2)}, u32[]{:S(2)}) collective-permute-start(bf16[248,128]{1,0:T(8,128)(2,1)S(1)} %depth_sum.1.total_ref.refs_0_), channel_id=1, source_target_pairs={{0,8},{8,0},{16,24},{24,16},{1,9},{9,1},{17,25},{25,17},{2,10},{10... | collective-permute-start | bytes 190472 | tf_op jit(solution)/shard_map/ppermute | solution.py:544
  31.9 1.3 %store.1 = (bf16[4,16,3072]{2,1,0:T(8,128)(2,1)}, bf16[8,32,3072]{2,1,0:T(8,128)(2,1)}) custom-call(bf16[248,128]{1,0:T(8,128)(2,1)S(1)} %depth_sum.1.total_ref.refs_0_, bf16[4,16,3072]{2,1,0:T(8,128)(2,1)S(1)} %get-tuple-element.55.refs_0_, bf16[8,32,3072]{2,1,0:T(8,128)(2,1)S(1)} %get-tuple-element.56.refs_1_), custom_call_target="tpu_custom_call" | custom-call | tf_op jit(solution)/shard_map/store/pallas_call | solution.py:535
  33.2 0.4 %collective-permute-done.12.refs_3_ = bf16[248,128]{1,0:T(8,128)(2,1)S(1)} collective-permute-done((bf16[248,128]{1,0:T(8,128)(2,1)S(1)}, bf16[248,128]{1,0:T(8,128)(2,1)S(1)}, u32[]{:S(2)}, u32[]{:S(2)}) %collective-permute-start.12) | collective-permute-done | bytes 63520 | tf_op jit(solution)/shard_map/ppermute | solution.py:544
  33.6 0.7 %collective-permute-done.11.refs_2_ = bf16[248,128]{1,0:T(8,128)(2,1)S(1)} collective-permute-done((bf16[248,128]{1,0:T(8,128)(2,1)S(1)}, bf16[248,128]{1,0:T(8,128)(2,1)S(1)}, u32[]{:S(2)}, u32[]{:S(2)}) %collective-permute-start.11) | collective-permute-done | bytes 63520 | tf_op jit(solution)/shard_map/ppermute | solution.py:544
  34.3 1.0 %collective-permute-done.10.refs_1_ = bf16[248,128]{1,0:T(8,128)(2,1)S(1)} collective-permute-done((bf16[248,128]{1,0:T(8,128)(2,1)S(1)}, bf16[248,128]{1,0:T(8,128)(2,1)S(1)}, u32[]{:S(2)}, u32[]{:S(2)}) %collective-permute-start.10) | collective-permute-done | bytes 63520 | tf_op jit(solution)/shard_map/ppermute | solution.py:544
  35.3 0.9 %sample_sum.1 = f32[27,24,96]{2,1,0:T(8,128)} custom-call(bf16[248,128]{1,0:T(8,128)(2,1)S(1)} %depth_sum.1.total_ref.refs_0_, bf16[248,128]{1,0:T(8,128)(2,1)S(1)} %collective-permute-done.10.refs_1_, bf16[248,128]{1,0:T(8,128)(2,1)S(1)} %collective-permute-done.11.refs_2_, bf16[248,128]{1,0:T(8,128)(2,1)S(1)} %collective-permute-done.12.refs_3_), custom_call_target="tpu_custom_call" | custom-call | tf_op jit(solution)/shard_map/sample_sum/pallas_call | solution.py:545
  (9 shorter events, 0.1 us)
Async XLA Ops:
  0.6 1.6 %copy-start = (bf16[1,8,32,3072]{3,2,1,0:T(8,128)(2,1)S(1)}, bf16[1,8,32,3072]{3,2,1,0:T(8,128)(2,1)}, u32[]{:S(2)}) copy-start(bf16[1,8,32,3072]{3,2,1,0:T(8,128)(2,1)} %param.3) | copy-start | bytes 4718596
  1.7 7.9 %collective-permute-start = (bf16[32,3072]{1,0:T(8,128)(2,1)S(1)}, bf16[32,3072]{1,0:T(8,128)(2,1)S(1)}, u32[]{:S(2)}, u32[]{:S(2)}) collective-permute-start(bf16[32,3072]{1,0:T(8,128)(2,1)S(1)} %get-tuple-element.31), channel_id=1, source_target_pairs={{0,1},{1,2},{2,3},{3,4},{4,5},{5,6},{6,7},{7,0},{8,9},{9,10},{10,1... | collective-permute-start | bytes 589832 | tf_op jit(solution)/shard_map/ppermute | solution.py:423
  2.2 7.4 %copy-start.1 = (bf16[1,4,16,3072]{3,2,1,0:T(8,128)(2,1)S(1)}, bf16[1,4,16,3072]{3,2,1,0:T(8,128)(2,1)}, u32[]{:S(2)}) copy-start(bf16[1,4,16,3072]{3,2,1,0:T(8,128)(2,1)} %param.5) | copy-start | bytes 1179652
  11.7 3.7 %collective-permute-start.2 = (bf16[96,2688]{1,0:T(8,128)(2,1)S(1)}, bf16[96,2688]{1,0:T(8,128)(2,1)S(1)}, u32[]{:S(2)}, u32[]{:S(2)}) collective-permute-start(bf16[96,2688]{1,0:T(8,128)(2,1)S(1)} %get-tuple-element.44), channel_id=1, source_target_pairs={{0,1},{1,0},{2,3},{3,2},{4,5},{5,4},{6,7},{7,6},{8,9},{9,8},{10,11... | collective-permute-start | bytes 1548296 | tf_op jit(solution)/shard_map/ppermute | solution.py:460
  11.8 13.2 %collective-permute-start.1 = (bf16[128,384]{1,0:T(8,128)(2,1)S(1)}, bf16[128,384]{1,0:T(8,128)(2,1)S(1)}, u32[]{:S(2)}, u32[]{:S(2)}) collective-permute-start(bf16[128,384]{1,0:T(8,128)(2,1)S(1)} %get-tuple-element.39), channel_id=1, source_target_pairs={{1,0},{2,1},{3,2},{4,3},{5,4},{6,5},{7,6},{0,7},{9,8},{10,9},{11,1... | collective-permute-start | bytes 294920 | tf_op jit(solution)/shard_map/ppermute | solution.py:461
  15.5 4.6 %collective-permute-start.3 = (bf16[2,120,128]{2,1,0:T(8,128)(2,1)S(1)}, bf16[2,120,128]{2,1,0:T(8,128)(2,1)S(1)}, u32[]{:S(2)}, u32[]{:S(2)}) collective-permute-start(bf16[2,120,128]{2,1,0:T(8,128)(2,1)S(1)} %get-tuple-element.46), channel_id=1, source_target_pairs={{0,8},{8,0},{16,24},{24,16},{1,9},{9,1},{17,25},{25,17},{2,10},{10... | collective-permute-start | bytes 184328 | tf_op jit(solution)/shard_map/ppermute | solution.py:489
  17.1 4.2 %collective-permute-start.4 = (bf16[2,120,128]{2,1,0:T(8,128)(2,1)S(1)}, bf16[2,120,128]{2,1,0:T(8,128)(2,1)S(1)}, u32[]{:S(2)}, u32[]{:S(2)}) collective-permute-start(bf16[2,120,128]{2,1,0:T(8,128)(2,1)S(1)} %get-tuple-element.47), channel_id=1, source_target_pairs={{0,16},{8,24},{16,0},{24,8},{1,17},{9,25},{17,1},{25,9},{2,18},{10... | collective-permute-start | bytes 184328 | tf_op jit(solution)/shard_map/ppermute | solution.py:490
  18.6 5.4 %collective-permute-start.5 = (bf16[2,120,128]{2,1,0:T(8,128)(2,1)S(1)}, bf16[2,120,128]{2,1,0:T(8,128)(2,1)S(1)}, u32[]{:S(2)}, u32[]{:S(2)}) collective-permute-start(bf16[2,120,128]{2,1,0:T(8,128)(2,1)S(1)} %get-tuple-element.51), channel_id=1, source_target_pairs={{0,8},{8,0},{16,24},{24,16},{1,9},{9,1},{17,25},{25,17},{2,10},{10... | collective-permute-start | bytes 184328 | tf_op jit(solution)/shard_map/ppermute | solution.py:489
  19.1 4.9 %collective-permute-start.6 = (bf16[2,120,128]{2,1,0:T(8,128)(2,1)S(1)}, bf16[2,120,128]{2,1,0:T(8,128)(2,1)S(1)}, u32[]{:S(2)}, u32[]{:S(2)}) collective-permute-start(bf16[2,120,128]{2,1,0:T(8,128)(2,1)S(1)} %get-tuple-element.52), channel_id=1, source_target_pairs={{0,16},{8,24},{16,0},{24,8},{1,17},{9,25},{17,1},{25,9},{2,18},{10... | collective-permute-start | bytes 184328 | tf_op jit(solution)/shard_map/ppermute | solution.py:490
  21.3 7.0 %collective-permute-start.7 = (bf16[248,128]{1,0:T(8,128)(2,1)S(1)}, bf16[248,128]{1,0:T(8,128)(2,1)S(1)}, u32[]{:S(2)}, u32[]{:S(2)}) collective-permute-start(bf16[248,128]{1,0:T(8,128)(2,1)S(1)} %get-tuple-element.48.refs_0_), channel_id=1, source_target_pairs={{0,4},{1,5},{2,6},{3,7},{4,0},{5,1},{6,2},{7,3},{8,12},{9,13},{10,... | collective-permute-start | bytes 190472 | tf_op jit(solution)/shard_map/ppermute | solution.py:504
  21.4 6.9 %collective-permute-start.8 = (bf16[248,128]{1,0:T(8,128)(2,1)S(1)}, bf16[248,128]{1,0:T(8,128)(2,1)S(1)}, u32[]{:S(2)}, u32[]{:S(2)}) collective-permute-start(bf16[248,128]{1,0:T(8,128)(2,1)S(1)} %get-tuple-element.49.refs_1_), channel_id=1, source_target_pairs={{0,6},{1,7},{2,4},{3,5},{4,2},{5,3},{6,0},{7,1},{8,14},{9,15},{10,... | collective-permute-start | bytes 190472 | tf_op jit(solution)/shard_map/ppermute | solution.py:504
  24.0 4.3 %collective-permute-start.9 = (bf16[248,128]{1,0:T(8,128)(2,1)S(1)}, bf16[248,128]{1,0:T(8,128)(2,1)S(1)}, u32[]{:S(2)}, u32[]{:S(2)}) collective-permute-start(bf16[248,128]{1,0:T(8,128)(2,1)S(1)} %get-tuple-element.54), channel_id=1, source_target_pairs={{0,2},{1,3},{2,0},{3,1},{4,6},{5,7},{6,4},{7,5},{8,10},{9,11},{10,... | collective-permute-start | bytes 190472 | tf_op jit(solution)/shard_map/ppermute | solution.py:514
  28.4 5.2 %collective-permute-start.12 = (bf16[248,128]{1,0:T(8,128)(2,1)S(1)}, bf16[248,128]{1,0:T(8,128)(2,1)S(1)}, u32[]{:S(2)}, u32[]{:S(2)}) collective-permute-start(bf16[248,128]{1,0:T(8,128)(2,1)S(1)} %depth_sum.1.total_ref.refs_0_), channel_id=1, source_target_pairs={{0,24},{8,16},{16,8},{24,0},{1,25},{9,17},{17,9},{25,1},{2,26},{10... | collective-permute-start | bytes 190472 | tf_op jit(solution)/shard_map/ppermute | solution.py:544
  29.9 4.3 %collective-permute-start.11 = (bf16[248,128]{1,0:T(8,128)(2,1)S(1)}, bf16[248,128]{1,0:T(8,128)(2,1)S(1)}, u32[]{:S(2)}, u32[]{:S(2)}) collective-permute-start(bf16[248,128]{1,0:T(8,128)(2,1)S(1)} %depth_sum.1.total_ref.refs_0_), channel_id=1, source_target_pairs={{0,16},{8,24},{16,0},{24,8},{1,17},{9,25},{17,1},{25,9},{2,18},{10... | collective-permute-start | bytes 190472 | tf_op jit(solution)/shard_map/ppermute | solution.py:544
  31.0 4.2 %collective-permute-start.10 = (bf16[248,128]{1,0:T(8,128)(2,1)S(1)}, bf16[248,128]{1,0:T(8,128)(2,1)S(1)}, u32[]{:S(2)}, u32[]{:S(2)}) collective-permute-start(bf16[248,128]{1,0:T(8,128)(2,1)S(1)} %depth_sum.1.total_ref.refs_0_), channel_id=1, source_target_pairs={{0,8},{8,0},{16,24},{24,16},{1,9},{9,1},{17,25},{25,17},{2,10},{10... | collective-permute-start | bytes 190472 | tf_op jit(solution)/shard_map/ppermute | solution.py:544

commit v7 on v6

--- a/solution.py
+++ b/solution.py
@@ -274,7 +274,8 @@
     )
 
 
-def pair_kernel(keep_ref, got_ref, *refs):
+def pair_kernel(keep_ref, got_ref, first_ref, passed_ref, *refs):
+    passed_ref[...] = first_ref[...]
     low, high = sample_bits()
     half, side = refs[1].shape[:2]
     rows = keep_ref.shape[0] // (2 * half)
@@ -458,7 +459,6 @@
         name="halo_and_sent_half",
     )(above, order, wide, even_band, odd_band, preact, cot)
     got = lax.ppermute(send, "space", in_chip)
-    below = lax.ppermute(first, "space", back)
     keep = pl.pallas_call(
         keep_kernel,
         out_shape=shape(terms, F32),
@@ -475,14 +475,15 @@
         shape((half, side, 128), BF16),
         shape((half, side, 128), BF16),
     )
-    early_mine, early_low, early_high, later_mine, later_low, later_high = pl.pallas_call(
+    first, early_mine, early_low, early_high, later_mine, later_low, later_high = pl.pallas_call(
         pair_kernel,
-        out_shape=batch * 2,
-        in_specs=[vmem] * 2,
-        out_specs=(vmem,) * 6,
+        out_shape=(shape(first.shape, BF16),) + batch * 2,
+        in_specs=[vmem] * 3,
+        out_specs=(vmem,) * 7,
         compiler_params=params,
         name="pair_sum",
-    )(keep, got)
+    )(keep, got, first)
+    below = lax.ppermute(first, "space", back)
 
     def crossed(low_half, high_half):
         return (

time: 36.3 us -> 36.6 us (level)
  waiting for transfers between devices: 7.39 us -> 8 us
  starting transfers between devices: 14.3 us -> 13.9 us
    ppermute x1, waiting for transfers between devices: 0.01 us -> 0.69 us  [per_device(): got = lax.ppermute(send, 'space', in_chip)]
  transfers between devices with their start and end apart: 13 -> 13, of which waited for: 6 -> 7; matrix products, arithmetic and copies ran while one was open for 0% -> 0% of each run, Pallas kernels for 27% -> 26%
where the time goes in v7:
time: 36.6 us; the launch traced here: 36.4 us
  starting transfers between devices  13.9 us (38%)
  Pallas kernels  13.8 us (38%)
  waiting for transfers between devices  8 us (22%)
  between operations  0.74 us (2%)
    pallas_call x1, Pallas kernels, per_device(): pl.pallas_call(own_kernel, out_shape=(shape((count, TAPS * SPAN), BF16),...  3.69 us
    ppermute x1, waiting for transfers between devices, per_device(): above = lax.ppermute(edge, 'space', onward)  3.68 us
    ppermute x3, starting transfers between devices, per_device(): lax.ppermute(total, 'sample', flipped(sample, j))  3.55 us
    pallas_call x1, Pallas kernels, per_device(): pl.pallas_call(input_kernel, out_shape=(shape(x.shape, BF16), shape((8, 1...  3.32 us
    ppermute x2, starting transfers between devices, per_device(): lax.ppermute(leaving[k - half], 'space', flipped(space, 2 * k))  2.65 us
    ppermute x1, starting transfers between devices, per_device(): below = lax.ppermute(first, 'space', back)  2.09 us
    pallas_call x1, Pallas kernels, per_device(): pl.pallas_call(halo_kernel, out_shape=(shape(cot.shape, BF16), shape((cou...  2.07 us
    ppermute x2, starting transfers between devices, crossed(): lax.ppermute(low_half, 'sample', flipped(sample, 1))  2.03 us
  transfers between devices with their start and end apart: 13, of which 7 were waited for; matrix products, arithmetic and copies ran while one was open for 0% of the time, Pallas kernels for 26%

profile of v7, /device:TPU:0, one launch (start us, length us, event | category | flops | bytes accessed | tf_op | source)
XLA Modules:
  0.0 36.4 jit_solution(2335678545485450982)
XLA Ops:
  0.6 1.1 %edge_plane.1 = (bf16[32,3072]{1,0:T(8,128)(2,1)S(1)}, bf16[384,256]{1,0:T(8,128)(2,1)S(1)}, bf16[384,384]{1,0:T(8,128)(2,1)S(1)}) custom-call(bf16[8,32,3072]{2,1,0:T(8,128)(2,1)} %bitcast.8), custom_call_target="tpu_custom_call" | custom-call | bytes 10485760 | tf_op jit(solution)/shard_map/edge_plane/pallas_call | solution.py:410
  1.7 0.5 %collective-permute-start = (bf16[32,3072]{1,0:T(8,128)(2,1)S(1)}, bf16[32,3072]{1,0:T(8,128)(2,1)S(1)}, u32[]{:S(2)}, u32[]{:S(2)}) collective-permute-start(bf16[32,3072]{1,0:T(8,128)(2,1)S(1)} %get-tuple-element.32), channel_id=1, source_target_pairs={{0,1},{1,2},{2,3},{3,4},{4,5},{5,6},{6,7},{7,0},{8,9},{9,10},{10,1... | collective-permute-start | bytes 589832 | tf_op jit(solution)/shard_map/ppermute | solution.py:424
  2.2 3.7 %own_planes.1 = (bf16[512,4608]{1,0:T(8,128)(2,1)S(1)}, bf16[3456,192]{1,0:T(8,128)(2,1)S(1)}, bf16[3456,192]{1,0:T(8,128)(2,1)S(1)}, f32[512,384]{1,0:T(8,128)S(1)}, bf16[9,288,192]{2,1,0:T(8,128)(2,1)S(1)}) custom-call(bf16[8,32,3072]{2,1,0:T(8,128)(2,1)S(1)} %bitcast.9, bf16[384,256]{1,0:T(8,128)(2,1)S(1)} %get-tuple-element.34.split_ref, ...), custom_call_target="tpu_custom_call" | custom-call | flops 1811939328 | bytes 12582912 | tf_op jit(solution)/shard_map/own_planes/pallas_call | solution.py:425
  5.9 3.7 %collective-permute-done.above_ref = bf16[32,3072]{1,0:T(8,128)(2,1)S(1)} collective-permute-done((bf16[32,3072]{1,0:T(8,128)(2,1)S(1)}, bf16[32,3072]{1,0:T(8,128)(2,1)S(1)}, u32[]{:S(2)}, u32[]{:S(2)}) %collective-permute-start) | collective-permute-done | bytes 196640 | tf_op jit(solution)/shard_map/ppermute | solution.py:424
  9.6 2.1 %halo_and_sent_half.1 = (bf16[4,16,3072]{2,1,0:T(8,128)(2,1)S(1)}, bf16[512,384]{1,0:T(8,128)(2,1)S(1)}, bf16[128,384]{1,0:T(8,128)(2,1)S(1)}, bf16[384,512]{1,0...) custom-call(bf16[32,3072]{1,0:T(8,128)(2,1)S(1)} %collective-permute-done.above_ref, ...), custom_call_target="tpu_custom_call" | custom-call | flops 905969664 | bytes 8388608 | tf_op jit(solution)/shard_map/halo_and_sent_half/pallas_call | solution.py:442
  11.7 0.1 collective-permute-start.1
  11.8 1.2 %kept_half.1.keep_ref = f32[96,2688]{1,0:T(8,128)S(1)} custom-call(bf16[384,512]{1,0:T(8,128)(2,1)S(1)} %get-tuple-element.40.turned_ref, bf16[128,1536]{1,0:T(8,128)(2,1)S(1)} %get-tuple-element.41.edge, bf16[512,4608]{1,0:T(8,128)(2,1)S(1)} %get-tuple-element.35.wide), custom_call_target="tpu_custom_call" | custom-call | flops 905969664 | bytes 8388608 | tf_op jit(solution)/shard_map/kept_half/pallas_call | solution.py:462
  13.0 0.7 %collective-permute-done.1.got_ref = bf16[96,2688]{1,0:T(8,128)(2,1)S(1)} collective-permute-done((bf16[96,2688]{1,0:T(8,128)(2,1)S(1)}, bf16[96,2688]{1,0:T(8,128)(2,1)S(1)}, u32[]{:S(2)}, u32[]{:S(2)}) %collective-permute-start.1) | collective-permute-done | bytes 516128 | tf_op jit(solution)/shard_map/ppermute | solution.py:461
  13.6 0.1 pair_sum.1
  13.8 2.1 %collective-permute-start.2 = (bf16[128,384]{1,0:T(8,128)(2,1)S(1)}, bf16[128,384]{1,0:T(8,128)(2,1)S(1)}, u32[]{:S(2)}, u32[]{:S(2)}) collective-permute-start(bf16[128,384]{1,0:T(8,128)(2,1)S(1)} %get-tuple-element.44), channel_id=1, source_target_pairs={{1,0},{2,1},{3,2},{4,3},{5,4},{6,5},{7,6},{0,7},{9,8},{10,9},{11,1... | collective-permute-start | bytes 294920 | tf_op jit(solution)/shard_map/ppermute | solution.py:486
  15.9 1.5 %collective-permute-start.3 = (bf16[2,120,128]{2,1,0:T(8,128)(2,1)S(1)}, bf16[2,120,128]{2,1,0:T(8,128)(2,1)S(1)}, u32[]{:S(2)}, u32[]{:S(2)}) collective-permute-start(bf16[2,120,128]{2,1,0:T(8,128)(2,1)S(1)} %get-tuple-element.48), channel_id=1, source_target_pairs={{0,8},{8,0},{16,24},{24,16},{1,9},{9,1},{17,25},{25,17},{2,10},{10... | collective-permute-start | bytes 184328 | tf_op jit(solution)/shard_map/ppermute | solution.py:490
  17.4 1.5 %collective-permute-start.4 = (bf16[2,120,128]{2,1,0:T(8,128)(2,1)S(1)}, bf16[2,120,128]{2,1,0:T(8,128)(2,1)S(1)}, u32[]{:S(2)}, u32[]{:S(2)}) collective-permute-start(bf16[2,120,128]{2,1,0:T(8,128)(2,1)S(1)} %get-tuple-element.49), channel_id=1, source_target_pairs={{0,16},{8,24},{16,0},{24,8},{1,17},{9,25},{17,1},{25,9},{2,18},{10... | collective-permute-start | bytes 184328 | tf_op jit(solution)/shard_map/ppermute | solution.py:491
  18.9 0.5 %collective-permute-start.5 = (bf16[2,120,128]{2,1,0:T(8,128)(2,1)S(1)}, bf16[2,120,128]{2,1,0:T(8,128)(2,1)S(1)}, u32[]{:S(2)}, u32[]{:S(2)}) collective-permute-start(bf16[2,120,128]{2,1,0:T(8,128)(2,1)S(1)} %get-tuple-element.53), channel_id=1, source_target_pairs={{0,8},{8,0},{16,24},{24,16},{1,9},{9,1},{17,25},{25,17},{2,10},{10... | collective-permute-start | bytes 184328 | tf_op jit(solution)/shard_map/ppermute | solution.py:490
  19.4 0.5 %collective-permute-start.6 = (bf16[2,120,128]{2,1,0:T(8,128)(2,1)S(1)}, bf16[2,120,128]{2,1,0:T(8,128)(2,1)S(1)}, u32[]{:S(2)}, u32[]{:S(2)}) collective-permute-start(bf16[2,120,128]{2,1,0:T(8,128)(2,1)S(1)} %get-tuple-element.54), channel_id=1, source_target_pairs={{0,16},{8,24},{16,0},{24,8},{1,17},{9,25},{17,1},{25,9},{2,18},{10... | collective-permute-start | bytes 184328 | tf_op jit(solution)/shard_map/ppermute | solution.py:491
  19.9 0.5 %collective-permute-done.3.low_ref = bf16[2,120,128]{2,1,0:T(8,128)(2,1)S(1)} collective-permute-done((bf16[2,120,128]{2,1,0:T(8,128)(2,1)S(1)}, bf16[2,120,128]{2,1,0:T(8,128)(2,1)S(1)}, u32[]{:S(2)}, u32[]{:S(2)}) %collective-permute-start.3) | collective-permute-done | bytes 61472 | tf_op jit(solution)/shard_map/ppermute | solution.py:490
  20.4 1.2 %collective-permute-done.4.high_ref = bf16[2,120,128]{2,1,0:T(8,128)(2,1)S(1)} collective-permute-done((bf16[2,120,128]{2,1,0:T(8,128)(2,1)S(1)}, bf16[2,120,128]{2,1,0:T(8,128)(2,1)S(1)}, u32[]{:S(2)}, u32[]{:S(2)}) %collective-permute-start.4) | collective-permute-done | bytes 61472 | tf_op jit(solution)/shard_map/ppermute | solution.py:491
  21.6 0.1 collective-permute-start.7
  21.7 2.6 %collective-permute-start.8 = (bf16[248,128]{1,0:T(8,128)(2,1)S(1)}, bf16[248,128]{1,0:T(8,128)(2,1)S(1)}, u32[]{:S(2)}, u32[]{:S(2)}) collective-permute-start(bf16[248,128]{1,0:T(8,128)(2,1)S(1)} %get-tuple-element.51.refs_1_), channel_id=1, source_target_pairs={{0,6},{1,7},{2,4},{3,5},{4,2},{5,3},{6,0},{7,1},{8,14},{9,15},{10,... | collective-permute-start | bytes 190472 | tf_op jit(solution)/shard_map/ppermute | solution.py:505
  24.3 0.0 collective-permute-done.6.refs_4_
  24.3 1.0 %collective-permute-start.9 = (bf16[248,128]{1,0:T(8,128)(2,1)S(1)}, bf16[248,128]{1,0:T(8,128)(2,1)S(1)}, u32[]{:S(2)}, u32[]{:S(2)}) collective-permute-start(bf16[248,128]{1,0:T(8,128)(2,1)S(1)} %get-tuple-element.56), channel_id=1, source_target_pairs={{0,2},{1,3},{2,0},{3,1},{4,6},{5,7},{6,4},{7,5},{8,10},{9,11},{10,... | collective-permute-start | bytes 190472 | tf_op jit(solution)/shard_map/ppermute | solution.py:515
  25.3 3.3 %input_grad.1 = (bf16[8,32,3072]{2,1,0:T(8,128)(2,1)S(1)}, f32[8,128]{1,0:T(8,128)S(1)}) custom-call(bf16[512,384]{1,0:T(8,128)(2,1)S(1)} %get-tuple-element.39.gp_ref, bf16[128,384]{1,0:T(8,128)(2,1)S(1)} %collective-permute-done.2.below_ref, bf16[9,288,192]{2,1,0:T(8,128)(2,1)S(1)} %get-tuple-element.45.w_ref), custom_call_target="tpu_custom_call" | custom-call | flops 1811939328 | bytes 8388608 | tf_op jit(solution)/shard_map/input_grad/pallas_call | solution.py:517
  28.6 0.0 collective-permute-done.9.refs_2_
  28.6 0.0 collective-permute-done.7.refs_0_
  28.6 0.0 collective-permute-done.8.refs_1_
  28.7 1.6 %collective-permute-start.12 = (bf16[248,128]{1,0:T(8,128)(2,1)S(1)}, bf16[248,128]{1,0:T(8,128)(2,1)S(1)}, u32[]{:S(2)}, u32[]{:S(2)}) collective-permute-start(bf16[248,128]{1,0:T(8,128)(2,1)S(1)} %depth_sum.1.total_ref.refs_0_), channel_id=1, source_target_pairs={{0,24},{8,16},{16,8},{24,0},{1,25},{9,17},{17,9},{25,1},{2,26},{10... | collective-permute-start | bytes 190472 | tf_op jit(solution)/shard_map/ppermute | solution.py:545
  30.3 1.0 %collective-permute-start.11 = (bf16[248,128]{1,0:T(8,128)(2,1)S(1)}, bf16[248,128]{1,0:T(8,128)(2,1)S(1)}, u32[]{:S(2)}, u32[]{:S(2)}) collective-permute-start(bf16[248,128]{1,0:T(8,128)(2,1)S(1)} %depth_sum.1.total_ref.refs_0_), channel_id=1, source_target_pairs={{0,16},{8,24},{16,0},{24,8},{1,17},{9,25},{17,1},{25,9},{2,18},{10... | collective-permute-start | bytes 190472 | tf_op jit(solution)/shard_map/ppermute | solution.py:545
  31.3 1.0 %collective-permute-start.10 = (bf16[248,128]{1,0:T(8,128)(2,1)S(1)}, bf16[248,128]{1,0:T(8,128)(2,1)S(1)}, u32[]{:S(2)}, u32[]{:S(2)}) collective-permute-start(bf16[248,128]{1,0:T(8,128)(2,1)S(1)} %depth_sum.1.total_ref.refs_0_), channel_id=1, source_target_pairs={{0,8},{8,0},{16,24},{24,16},{1,9},{9,1},{17,25},{25,17},{2,10},{10... | collective-permute-start | bytes 190472 | tf_op jit(solution)/shard_map/ppermute | solution.py:545
  32.3 1.3 %store.1 = (bf16[4,16,3072]{2,1,0:T(8,128)(2,1)}, bf16[8,32,3072]{2,1,0:T(8,128)(2,1)}) custom-call(bf16[248,128]{1,0:T(8,128)(2,1)S(1)} %depth_sum.1.total_ref.refs_0_, bf16[4,16,3072]{2,1,0:T(8,128)(2,1)S(1)} %get-tuple-element.57.refs_0_, bf16[8,32,3072]{2,1,0:T(8,128)(2,1)S(1)} %get-tuple-element.58.refs_1_), custom_call_target="tpu_custom_call" | custom-call | tf_op jit(solution)/shard_map/store/pallas_call | solution.py:536
  33.6 0.4 collective-permute-done.12.refs_3_
  33.9 0.7 %collective-permute-done.11.refs_2_ = bf16[248,128]{1,0:T(8,128)(2,1)S(1)} collective-permute-done((bf16[248,128]{1,0:T(8,128)(2,1)S(1)}, bf16[248,128]{1,0:T(8,128)(2,1)S(1)}, u32[]{:S(2)}, u32[]{:S(2)}) %collective-permute-start.11) | collective-permute-done | bytes 63520 | tf_op jit(solution)/shard_map/ppermute | solution.py:545
  34.6 0.9 %collective-permute-done.10.refs_1_ = bf16[248,128]{1,0:T(8,128)(2,1)S(1)} collective-permute-done((bf16[248,128]{1,0:T(8,128)(2,1)S(1)}, bf16[248,128]{1,0:T(8,128)(2,1)S(1)}, u32[]{:S(2)}, u32[]{:S(2)}) %collective-permute-start.10) | collective-permute-done | bytes 63520 | tf_op jit(solution)/shard_map/ppermute | solution.py:545
  35.5 0.9 %sample_sum.1 = f32[27,24,96]{2,1,0:T(8,128)} custom-call(bf16[248,128]{1,0:T(8,128)(2,1)S(1)} %depth_sum.1.total_ref.refs_0_, bf16[248,128]{1,0:T(8,128)(2,1)S(1)} %collective-permute-done.10.refs_1_, bf16[248,128]{1,0:T(8,128)(2,1)S(1)} %collective-permute-done.11.refs_2_, bf16[248,128]{1,0:T(8,128)(2,1)S(1)} %collective-permute-done.12.refs_3_), custom_call_target="tpu_custom_call" | custom-call | tf_op jit(solution)/shard_map/sample_sum/pallas_call | solution.py:546
  (9 shorter events, 0.1 us)
Async XLA Ops:
  0.6 1.6 %copy-start = (bf16[1,8,32,3072]{3,2,1,0:T(8,128)(2,1)S(1)}, bf16[1,8,32,3072]{3,2,1,0:T(8,128)(2,1)}, u32[]{:S(2)}) copy-start(bf16[1,8,32,3072]{3,2,1,0:T(8,128)(2,1)} %param.3) | copy-start | bytes 4718596
  1.7 7.9 %collective-permute-start = (bf16[32,3072]{1,0:T(8,128)(2,1)S(1)}, bf16[32,3072]{1,0:T(8,128)(2,1)S(1)}, u32[]{:S(2)}, u32[]{:S(2)}) collective-permute-start(bf16[32,3072]{1,0:T(8,128)(2,1)S(1)} %get-tuple-element.32), channel_id=1, source_target_pairs={{0,1},{1,2},{2,3},{3,4},{4,5},{5,6},{6,7},{7,0},{8,9},{9,10},{10,1... | collective-permute-start | bytes 589832 | tf_op jit(solution)/shard_map/ppermute | solution.py:424
  2.2 7.4 %copy-start.1 = (bf16[1,4,16,3072]{3,2,1,0:T(8,128)(2,1)S(1)}, bf16[1,4,16,3072]{3,2,1,0:T(8,128)(2,1)}, u32[]{:S(2)}) copy-start(bf16[1,4,16,3072]{3,2,1,0:T(8,128)(2,1)} %param.5) | copy-start | bytes 1179652
  11.7 2.0 %collective-permute-start.1 = (bf16[96,2688]{1,0:T(8,128)(2,1)S(1)}, bf16[96,2688]{1,0:T(8,128)(2,1)S(1)}, u32[]{:S(2)}, u32[]{:S(2)}) collective-permute-start(bf16[96,2688]{1,0:T(8,128)(2,1)S(1)} %get-tuple-element.42), channel_id=1, source_target_pairs={{0,1},{1,0},{2,3},{3,2},{4,5},{5,4},{6,7},{7,6},{8,9},{9,8},{10,11... | collective-permute-start | bytes 1548296 | tf_op jit(solution)/shard_map/ppermute | solution.py:461
  13.8 11.5 %collective-permute-start.2 = (bf16[128,384]{1,0:T(8,128)(2,1)S(1)}, bf16[128,384]{1,0:T(8,128)(2,1)S(1)}, u32[]{:S(2)}, u32[]{:S(2)}) collective-permute-start(bf16[128,384]{1,0:T(8,128)(2,1)S(1)} %get-tuple-element.44), channel_id=1, source_target_pairs={{1,0},{2,1},{3,2},{4,3},{5,4},{6,5},{7,6},{0,7},{9,8},{10,9},{11,1... | collective-permute-start | bytes 294920 | tf_op jit(solution)/shard_map/ppermute | solution.py:486
  15.9 4.5 %collective-permute-start.3 = (bf16[2,120,128]{2,1,0:T(8,128)(2,1)S(1)}, bf16[2,120,128]{2,1,0:T(8,128)(2,1)S(1)}, u32[]{:S(2)}, u32[]{:S(2)}) collective-permute-start(bf16[2,120,128]{2,1,0:T(8,128)(2,1)S(1)} %get-tuple-element.48), channel_id=1, source_target_pairs={{0,8},{8,0},{16,24},{24,16},{1,9},{9,1},{17,25},{25,17},{2,10},{10... | collective-permute-start | bytes 184328 | tf_op jit(solution)/shard_map/ppermute | solution.py:490
  17.4 4.2 %collective-permute-start.4 = (bf16[2,120,128]{2,1,0:T(8,128)(2,1)S(1)}, bf16[2,120,128]{2,1,0:T(8,128)(2,1)S(1)}, u32[]{:S(2)}, u32[]{:S(2)}) collective-permute-start(bf16[2,120,128]{2,1,0:T(8,128)(2,1)S(1)} %get-tuple-element.49), channel_id=1, source_target_pairs={{0,16},{8,24},{16,0},{24,8},{1,17},{9,25},{17,1},{25,9},{2,18},{10... | collective-permute-start | bytes 184328 | tf_op jit(solution)/shard_map/ppermute | solution.py:491
  18.9 5.4 %collective-permute-start.5 = (bf16[2,120,128]{2,1,0:T(8,128)(2,1)S(1)}, bf16[2,120,128]{2,1,0:T(8,128)(2,1)S(1)}, u32[]{:S(2)}, u32[]{:S(2)}) collective-permute-start(bf16[2,120,128]{2,1,0:T(8,128)(2,1)S(1)} %get-tuple-element.53), channel_id=1, source_target_pairs={{0,8},{8,0},{16,24},{24,16},{1,9},{9,1},{17,25},{25,17},{2,10},{10... | collective-permute-start | bytes 184328 | tf_op jit(solution)/shard_map/ppermute | solution.py:490
  19.4 4.9 %collective-permute-start.6 = (bf16[2,120,128]{2,1,0:T(8,128)(2,1)S(1)}, bf16[2,120,128]{2,1,0:T(8,128)(2,1)S(1)}, u32[]{:S(2)}, u32[]{:S(2)}) collective-permute-start(bf16[2,120,128]{2,1,0:T(8,128)(2,1)S(1)} %get-tuple-element.54), channel_id=1, source_target_pairs={{0,16},{8,24},{16,0},{24,8},{1,17},{9,25},{17,1},{25,9},{2,18},{10... | collective-permute-start | bytes 184328 | tf_op jit(solution)/shard_map/ppermute | solution.py:491
  21.6 7.0 %collective-permute-start.7 = (bf16[248,128]{1,0:T(8,128)(2,1)S(1)}, bf16[248,128]{1,0:T(8,128)(2,1)S(1)}, u32[]{:S(2)}, u32[]{:S(2)}) collective-permute-start(bf16[248,128]{1,0:T(8,128)(2,1)S(1)} %get-tuple-element.50.refs_0_), channel_id=1, source_target_pairs={{0,4},{1,5},{2,6},{3,7},{4,0},{5,1},{6,2},{7,3},{8,12},{9,13},{10,... | collective-permute-start | bytes 190472 | tf_op jit(solution)/shard_map/ppermute | solution.py:505
  21.7 6.9 %collective-permute-start.8 = (bf16[248,128]{1,0:T(8,128)(2,1)S(1)}, bf16[248,128]{1,0:T(8,128)(2,1)S(1)}, u32[]{:S(2)}, u32[]{:S(2)}) collective-permute-start(bf16[248,128]{1,0:T(8,128)(2,1)S(1)} %get-tuple-element.51.refs_1_), channel_id=1, source_target_pairs={{0,6},{1,7},{2,4},{3,5},{4,2},{5,3},{6,0},{7,1},{8,14},{9,15},{10,... | collective-permute-start | bytes 190472 | tf_op jit(solution)/shard_map/ppermute | solution.py:505
  24.3 4.3 %collective-permute-start.9 = (bf16[248,128]{1,0:T(8,128)(2,1)S(1)}, bf16[248,128]{1,0:T(8,128)(2,1)S(1)}, u32[]{:S(2)}, u32[]{:S(2)}) collective-permute-start(bf16[248,128]{1,0:T(8,128)(2,1)S(1)} %get-tuple-element.56), channel_id=1, source_target_pairs={{0,2},{1,3},{2,0},{3,1},{4,6},{5,7},{6,4},{7,5},{8,10},{9,11},{10,... | collective-permute-start | bytes 190472 | tf_op jit(solution)/shard_map/ppermute | solution.py:515
  28.7 5.2 %collective-permute-start.12 = (bf16[248,128]{1,0:T(8,128)(2,1)S(1)}, bf16[248,128]{1,0:T(8,128)(2,1)S(1)}, u32[]{:S(2)}, u32[]{:S(2)}) collective-permute-start(bf16[248,128]{1,0:T(8,128)(2,1)S(1)} %depth_sum.1.total_ref.refs_0_), channel_id=1, source_target_pairs={{0,24},{8,16},{16,8},{24,0},{1,25},{9,17},{17,9},{25,1},{2,26},{10... | collective-permute-start | bytes 190472 | tf_op jit(solution)/shard_map/ppermute | solution.py:545
  30.3 4.3 %collective-permute-start.11 = (bf16[248,128]{1,0:T(8,128)(2,1)S(1)}, bf16[248,128]{1,0:T(8,128)(2,1)S(1)}, u32[]{:S(2)}, u32[]{:S(2)}) collective-permute-start(bf16[248,128]{1,0:T(8,128)(2,1)S(1)} %depth_sum.1.total_ref.refs_0_), channel_id=1, source_target_pairs={{0,16},{8,24},{16,0},{24,8},{1,17},{9,25},{17,1},{25,9},{2,18},{10... | collective-permute-start | bytes 190472 | tf_op jit(solution)/shard_map/ppermute | solution.py:545
  31.3 4.2 %collective-permute-start.10 = (bf16[248,128]{1,0:T(8,128)(2,1)S(1)}, bf16[248,128]{1,0:T(8,128)(2,1)S(1)}, u32[]{:S(2)}, u32[]{:S(2)}) collective-permute-start(bf16[248,128]{1,0:T(8,128)(2,1)S(1)} %depth_sum.1.total_ref.refs_0_), channel_id=1, source_target_pairs={{0,8},{8,0},{16,24},{24,16},{1,9},{9,1},{17,25},{25,17},{2,10},{10... | collective-permute-start | bytes 190472 | tf_op jit(solution)/shard_map/ppermute | solution.py:545

commit v8 on v5

--- a/solution.py
+++ b/solution.py
@@ -57,10 +57,14 @@
         wide[at : at + 16, tap * SPAN : tap * SPAN + 128] = jnp.zeros((16, 128), BF16)
 
 
-def edge_kernel(width, x_hbm, edge_ref, split_ref, order_ref, sem):
+def edge_kernel(x_hbm, edge_ref, split_ref, sem):
     copy = pltpu.make_async_copy(x_hbm.at[x_hbm.shape[0] - 1], edge_ref, sem)
     copy.start()
     split_ref[...] = row_split(x_hbm.shape[0])
+    copy.wait()
+
+
+def fill_order(order_ref, width):
     at = lax.axis_index("space")
     core = at % 2
     chip = at // 2
@@ -81,7 +85,6 @@
         if high != width:
             source = jnp.where((channel >= width) & (channel < high), -1, source)
     order_ref[...] = jnp.where(iota(shape, 1) == source, 1.0, 0.0).astype(BF16)
-    copy.wait()
 
 
 def by_parity(wide, even_band, odd_band, taps):
@@ -92,13 +95,16 @@
     return sides
 
 
-def own_kernel(x_ref, split_ref, w_hbm, wide, even_band, odd_band, preact, w_ref, sem):
+def own_kernel(
+    width, x_ref, split_ref, w_hbm, wide, even_band, odd_band, preact, w_ref, order_ref, sem
+):
     planes = x_ref.shape[0]
     outs = planes // 2
     cells = x_ref.shape[2] // BLOCK
     per_out = cells * 16
     copy = pltpu.make_async_copy(w_hbm, w_ref, sem)
     copy.start()
+    fill_order(order_ref, width)
     split = split_ref[...]
     wide[0:per_out, 0 : 3 * SPAN] = jnp.zeros((per_out, 3 * SPAN), BF16)
     x = x_ref[...].reshape(planes * 32, x_ref.shape[2])
@@ -400,32 +406,32 @@
     shape = jax.ShapeDtypeStruct
     flops = 2 * count * TAPS * SPAN * BLOCK
 
-    edge, split, order = pl.pallas_call(
-        functools.partial(edge_kernel, width),
+    edge, split = pl.pallas_call(
+        edge_kernel,
         out_shape=(
             shape((rows, lanes), BF16),
             shape((3 * planes * 16, planes * 32), BF16),
-            shape((4 * kept_rows, 2 * COUT), BF16),
         ),
         in_specs=[hbm],
-        out_specs=(vmem,) * 3,
+        out_specs=(vmem,) * 2,
         scratch_shapes=[pltpu.SemaphoreType.DMA(())],
         compiler_params=params,
         cost_estimate=pl.CostEstimate(flops=0, bytes_accessed=10 << 20, transcendentals=0),
         name="edge_plane",
     )(pltpu.with_memory_space_constraint(x, pltpu.HBM))
     above = lax.ppermute(edge, "space", onward)
-    wide, even_band, odd_band, preact, w_in = pl.pallas_call(
-        own_kernel,
+    wide, even_band, odd_band, preact, w_in, order = pl.pallas_call(
+        functools.partial(own_kernel, width),
         out_shape=(
             shape((count, TAPS * SPAN), BF16),
             shape((TAPS * BLOCK, COUT), BF16),
             shape((TAPS * BLOCK, COUT), BF16),
             shape((count, BLOCK), F32),
             shape(w.shape, BF16),
+            shape((4 * kept_rows, 2 * COUT), BF16),
         ),
         in_specs=[vmem, vmem, hbm],
-        out_specs=(vmem,) * 5,
+        out_specs=(vmem,) * 6,
         scratch_shapes=[pltpu.SemaphoreType.DMA(())],
         compiler_params=params,
         cost_estimate=pl.CostEstimate(flops=flops, bytes_accessed=12 << 20, transcendentals=0),

time: 36.1 us -> 36.1 us (level)
  no operation moved by 1% of the time
where the time goes in v8:
time: 36.1 us; the launch traced here: 35.9 us
  Pallas kernels  13.8 us (38%)
  starting transfers between devices  12.2 us (34%)
  waiting for transfers between devices  9.18 us (25%)
  between operations  0.72 us (2%)
    pallas_call x1, Pallas kernels, per_device(): pl.pallas_call(functools.partial(own_kernel, width), out_shape=(shape((co...  3.69 us
    ppermute x1, waiting for transfers between devices, per_device(): above = lax.ppermute(edge, 'space', onward)  3.68 us
    ppermute x3, starting transfers between devices, per_device(): lax.ppermute(leaving[k - 1], 'space', flipped(space, 2 * k))  3.55 us
    ppermute x3, starting transfers between devices, per_device(): lax.ppermute(total, 'sample', flipped(sample, j))  3.55 us
    pallas_call x1, Pallas kernels, per_device(): pl.pallas_call(input_kernel, out_shape=(shape(x.shape, BF16), shape((8, 1...  3.32 us
    pallas_call x1, Pallas kernels, per_device(): pl.pallas_call(halo_kernel, out_shape=(shape(cot.shape, BF16), shape((cou...  2.08 us
    ppermute x1, starting transfers between devices, per_device(): low = lax.ppermute(low, 'sample', flipped(sample, 1))  2.05 us
    ppermute x1, starting transfers between devices, per_device(): lax.ppermute(high_lanes, 'sample', flipped(sample, sample // 2))  1.52 us
  transfers between devices with their start and end apart: 11, of which 9 were waited for; matrix products, arithmetic and copies ran while one was open for 0% of the time, Pallas kernels for 27%

profile of v8, /device:TPU:0, one launch (start us, length us, event | category | flops | bytes accessed | tf_op | source)
XLA Modules:
  0.0 35.9 jit_solution(10858204634822203105)
XLA Ops:
  0.6 0.0 copy-start
  0.6 1.1 %edge_plane.1 = (bf16[32,3072]{1,0:T(8,128)(2,1)S(1)}, bf16[384,256]{1,0:T(8,128)(2,1)S(1)}) custom-call(bf16[8,32,3072]{2,1,0:T(8,128)(2,1)} %bitcast.8), custom_call_target="tpu_custom_call" | custom-call | bytes 10485760 | tf_op jit(solution)/shard_map/edge_plane/pallas_call | solution.py:409
  1.7 0.5 %collective-permute-start = (bf16[32,3072]{1,0:T(8,128)(2,1)S(1)}, bf16[32,3072]{1,0:T(8,128)(2,1)S(1)}, u32[]{:S(2)}, u32[]{:S(2)}) collective-permute-start(bf16[32,3072]{1,0:T(8,128)(2,1)S(1)} %get-tuple-element.28), channel_id=1, source_target_pairs={{0,1},{1,2},{2,3},{3,4},{4,5},{5,6},{6,7},{7,0},{8,9},{9,10},{10,1... | collective-permute-start | bytes 589832 | tf_op jit(solution)/shard_map/ppermute | solution.py:422
  2.2 3.7 %own_planes.1 = (bf16[512,4608]{1,0:T(8,128)(2,1)S(1)}, bf16[3456,192]{1,0:T(8,128)(2,1)S(1)}, bf16[3456,192]{1,0:T(8,128)(2,1)S(1)}, f32[512,384]{1,0:T(8,128)S...) custom-call(bf16[8,32,3072]{2,1,0:T(8,128)(2,1)S(1)} %bitcast.9, ...), custom_call_target="tpu_custom_call" | custom-call | flops 1811939328 | bytes 12582912 | tf_op jit(solution)/shard_map/own_planes/pallas_call | solution.py:423
  5.9 3.7 %collective-permute-done.above_ref = bf16[32,3072]{1,0:T(8,128)(2,1)S(1)} collective-permute-done((bf16[32,3072]{1,0:T(8,128)(2,1)S(1)}, bf16[32,3072]{1,0:T(8,128)(2,1)S(1)}, u32[]{:S(2)}, u32[]{:S(2)}) %collective-permute-start) | collective-permute-done | bytes 196640 | tf_op jit(solution)/shard_map/ppermute | solution.py:422
  9.6 2.1 %halo_and_sent_half.1 = (bf16[4,16,3072]{2,1,0:T(8,128)(2,1)S(1)}, bf16[512,384]{1,0:T(8,128)(2,1)S(1)}, bf16[128,384]{1,0:T(8,128)(2,1)S(1)}, bf16[384,512]{1,0...) custom-call(bf16[32,3072]{1,0:T(8,128)(2,1)S(1)} %collective-permute-done.above_ref, ...), custom_call_target="tpu_custom_call" | custom-call | flops 905969664 | bytes 8388608 | tf_op jit(solution)/shard_map/halo_and_sent_half/pallas_call | solution.py:441
  11.7 0.1 collective-permute-start.2
  11.8 1.2 %kept_half.1.keep_ref = f32[96,2688]{1,0:T(8,128)S(1)} custom-call(bf16[384,512]{1,0:T(8,128)(2,1)S(1)} %get-tuple-element.39.turned_ref, bf16[128,1536]{1,0:T(8,128)(2,1)S(1)} %get-tuple-element.40.edge, bf16[512,4608]{1,0:T(8,128)(2,1)S(1)} %get-tuple-element.31.wide), custom_call_target="tpu_custom_call" | custom-call | flops 905969664 | bytes 8388608 | tf_op jit(solution)/shard_map/kept_half/pallas_call | solution.py:462
  13.0 0.7 %collective-permute-done.2.got_ref = bf16[96,2688]{1,0:T(8,128)(2,1)S(1)} collective-permute-done((bf16[96,2688]{1,0:T(8,128)(2,1)S(1)}, bf16[96,2688]{1,0:T(8,128)(2,1)S(1)}, u32[]{:S(2)}, u32[]{:S(2)}) %collective-permute-start.2) | collective-permute-done | bytes 516128 | tf_op jit(solution)/shard_map/ppermute | solution.py:460
  13.6 0.1 pair_sum.1
  13.8 2.1 %collective-permute-start.3 = (bf16[4,120,128]{2,1,0:T(8,128)(2,1)S(1)}, bf16[4,120,128]{2,1,0:T(8,128)(2,1)S(1)}, u32[]{:S(2)}, u32[]{:S(2)}) collective-permute-start(bf16[4,120,128]{2,1,0:T(8,128)(2,1)S(1)} %get-tuple-element.43), channel_id=1, source_target_pairs={{0,8},{8,0},{16,24},{24,16},{1,9},{9,1},{17,25},{25,17},{2,10},{10... | collective-permute-start | bytes 368648 | tf_op jit(solution)/shard_map/ppermute | solution.py:484
  15.8 1.5 %collective-permute-start.4 = (bf16[4,120,128]{2,1,0:T(8,128)(2,1)S(1)}, bf16[4,120,128]{2,1,0:T(8,128)(2,1)S(1)}, u32[]{:S(2)}, u32[]{:S(2)}) collective-permute-start(bf16[4,120,128]{2,1,0:T(8,128)(2,1)S(1)} %get-tuple-element.44), channel_id=1, source_target_pairs={{0,16},{8,24},{16,0},{24,8},{1,17},{9,25},{17,1},{25,9},{2,18},{10... | collective-permute-start | bytes 368648 | tf_op jit(solution)/shard_map/ppermute | solution.py:485
  17.4 1.0 %collective-permute-start.1 = (bf16[128,384]{1,0:T(8,128)(2,1)S(1)}, bf16[128,384]{1,0:T(8,128)(2,1)S(1)}, u32[]{:S(2)}, u32[]{:S(2)}) collective-permute-start(bf16[128,384]{1,0:T(8,128)(2,1)S(1)} %get-tuple-element.36), channel_id=1, source_target_pairs={{1,0},{2,1},{3,2},{4,3},{5,4},{6,5},{7,6},{0,7},{9,8},{10,9},{11,1... | collective-permute-start | bytes 294920 | tf_op jit(solution)/shard_map/ppermute | solution.py:461
  18.3 1.1 %collective-permute-done.3.low_ref = bf16[4,120,128]{2,1,0:T(8,128)(2,1)S(1)} collective-permute-done((bf16[4,120,128]{2,1,0:T(8,128)(2,1)S(1)}, bf16[4,120,128]{2,1,0:T(8,128)(2,1)S(1)}, u32[]{:S(2)}, u32[]{:S(2)}) %collective-permute-start.3) | collective-permute-done | bytes 122912 | tf_op jit(solution)/shard_map/ppermute | solution.py:484
  19.5 1.5 %collective-permute-done.4.high_ref = bf16[4,120,128]{2,1,0:T(8,128)(2,1)S(1)} collective-permute-done((bf16[4,120,128]{2,1,0:T(8,128)(2,1)S(1)}, bf16[4,120,128]{2,1,0:T(8,128)(2,1)S(1)}, u32[]{:S(2)}, u32[]{:S(2)}) %collective-permute-start.4) | collective-permute-done | bytes 122912 | tf_op jit(solution)/shard_map/ppermute | solution.py:485
  20.9 0.1 cross_sum.1
  21.0 1.0 %collective-permute-start.5 = (bf16[248,128]{1,0:T(8,128)(2,1)S(1)}, bf16[248,128]{1,0:T(8,128)(2,1)S(1)}, u32[]{:S(2)}, u32[]{:S(2)}) collective-permute-start(bf16[248,128]{1,0:T(8,128)(2,1)S(1)} %get-tuple-element.46), channel_id=1, source_target_pairs={{0,4},{1,5},{2,6},{3,7},{4,0},{5,1},{6,2},{7,3},{8,12},{9,13},{10,... | collective-permute-start | bytes 190472 | tf_op jit(solution)/shard_map/ppermute | solution.py:495
  22.0 1.4 %collective-permute-start.6 = (bf16[248,128]{1,0:T(8,128)(2,1)S(1)}, bf16[248,128]{1,0:T(8,128)(2,1)S(1)}, u32[]{:S(2)}, u32[]{:S(2)}) collective-permute-start(bf16[248,128]{1,0:T(8,128)(2,1)S(1)} %get-tuple-element.47), channel_id=1, source_target_pairs={{0,6},{1,7},{2,4},{3,5},{4,2},{5,3},{6,0},{7,1},{8,14},{9,15},{10,... | collective-permute-start | bytes 190472 | tf_op jit(solution)/shard_map/ppermute | solution.py:495
  23.4 1.2 %collective-permute-start.7 = (bf16[248,128]{1,0:T(8,128)(2,1)S(1)}, bf16[248,128]{1,0:T(8,128)(2,1)S(1)}, u32[]{:S(2)}, u32[]{:S(2)}) collective-permute-start(bf16[248,128]{1,0:T(8,128)(2,1)S(1)} %get-tuple-element.48), channel_id=1, source_target_pairs={{0,2},{1,3},{2,0},{3,1},{4,6},{5,7},{6,4},{7,5},{8,10},{9,11},{10,... | collective-permute-start | bytes 190472 | tf_op jit(solution)/shard_map/ppermute | solution.py:495
  24.5 0.0 collective-permute-done.1.below_ref
  24.5 3.3 %input_grad.1 = (bf16[8,32,3072]{2,1,0:T(8,128)(2,1)S(1)}, f32[8,128]{1,0:T(8,128)S(1)}) custom-call(bf16[512,384]{1,0:T(8,128)(2,1)S(1)} %get-tuple-element.35.gp_ref, bf16[128,384]{1,0:T(8,128)(2,1)S(1)} %collective-permute-done.1.below_ref, bf16[9,288,192]{2,1,0:T(8,128)(2,1)S(1)} %get-tuple-element.37.w_ref), custom_call_target="tpu_custom_call" | custom-call | flops 1811939328 | bytes 8388608 | tf_op jit(solution)/shard_map/input_grad/pallas_call | solution.py:499
  27.9 0.0 collective-permute-done.5.refs_0_
  27.9 0.3 collective-permute-done.6.refs_1_
  28.2 0.4 collective-permute-done.7.refs_2_
  28.6 1.6 %collective-permute-start.10 = (bf16[248,128]{1,0:T(8,128)(2,1)S(1)}, bf16[248,128]{1,0:T(8,128)(2,1)S(1)}, u32[]{:S(2)}, u32[]{:S(2)}) collective-permute-start(bf16[248,128]{1,0:T(8,128)(2,1)S(1)} %depth_sum.1.total_ref.refs_0_), channel_id=1, source_target_pairs={{0,24},{8,16},{16,8},{24,0},{1,25},{9,17},{17,9},{25,1},{2,26},{10... | collective-permute-start | bytes 190472 | tf_op jit(solution)/shard_map/ppermute | solution.py:527
  30.2 0.5 %collective-permute-start.9 = (bf16[248,128]{1,0:T(8,128)(2,1)S(1)}, bf16[248,128]{1,0:T(8,128)(2,1)S(1)}, u32[]{:S(2)}, u32[]{:S(2)}) collective-permute-start(bf16[248,128]{1,0:T(8,128)(2,1)S(1)} %depth_sum.1.total_ref.refs_0_), channel_id=1, source_target_pairs={{0,16},{8,24},{16,0},{24,8},{1,17},{9,25},{17,1},{25,9},{2,18},{10... | collective-permute-start | bytes 190472 | tf_op jit(solution)/shard_map/ppermute | solution.py:527
  30.7 1.4 %collective-permute-start.8 = (bf16[248,128]{1,0:T(8,128)(2,1)S(1)}, bf16[248,128]{1,0:T(8,128)(2,1)S(1)}, u32[]{:S(2)}, u32[]{:S(2)}) collective-permute-start(bf16[248,128]{1,0:T(8,128)(2,1)S(1)} %depth_sum.1.total_ref.refs_0_), channel_id=1, source_target_pairs={{0,8},{8,0},{16,24},{24,16},{1,9},{9,1},{17,25},{25,17},{2,10},{10... | collective-permute-start | bytes 190472 | tf_op jit(solution)/shard_map/ppermute | solution.py:527
  32.2 1.3 %store.1 = (bf16[4,16,3072]{2,1,0:T(8,128)(2,1)}, bf16[8,32,3072]{2,1,0:T(8,128)(2,1)}) custom-call(bf16[248,128]{1,0:T(8,128)(2,1)S(1)} %depth_sum.1.total_ref.refs_0_, bf16[4,16,3072]{2,1,0:T(8,128)(2,1)S(1)} %get-tuple-element.49.refs_0_, bf16[8,32,3072]{2,1,0:T(8,128)(2,1)S(1)} %get-tuple-element.50.refs_1_), custom_call_target="tpu_custom_call" | custom-call | tf_op jit(solution)/shard_map/store/pallas_call | solution.py:518
  33.5 0.4 collective-permute-done.10.refs_3_
  33.8 0.7 %collective-permute-done.9.refs_2_ = bf16[248,128]{1,0:T(8,128)(2,1)S(1)} collective-permute-done((bf16[248,128]{1,0:T(8,128)(2,1)S(1)}, bf16[248,128]{1,0:T(8,128)(2,1)S(1)}, u32[]{:S(2)}, u32[]{:S(2)}) %collective-permute-start.9) | collective-permute-done | bytes 63520 | tf_op jit(solution)/shard_map/ppermute | solution.py:527
  34.5 0.5 %collective-permute-done.8.refs_1_ = bf16[248,128]{1,0:T(8,128)(2,1)S(1)} collective-permute-done((bf16[248,128]{1,0:T(8,128)(2,1)S(1)}, bf16[248,128]{1,0:T(8,128)(2,1)S(1)}, u32[]{:S(2)}, u32[]{:S(2)}) %collective-permute-start.8) | collective-permute-done | bytes 63520 | tf_op jit(solution)/shard_map/ppermute | solution.py:527
  35.0 0.9 %sample_sum.1 = f32[27,24,96]{2,1,0:T(8,128)} custom-call(bf16[248,128]{1,0:T(8,128)(2,1)S(1)} %depth_sum.1.total_ref.refs_0_, bf16[248,128]{1,0:T(8,128)(2,1)S(1)} %collective-permute-done.8.refs_1_, bf16[248,128]{1,0:T(8,128)(2,1)S(1)} %collective-permute-done.9.refs_2_, bf16[248,128]{1,0:T(8,128)(2,1)S(1)} %collective-permute-done.10.refs_3_), custom_call_target="tpu_custom_call" | custom-call | tf_op jit(solution)/shard_map/sample_sum/pallas_call | solution.py:528
  (4 shorter events, 0.0 us)
Async XLA Ops:
  0.6 1.6 %copy-start = (bf16[1,8,32,3072]{3,2,1,0:T(8,128)(2,1)S(1)}, bf16[1,8,32,3072]{3,2,1,0:T(8,128)(2,1)}, u32[]{:S(2)}) copy-start(bf16[1,8,32,3072]{3,2,1,0:T(8,128)(2,1)} %param.3) | copy-start | bytes 4718596
  1.7 7.9 %collective-permute-start = (bf16[32,3072]{1,0:T(8,128)(2,1)S(1)}, bf16[32,3072]{1,0:T(8,128)(2,1)S(1)}, u32[]{:S(2)}, u32[]{:S(2)}) collective-permute-start(bf16[32,3072]{1,0:T(8,128)(2,1)S(1)} %get-tuple-element.28), channel_id=1, source_target_pairs={{0,1},{1,2},{2,3},{3,4},{4,5},{5,6},{6,7},{7,0},{8,9},{9,10},{10,1... | collective-permute-start | bytes 589832 | tf_op jit(solution)/shard_map/ppermute | solution.py:422
  2.2 7.4 %copy-start.1 = (bf16[1,4,16,3072]{3,2,1,0:T(8,128)(2,1)S(1)}, bf16[1,4,16,3072]{3,2,1,0:T(8,128)(2,1)}, u32[]{:S(2)}) copy-start(bf16[1,4,16,3072]{3,2,1,0:T(8,128)(2,1)} %param.5) | copy-start | bytes 1179652
  11.7 2.0 %collective-permute-start.2 = (bf16[96,2688]{1,0:T(8,128)(2,1)S(1)}, bf16[96,2688]{1,0:T(8,128)(2,1)S(1)}, u32[]{:S(2)}, u32[]{:S(2)}) collective-permute-start(bf16[96,2688]{1,0:T(8,128)(2,1)S(1)} %get-tuple-element.41), channel_id=1, source_target_pairs={{0,1},{1,0},{2,3},{3,2},{4,5},{5,4},{6,7},{7,6},{8,9},{9,8},{10,11... | collective-permute-start | bytes 1548296 | tf_op jit(solution)/shard_map/ppermute | solution.py:460
  13.8 5.7 %collective-permute-start.3 = (bf16[4,120,128]{2,1,0:T(8,128)(2,1)S(1)}, bf16[4,120,128]{2,1,0:T(8,128)(2,1)S(1)}, u32[]{:S(2)}, u32[]{:S(2)}) collective-permute-start(bf16[4,120,128]{2,1,0:T(8,128)(2,1)S(1)} %get-tuple-element.43), channel_id=1, source_target_pairs={{0,8},{8,0},{16,24},{24,16},{1,9},{9,1},{17,25},{25,17},{2,10},{10... | collective-permute-start | bytes 368648 | tf_op jit(solution)/shard_map/ppermute | solution.py:484
  15.8 5.1 %collective-permute-start.4 = (bf16[4,120,128]{2,1,0:T(8,128)(2,1)S(1)}, bf16[4,120,128]{2,1,0:T(8,128)(2,1)S(1)}, u32[]{:S(2)}, u32[]{:S(2)}) collective-permute-start(bf16[4,120,128]{2,1,0:T(8,128)(2,1)S(1)} %get-tuple-element.44), channel_id=1, source_target_pairs={{0,16},{8,24},{16,0},{24,8},{1,17},{9,25},{17,1},{25,9},{2,18},{10... | collective-permute-start | bytes 368648 | tf_op jit(solution)/shard_map/ppermute | solution.py:485
  17.4 7.2 %collective-permute-start.1 = (bf16[128,384]{1,0:T(8,128)(2,1)S(1)}, bf16[128,384]{1,0:T(8,128)(2,1)S(1)}, u32[]{:S(2)}, u32[]{:S(2)}) collective-permute-start(bf16[128,384]{1,0:T(8,128)(2,1)S(1)} %get-tuple-element.36), channel_id=1, source_target_pairs={{1,0},{2,1},{3,2},{4,3},{5,4},{6,5},{7,6},{0,7},{9,8},{10,9},{11,1... | collective-permute-start | bytes 294920 | tf_op jit(solution)/shard_map/ppermute | solution.py:461
  21.0 6.9 %collective-permute-start.5 = (bf16[248,128]{1,0:T(8,128)(2,1)S(1)}, bf16[248,128]{1,0:T(8,128)(2,1)S(1)}, u32[]{:S(2)}, u32[]{:S(2)}) collective-permute-start(bf16[248,128]{1,0:T(8,128)(2,1)S(1)} %get-tuple-element.46), channel_id=1, source_target_pairs={{0,4},{1,5},{2,6},{3,7},{4,0},{5,1},{6,2},{7,3},{8,12},{9,13},{10,... | collective-permute-start | bytes 190472 | tf_op jit(solution)/shard_map/ppermute | solution.py:495
  22.0 6.2 %collective-permute-start.6 = (bf16[248,128]{1,0:T(8,128)(2,1)S(1)}, bf16[248,128]{1,0:T(8,128)(2,1)S(1)}, u32[]{:S(2)}, u32[]{:S(2)}) collective-permute-start(bf16[248,128]{1,0:T(8,128)(2,1)S(1)} %get-tuple-element.47), channel_id=1, source_target_pairs={{0,6},{1,7},{2,4},{3,5},{4,2},{5,3},{6,0},{7,1},{8,14},{9,15},{10,... | collective-permute-start | bytes 190472 | tf_op jit(solution)/shard_map/ppermute | solution.py:495
  23.4 5.2 %collective-permute-start.7 = (bf16[248,128]{1,0:T(8,128)(2,1)S(1)}, bf16[248,128]{1,0:T(8,128)(2,1)S(1)}, u32[]{:S(2)}, u32[]{:S(2)}) collective-permute-start(bf16[248,128]{1,0:T(8,128)(2,1)S(1)} %get-tuple-element.48), channel_id=1, source_target_pairs={{0,2},{1,3},{2,0},{3,1},{4,6},{5,7},{6,4},{7,5},{8,10},{9,11},{10,... | collective-permute-start | bytes 190472 | tf_op jit(solution)/shard_map/ppermute | solution.py:495
  28.6 5.2 %collective-permute-start.10 = (bf16[248,128]{1,0:T(8,128)(2,1)S(1)}, bf16[248,128]{1,0:T(8,128)(2,1)S(1)}, u32[]{:S(2)}, u32[]{:S(2)}) collective-permute-start(bf16[248,128]{1,0:T(8,128)(2,1)S(1)} %depth_sum.1.total_ref.refs_0_), channel_id=1, source_target_pairs={{0,24},{8,16},{16,8},{24,0},{1,25},{9,17},{17,9},{25,1},{2,26},{10... | collective-permute-start | bytes 190472 | tf_op jit(solution)/shard_map/ppermute | solution.py:527
  30.2 4.3 %collective-permute-start.9 = (bf16[248,128]{1,0:T(8,128)(2,1)S(1)}, bf16[248,128]{1,0:T(8,128)(2,1)S(1)}, u32[]{:S(2)}, u32[]{:S(2)}) collective-permute-start(bf16[248,128]{1,0:T(8,128)(2,1)S(1)} %depth_sum.1.total_ref.refs_0_), channel_id=1, source_target_pairs={{0,16},{8,24},{16,0},{24,8},{1,17},{9,25},{17,1},{25,9},{2,18},{10... | collective-permute-start | bytes 190472 | tf_op jit(solution)/shard_map/ppermute | solution.py:527
  30.7 4.2 %collective-permute-start.8 = (bf16[248,128]{1,0:T(8,128)(2,1)S(1)}, bf16[248,128]{1,0:T(8,128)(2,1)S(1)}, u32[]{:S(2)}, u32[]{:S(2)}) collective-permute-start(bf16[248,128]{1,0:T(8,128)(2,1)S(1)} %depth_sum.1.total_ref.refs_0_), channel_id=1, source_target_pairs={{0,8},{8,0},{16,24},{24,16},{1,9},{9,1},{17,25},{25,17},{2,10},{10... | collective-permute-start | bytes 190472 | tf_op jit(solution)/shard_map/ppermute | solution.py:527
